TPU v7x, 32 devices: a whole 2x2x4 slice. The times are simulated.
32 devices in a mesh: dp: 16 (over z, x, core), expert: 2 (over y).
Axes of the slice: x: 2, y: 2, z: 4, core: 2. Of those that a mesh axis runs over, the one named last changes fastest.
Arguments:
- tokens: bfloat16 [2, 3584, 1536], P('expert', 'dp'), may hold values from -6 to 6
- attn_gain: bfloat16 [1536], P('dp'), may hold values from 0.099609375 to 1.8984375
- query_weight: bfloat16 [1536, 1536], P('dp'), may hold values from -0.15625 to 0.15625
- key_weight: bfloat16 [1536, 256], P('dp'), may hold values from -0.15625 to 0.15625
- value_weight: bfloat16 [1536, 256], P('dp'), may hold values from -0.15625 to 0.15625
- out_weight: bfloat16 [1536, 1536], P('dp'), may hold values from -0.875 to 0.875
- moe_gain: bfloat16 [1536], P('dp'), may hold values from 0.099609375 to 1.8984375
- router_weight: bfloat16 [1536, 32], P('dp'), may hold values from -0.063964844 to 0.063964844
- gate_weight: bfloat16 [32, 1536, 768], P('expert', 'dp'), may hold values from -0.15625 to 0.15625
- up_weight: bfloat16 [32, 1536, 768], P('expert', 'dp'), may hold values from -0.15625 to 0.15625
- down_weight: bfloat16 [32, 768, 1536], P('expert', 'dp'), may hold values from -0.4375 to 0.4375
- parents: int32 [2, 16], P('expert'), may hold values from 0 to 14, as said below
- routes: int32 [2, 3584, 4], P('expert', 'dp'), may hold values from 0 to 31, all different within a row
- claim_order: int32 [2, 16, 896], P('expert', 'dp'), may hold values from 0 to 895, each once within a row
- cotangent: bfloat16 [2, 3584, 1536], P('expert', 'dp'), may hold values from -6 to 6
Outputs:
- block_out: bfloat16 [2, 3584, 1536], P('expert', 'dp')
- grad_tokens: float32 [2, 3584, 1536], P('expert', 'dp')
- grad_attn_gain: float32 [1536], P('dp')
- grad_query: float32 [1536, 1536], P('dp')
- grad_key: float32 [1536, 256], P('dp')
- grad_value: float32 [1536, 256], P('dp')
- grad_out: float32 [1536, 1536], P('dp')
- grad_moe_gain: float32 [1536], P('dp')
- grad_router: float32 [1536, 32], P('dp')
- grad_gate: float32 [32, 1536, 768], P('expert', 'dp')
- grad_up: float32 [32, 1536, 768], P('expert', 'dp')
- grad_down: float32 [32, 768, 1536], P('expert', 'dp')
Inputs may be any that keep to these rules, and one draw needn't show every extreme that they name: parents[g, 0] = 0 and parents[g, s] < s for s >= 1. `routes`: each token names 4 different experts. `claim_order`: within each segment a permutation of its pairs, numbered token * 4 + choice within the segment.
All inputs are finite; a program needn't handle non-finite values.
Results may differ from a plain program's by a relative error of at most 0.024.
Values may be sent and summed in bfloat16 or wider, within the bound.
A program may use at most 384 MiB of HBM per device.

v0:
```python
import jax
import jax.numpy as jnp
from jax import lax
from jax.sharding import PartitionSpec as P

HEADS = 12
KV_HEADS = 2
HEAD = 128
EXPERTS = 32
TOP = 4
CAP = 28


epsilon = 1e-06
theta = 10000.0
highest = lax.Precision.HIGHEST


def ancestry(parents):
    row_count = parents.shape[0]
    labels = jnp.arange(row_count, dtype=jnp.int32)
    linked = (parents[:, None] == labels[None, :]).astype(jnp.float32)
    reach_all = jnp.minimum(jnp.eye(row_count, dtype=jnp.float32) + linked, 1.0)
    for doubling in range(max(1, (row_count - 1).bit_length())):
        reach_all = jnp.minimum(jnp.dot(reach_all, reach_all, precision=highest), 1.0)
    return reach_all


def rope_tables(positions, head_size):
    halfway = head_size // 2
    frequency = theta ** (-jnp.arange(halfway, dtype=jnp.float32) * 2.0 / head_size)
    angles = positions[:, None] * frequency[None, :]
    return (jnp.cos(angles)[:, None, :], jnp.sin(angles)[:, None, :])


def rotate(values, cosine, sine_part):
    halfway = values.shape[-1] // 2
    first_half = values[..., :halfway]
    second = values[..., halfway:]
    return jnp.concatenate(
        [first_half * cosine - second * sine_part, second * cosine + first_half * sine_part],
        axis=-1,
    )


def norm_backward(grad_hidden, normed, row_scale, gain):
    grad_normed = grad_hidden * gain
    grad_gain = jnp.sum(grad_hidden * normed, axis=0)
    grad_rows = row_scale * (
        grad_normed - normed * jnp.mean(grad_normed * normed, axis=-1, keepdims=True)
    )
    return (grad_rows, grad_gain)


def local(
    tokens,
    attn_gain,
    query_weight,
    key_weight,
    value_weight,
    out_weight,
    moe_gain,
    router_weight,
    gate_weight,
    up_weight,
    down_weight,
    parents,
    routes,
    claim_order,
    cotangent,
):
    (
        gain_one,
        query_full,
        key_full,
        value_full,
        out_full,
        gain_two,
        router_full,
        gate_full,
        up_full,
        down_full,
    ) = (
        lax.all_gather(attn_gain, "dp", axis=0, tiled=True),
        lax.all_gather(query_weight, "dp", axis=0, tiled=True),
        lax.all_gather(key_weight, "dp", axis=0, tiled=True),
        lax.all_gather(value_weight, "dp", axis=0, tiled=True),
        lax.all_gather(out_weight, "dp", axis=0, tiled=True),
        lax.all_gather(moe_gain, "dp", axis=0, tiled=True),
        lax.all_gather(router_weight, "dp", axis=0, tiled=True),
        lax.all_gather(gate_weight, "dp", axis=1, tiled=True),
        lax.all_gather(up_weight, "dp", axis=1, tiled=True),
        lax.all_gather(down_weight, "dp", axis=1, tiled=True),
    )
    tok_count = tokens.shape[1]
    model_width = tokens.shape[2]
    segment = lax.axis_index("dp")
    segment_count = lax.axis_size("dp")
    expert_peers = lax.axis_size("expert")
    local_experts = gate_weight.shape[0]
    repeat_heads = HEADS // KV_HEADS
    score_scale = HEAD ** (-0.5)
    query_rows = repeat_heads * tok_count
    reach_all = ancestry(parents[0])
    reach_row = reach_all[segment]
    path_depth = jnp.sum(reach_row) - 1.0
    positions = path_depth * tok_count + jnp.arange(tok_count, dtype=jnp.float32)
    cosine, sine_part = rope_tables(positions, HEAD)
    inputs = tokens[0].astype(jnp.float32)
    scale_one = lax.rsqrt(jnp.mean(inputs * inputs, axis=-1, keepdims=True) + epsilon)
    normed_one = inputs * scale_one
    gain_first = gain_one.astype(jnp.float32)
    hidden_one = (normed_one * gain_first).astype(jnp.bfloat16)
    query_raw = jnp.dot(hidden_one, query_full, preferred_element_type=jnp.float32).reshape(
        tok_count, HEADS, HEAD
    )
    key_raw = jnp.dot(hidden_one, key_full, preferred_element_type=jnp.float32).reshape(
        tok_count, KV_HEADS, HEAD
    )
    value_low = jnp.dot(hidden_one, value_full, preferred_element_type=jnp.float32).astype(
        jnp.bfloat16
    )
    query_rot = rotate(query_raw, cosine, sine_part).astype(jnp.bfloat16)
    key_rot = (
        rotate(key_raw, cosine, sine_part).astype(jnp.bfloat16).reshape(tok_count, KV_HEADS * HEAD)
    )
    key_all, value_all = (
        lax.all_gather(key_rot, "dp", axis=0, tiled=True),
        lax.all_gather(value_low, "dp", axis=0, tiled=True),
    )
    total_keys = key_all.shape[0]
    key_blocks = key_all.reshape(segment_count, tok_count, KV_HEADS, HEAD)
    value_blocks = value_all.reshape(segment_count, tok_count, KV_HEADS, HEAD)
    segment_labels = jnp.arange(segment_count, dtype=jnp.int32)
    query_groups = (
        query_rot.reshape(tok_count, KV_HEADS, repeat_heads, HEAD)
        .transpose(1, 2, 0, 3)
        .reshape(KV_HEADS, query_rows, HEAD)
    )
    query_offsets = jnp.arange(tok_count, dtype=jnp.int32)
    causal_tile = jnp.tile(query_offsets[None, :] <= query_offsets[:, None], (repeat_heads, 1))

    def scores_of(key_block, label):
        raw_scores = (
            jnp.einsum("grh,kgh->grk", query_groups, key_block, preferred_element_type=jnp.float32)
            * score_scale
        )
        allowed = causal_tile | (label != segment)
        return jnp.where(allowed[None], raw_scores, -1000000000.0)

    def on_path(label):
        return reach_row[label] > 0.5

    def pass_stats(state_pair, inputs_block):
        key_block, value_block, label = inputs_block

        def visit(state):
            row_max, row_sum = state
            scores = scores_of(key_block, label)
            new_max = jnp.maximum(row_max, jnp.max(scores, axis=-1))
            new_sum = row_sum * jnp.exp(row_max - new_max) + jnp.sum(
                jnp.exp(scores - new_max[..., None]), axis=-1
            )
            return (new_max, new_sum)

        return (lax.cond(on_path(label), visit, lambda state: state, state_pair), None)

    start_max = jnp.full((KV_HEADS, query_rows), -1e30, jnp.float32)
    start_sum = jnp.zeros((KV_HEADS, query_rows), jnp.float32)
    (row_max, row_sum), unused = lax.scan(
        pass_stats, (start_max, start_sum), (key_blocks, value_blocks, segment_labels)
    )

    def probs_of(key_block, label):
        return jnp.exp(scores_of(key_block, label) - row_max[..., None]) / row_sum[..., None]

    def pass_values(state_pair, inputs_block):
        key_block, value_block, label = inputs_block

        def visit(state):
            accumulated, exact_out = state
            prob_block = probs_of(key_block, label)
            accumulated = accumulated + jnp.einsum(
                "grk,kgh->grh",
                prob_block.astype(jnp.bfloat16),
                value_block,
                preferred_element_type=jnp.float32,
            )
            exact_out = exact_out + jnp.einsum(
                "grk,kgh->grh",
                prob_block,
                value_block.astype(jnp.float32),
                preferred_element_type=jnp.float32,
                precision=highest,
            )
            return (accumulated, exact_out)

        return (lax.cond(on_path(label), visit, lambda state: state, state_pair), None)

    zero_out = jnp.zeros((KV_HEADS, query_rows, HEAD), jnp.float32)
    (accumulated, exact_out), unused = lax.scan(
        pass_values, (zero_out, zero_out), (key_blocks, value_blocks, segment_labels)
    )
    attended = (
        accumulated.reshape(KV_HEADS, repeat_heads, tok_count, HEAD)
        .transpose(2, 0, 1, 3)
        .reshape(tok_count, HEADS * HEAD)
        .astype(jnp.bfloat16)
    )
    branch = jnp.dot(attended, out_full, preferred_element_type=jnp.float32)
    middle = inputs + branch
    scale_two = lax.rsqrt(jnp.mean(middle * middle, axis=-1, keepdims=True) + epsilon)
    normed_two = middle * scale_two
    gain_second = gain_two.astype(jnp.float32)
    hidden_two = (normed_two * gain_second).astype(jnp.bfloat16)
    logits = jnp.dot(hidden_two, router_full, preferred_element_type=jnp.float32)
    picked_one = (
        routes[0][:, :, None] == jnp.arange(EXPERTS, dtype=jnp.int32)[None, None, :]
    ).astype(jnp.float32)
    chosen = jnp.sum(picked_one * logits[:, None, :], axis=-1)
    gate_probs = jax.nn.softmax(chosen, axis=-1)
    expert_ids = routes[0].reshape(-1)
    order_row = claim_order[0, 0]
    pair_count = expert_ids.shape[0]
    member = (expert_ids[:, None] == jnp.arange(EXPERTS, dtype=jnp.int32)[None, :]).astype(
        jnp.bfloat16
    )
    earlier = (order_row[None, :] < order_row[:, None]).astype(jnp.bfloat16)
    before = jnp.dot(earlier, member, preferred_element_type=jnp.float32)
    slot_index = jnp.sum(before * member.astype(jnp.float32), axis=1).astype(jnp.int32)
    owner_rank = expert_ids // local_experts
    local_rank = expert_ids % local_experts
    target = jnp.where(
        slot_index < CAP, (local_rank * expert_peers + owner_rank) * CAP + slot_index, EXPERTS * CAP
    )
    slot_pairs = (
        jnp.full((EXPERTS * CAP + 1,), pair_count, jnp.int32)
        .at[target]
        .set(jnp.arange(pair_count, dtype=jnp.int32))[: EXPERTS * CAP]
    )
    padded_two = jnp.concatenate([hidden_two, jnp.zeros((1, model_width), jnp.bfloat16)], axis=0)
    send_rows = padded_two[slot_pairs // TOP].reshape(local_experts, expert_peers, CAP, model_width)
    arrived = lax.all_to_all(send_rows, "expert", split_axis=1, concat_axis=1, tiled=True)
    expert_rows = arrived.reshape(local_experts, expert_peers * CAP, model_width)
    gate_act = jnp.einsum(
        "erd,edf->erf", expert_rows, gate_full, preferred_element_type=jnp.float32
    )
    up_act = jnp.einsum("erd,edf->erf", expert_rows, up_full, preferred_element_type=jnp.float32)
    inner = (jax.nn.silu(gate_act) * up_act).astype(jnp.bfloat16)
    expert_out = jnp.einsum(
        "erf,efd->erd", inner, down_full, preferred_element_type=jnp.float32
    ).astype(jnp.bfloat16)
    returned = lax.all_to_all(
        expert_out.reshape(local_experts, expert_peers, CAP, model_width),
        "expert",
        split_axis=1,
        concat_axis=1,
        tiled=True,
    )
    returned = jnp.concatenate(
        [returned.reshape(EXPERTS * CAP, model_width), jnp.zeros((1, model_width), jnp.bfloat16)],
        axis=0,
    )
    pair_out = returned[target].reshape(tok_count, TOP, model_width).astype(jnp.float32)
    mixture = jnp.sum(gate_probs[:, :, None] * pair_out, axis=1)
    block_out = (middle + mixture).astype(jnp.bfloat16)
    grad_result = cotangent[0].astype(jnp.float32)
    grad_gates = jnp.sum(pair_out * grad_result[:, None, :], axis=-1)
    grad_pairs = (
        (gate_probs[:, :, None] * grad_result[:, None, :])
        .astype(jnp.bfloat16)
        .reshape(pair_count, model_width)
    )
    grad_padded = jnp.concatenate([grad_pairs, jnp.zeros((1, model_width), jnp.bfloat16)], axis=0)
    grad_send = grad_padded[slot_pairs].reshape(local_experts, expert_peers, CAP, model_width)
    grad_arrived, rows_back = (
        lax.all_to_all(grad_send, "expert", split_axis=1, concat_axis=1, tiled=True),
        lax.all_to_all(send_rows, "expert", split_axis=1, concat_axis=1, tiled=True),
    )
    rows_again = rows_back.reshape(local_experts, expert_peers * CAP, model_width)
    gate_again = jnp.einsum(
        "erd,edf->erf", rows_again, gate_full, preferred_element_type=jnp.float32
    )
    up_again = jnp.einsum("erd,edf->erf", rows_again, up_full, preferred_element_type=jnp.float32)
    inner_again = (jax.nn.silu(gate_again) * up_again).astype(jnp.bfloat16)
    grad_expert_out = grad_arrived.reshape(local_experts, expert_peers * CAP, model_width)
    grad_inner = jnp.einsum(
        "erd,efd->erf", grad_expert_out, down_full, preferred_element_type=jnp.float32
    )
    grad_down_local = jnp.einsum(
        "erf,erd->efd", inner_again, grad_expert_out, preferred_element_type=jnp.float32
    )
    sigmoid_gate = jax.nn.sigmoid(gate_again)
    swish = gate_again * sigmoid_gate
    grad_gate_act = (
        grad_inner * up_again * (sigmoid_gate * (1.0 + gate_again * (1.0 - sigmoid_gate)))
    ).astype(jnp.bfloat16)
    grad_up_act = (grad_inner * swish).astype(jnp.bfloat16)
    grad_gate_local = jnp.einsum(
        "erd,erf->edf", rows_again, grad_gate_act, preferred_element_type=jnp.float32
    )
    grad_up_local = jnp.einsum(
        "erd,erf->edf", rows_again, grad_up_act, preferred_element_type=jnp.float32
    )
    grad_rows = (
        jnp.einsum("erf,edf->erd", grad_gate_act, gate_full, preferred_element_type=jnp.float32)
        + jnp.einsum("erf,edf->erd", grad_up_act, up_full, preferred_element_type=jnp.float32)
    ).astype(jnp.bfloat16)
    grad_back = lax.all_to_all(
        grad_rows.reshape(local_experts, expert_peers, CAP, model_width),
        "expert",
        split_axis=1,
        concat_axis=1,
        tiled=True,
    )
    grad_back = jnp.concatenate(
        [grad_back.reshape(EXPERTS * CAP, model_width), jnp.zeros((1, model_width), jnp.bfloat16)],
        axis=0,
    )
    grad_hidden_two = jnp.sum(
        grad_back[target].reshape(tok_count, TOP, model_width).astype(jnp.float32), axis=1
    )
    grad_chosen = gate_probs * (
        grad_gates - jnp.sum(gate_probs * grad_gates, axis=-1, keepdims=True)
    )
    grad_logits = jnp.sum(picked_one * grad_chosen[:, :, None], axis=1).astype(jnp.bfloat16)
    grad_hidden_two = grad_hidden_two + jnp.dot(
        grad_logits, router_full.T, preferred_element_type=jnp.float32
    )
    grad_router_local = jnp.dot(hidden_two.T, grad_logits, preferred_element_type=jnp.float32)
    grad_middle_norm, grad_gain_two = norm_backward(
        grad_hidden_two, normed_two, scale_two, gain_second
    )
    grad_middle = grad_result + grad_middle_norm
    grad_branch = grad_middle.astype(jnp.bfloat16)
    grad_out_local = jnp.dot(attended.T, grad_branch, preferred_element_type=jnp.float32)
    grad_attended = jnp.dot(grad_branch, out_full.T, preferred_element_type=jnp.float32).astype(
        jnp.bfloat16
    )
    grad_groups = (
        grad_attended.reshape(tok_count, KV_HEADS, repeat_heads, HEAD)
        .transpose(1, 2, 0, 3)
        .reshape(KV_HEADS, query_rows, HEAD)
    )
    row_delta = jnp.sum(grad_groups.astype(jnp.float32) * exact_out, axis=-1)
    zero_key = jnp.zeros((tok_count, KV_HEADS, HEAD), jnp.float32)

    def pass_grads(grad_query, inputs_block):
        key_block, value_block, label = inputs_block

        def visit(carried):
            prob_block = probs_of(key_block, label)
            grad_probs = jnp.einsum(
                "grh,kgh->grk", grad_groups, value_block, preferred_element_type=jnp.float32
            )
            grad_scores = (prob_block * (grad_probs - row_delta[..., None])).astype(jnp.bfloat16)
            carried = carried + jnp.einsum(
                "grk,kgh->grh", grad_scores, key_block, preferred_element_type=jnp.float32
            )
            grad_key_block = (
                jnp.einsum(
                    "grk,grh->kgh", grad_scores, query_groups, preferred_element_type=jnp.float32
                )
                * score_scale
            )
            grad_value_block = jnp.einsum(
                "grk,grh->kgh",
                prob_block.astype(jnp.bfloat16),
                grad_groups,
                preferred_element_type=jnp.float32,
            )
            return (carried, (grad_key_block, grad_value_block))

        def skip(carried):
            return (carried, (zero_key, zero_key))

        return lax.cond(on_path(label), visit, skip, grad_query)

    grad_query_groups, (grad_key_blocks, grad_value_blocks) = lax.scan(
        pass_grads,
        jnp.zeros((KV_HEADS, query_rows, HEAD), jnp.float32),
        (key_blocks, value_blocks, segment_labels),
    )
    grad_key_all = grad_key_blocks.reshape(total_keys, KV_HEADS * HEAD)
    grad_value_all = grad_value_blocks.reshape(total_keys, KV_HEADS * HEAD)
    grad_key_mine, grad_value_mine = (
        lax.psum_scatter(
            grad_key_all.astype(jnp.bfloat16), "dp", scatter_dimension=0, tiled=True
        ).astype(jnp.float32),
        lax.psum_scatter(
            grad_value_all.astype(jnp.bfloat16), "dp", scatter_dimension=0, tiled=True
        ).astype(jnp.float32),
    )
    grad_query_rot = (
        (grad_query_groups * score_scale)
        .reshape(KV_HEADS, repeat_heads, tok_count, HEAD)
        .transpose(2, 0, 1, 3)
        .reshape(tok_count, HEADS, HEAD)
    )
    grad_query_raw = (
        rotate(grad_query_rot, cosine, -sine_part)
        .reshape(tok_count, HEADS * HEAD)
        .astype(jnp.bfloat16)
    )
    grad_key_raw = (
        rotate(grad_key_mine.reshape(tok_count, KV_HEADS, HEAD), cosine, -sine_part)
        .reshape(tok_count, KV_HEADS * HEAD)
        .astype(jnp.bfloat16)
    )
    grad_value_raw = grad_value_mine.astype(jnp.bfloat16)
    grad_query_local = jnp.dot(hidden_one.T, grad_query_raw, preferred_element_type=jnp.float32)
    grad_key_local = jnp.dot(hidden_one.T, grad_key_raw, preferred_element_type=jnp.float32)
    grad_value_local = jnp.dot(hidden_one.T, grad_value_raw, preferred_element_type=jnp.float32)
    grad_hidden_one = (
        jnp.dot(grad_query_raw, query_full.T, preferred_element_type=jnp.float32)
        + jnp.dot(grad_key_raw, key_full.T, preferred_element_type=jnp.float32)
        + jnp.dot(grad_value_raw, value_full.T, preferred_element_type=jnp.float32)
    )
    grad_inputs_norm, grad_gain_one = norm_backward(
        grad_hidden_one, normed_one, scale_one, gain_first
    )
    grad_inputs = grad_middle + grad_inputs_norm
    grad_gate_mine, grad_up_mine, grad_down_mine = (
        lax.psum_scatter(
            grad_gate_local.astype(jnp.bfloat16), "dp", scatter_dimension=1, tiled=True
        ).astype(jnp.float32),
        lax.psum_scatter(
            grad_up_local.astype(jnp.bfloat16), "dp", scatter_dimension=1, tiled=True
        ).astype(jnp.float32),
        lax.psum_scatter(
            grad_down_local.astype(jnp.bfloat16), "dp", scatter_dimension=1, tiled=True
        ).astype(jnp.float32),
    )
    shard_rows = (
        lax.psum_scatter(
            grad_gain_one.astype(jnp.bfloat16), "dp", scatter_dimension=0, tiled=True
        ).astype(jnp.float32),
        lax.psum_scatter(
            grad_query_local.astype(jnp.bfloat16), "dp", scatter_dimension=0, tiled=True
        ).astype(jnp.float32),
        lax.psum_scatter(
            grad_key_local.astype(jnp.bfloat16), "dp", scatter_dimension=0, tiled=True
        ).astype(jnp.float32),
        lax.psum_scatter(
            grad_value_local.astype(jnp.bfloat16), "dp", scatter_dimension=0, tiled=True
        ).astype(jnp.float32),
        lax.psum_scatter(
            grad_out_local.astype(jnp.bfloat16), "dp", scatter_dimension=0, tiled=True
        ).astype(jnp.float32),
        lax.psum_scatter(
            grad_gain_two.astype(jnp.bfloat16), "dp", scatter_dimension=0, tiled=True
        ).astype(jnp.float32),
        lax.psum_scatter(
            grad_router_local.astype(jnp.bfloat16), "dp", scatter_dimension=0, tiled=True
        ).astype(jnp.float32),
    )
    shared = (
        lax.psum(shard_rows[0].astype(jnp.bfloat16), "expert").astype(jnp.float32),
        lax.psum(shard_rows[1].astype(jnp.bfloat16), "expert").astype(jnp.float32),
        lax.psum(shard_rows[2].astype(jnp.bfloat16), "expert").astype(jnp.float32),
        lax.psum(shard_rows[3].astype(jnp.bfloat16), "expert").astype(jnp.float32),
        lax.psum(shard_rows[4].astype(jnp.bfloat16), "expert").astype(jnp.float32),
        lax.psum(shard_rows[5].astype(jnp.bfloat16), "expert").astype(jnp.float32),
        lax.psum(shard_rows[6].astype(jnp.bfloat16), "expert").astype(jnp.float32),
    )
    return (
        block_out[None],
        grad_inputs[None],
        shared[0],
        shared[1],
        shared[2],
        shared[3],
        shared[4],
        shared[5],
        shared[6],
        grad_gate_mine,
        grad_up_mine,
        grad_down_mine,
    )


def solution(mesh):
    placed = (
        P("expert", "dp", None),
        P("dp"),
        P("dp", None),
        P("dp", None),
        P("dp", None),
        P("dp", None),
        P("dp"),
        P("dp", None),
        P("expert", "dp", None),
        P("expert", "dp", None),
        P("expert", "dp", None),
        P("expert", None),
        P("expert", "dp", None),
        P("expert", "dp", None),
        P("expert", "dp", None),
    )
    return jax.shard_map(
        local,
        mesh=mesh,
        in_specs=placed,
        out_specs=(
            P("expert", "dp", None),
            P("expert", "dp", None),
            P("dp"),
            P("dp", None),
            P("dp", None),
            P("dp", None),
            P("dp", None),
            P("dp"),
            P("dp", None),
            P("expert", "dp", None),
            P("expert", "dp", None),
            P("expert", "dp", None),
        ),
        check_vma=False,
    )
```

profile of v0, /device:TPU:8, one launch (start us, length us, event | category | flops | bytes accessed | tf_op | source)
XLA Modules:
  0.0 2816.8 jit_solution(11772685540079479852)
XLA Ops:
  8.6 21.3 all_gather.37
  32.1 25.2 all-reduce.9
  61.9 24.9 all_gather.40
  97.9 7.4 mul.445
  105.4 20.5 all-gather
  138.3 13.0 all-gather.13.cloned.1.call-done
  156.6 50.1 %all-gather.11.cloned.1.call-done = bf16[1536,1536]{1,0:T(8,128)(2,1)} async-done(((bf16[96,1536]{1,0:T(8,128)(2,1)}), bf16[1536,1536]{1,0:T(8,128)(2,1)}) %all-gather.11.cloned.1.call-update) | async-done | bytes 4718608 | tf_op jit(solution)/shard_map/all_gather | solution.py:85
  206.7 6.6 copy.186
  219.5 115.0 %while.44 = (s32[]{:T(128)}, f32[2,1344]{1,0:T(2,128)}, f32[2,1344]{1,0:T(2,128)}, s32[16]{0:T(128)S(1)}, f32[16]{0:T(128)}, /*index=5*/s32[]{:T(128)}, bf16[16,...) while((s32[]{:T(128)}, f32[2,1344]{1,0:T(2,128)}, ...), condition=%wide.region_7.8_spmd.clone, body=%wide.region_2.7_spmd.clone.sunk | while | flops 157457664 | bytes 7616831 | solution.py:170
  335.6 131.2 %while.45 = (s32[]{:T(128)}, f32[2,1344,128]{2,1,0:T(8,128)S(1)}, f32[2,1344,128]{2,1,0:T(8,128)S(1)}, s32[16]{0:T(128)S(1)}, f32[16]{0:T(128)}, /*index=5*/s32[...) while((s32[]{:T(128)}, f32[2,1344,128]{2,1,0:T(8,128)S(1)}, ...), condition=%wide.region_11.12_spmd.clone, body=%wide.region_8.11_spmd.clone.sunk | while | flops 1237125120 | bytes 15643503 | solution.py:201
  341.3 9.1 conditional.10
  355.8 9.1 conditional.10
  370.2 9.1 conditional.10
  384.6 9.1 conditional.10
  399.0 9.1 conditional.10
  517.8 22.4 fusion.59
  540.2 97.6 %all-gather.19.cloned.1.call-done = bf16[16,1536,768]{2,1,0:T(8,128)(2,1)} async-done(((bf16[16,96,768]{2,1,0:T(8,128)(2,1)}), bf16[16,1536,768]{2,1,0:T(8,128)(2,1)}) %all-gather.19.cloned.1.call-update) | async-done | bytes 37748752 | tf_op jit(solution)/shard_map/all_gather | solution.py:92
  637.8 23.4 fusion.57
  661.2 166.0 %all-gather.21.cloned.1.call-done = bf16[16,768,1536]{2,1,0:T(8,128)(2,1)} async-done(((bf16[16,48,1536]{2,1,0:T(8,128)(2,1)}), bf16[16,768,1536]{2,1,0:T(8,128)(2,1)}) %all-gather.21.cloned.1.call-update) | async-done | bytes 37748752 | tf_op jit(solution)/shard_map/all_gather | solution.py:93
  827.1 21.0 multiply_convert_fusion.1
  848.1 20.1 fusion.133
  868.2 19.6 add_convert_fusion
  897.1 16.6 convolution_convert_fusion.5
  917.9 11.9 all-to-all-done.3
  947.4 6.3 reshape.590
  953.6 13.1 all-to-all-done.1
  978.7 6.4 reshape.588
  985.0 8.5 multiply_reduce_fusion
  1009.5 133.9 %while.46 = (s32[]{:T(128)}, f32[2,1344,128]{2,1,0:T(8,128)S(1)}, bf16[16,224,2,128]{3,1,2,0:T(8,128)(2,1)}, bf16[16,224,2,128]{3,1,2,0:T(8,128)(2,1)}, s32[16]{...) while((s32[]{:T(128)}, f32[2,1344,128]{2,1,0:T(8,128)S(1)}, ...), condition=%wide.region_28.29_spmd.clone, body=%wide.region_25.28_spmd.clone.sunk | while | flops 776280064 | bytes 19267456 | solution.py:379
  1014.8 7.4 conditional.11
  1028.2 7.4 conditional.11
  1041.6 7.4 conditional.11
  1055.0 7.4 conditional.11
  1068.5 7.4 conditional.11
  1155.2 80.3 %reduce-scatter.13.cloned.1.call-done = bf16[224,256]{1,0:T(8,128)(2,1)} async-done(((bf16[3584,256]{1,0:T(8,128)(2,1)}), bf16[224,256]{1,0:T(8,128)(2,1)}) %reduce-scatter.13.cloned.1.call-update) | async-done | bytes 114704 | tf_op jit(solution)/shard_map/reduce_scatter | solution.py:387
  1238.5 60.8 %reduce-scatter.15.cloned.1.call-done = bf16[224,256]{1,0:T(8,128)(2,1)} async-done(((bf16[3584,256]{1,0:T(8,128)(2,1)}), bf16[224,256]{1,0:T(8,128)(2,1)}) %reduce-scatter.15.cloned.1.call-update) | async-done | bytes 114704 | tf_op jit(solution)/shard_map/reduce_scatter | solution.py:390
  1319.2 38.7 %reduce-scatter.31.cloned.1.call-done = bf16[96,32]{1,0:T(8,128)(2,1)} async-done(((bf16[1536,32]{1,0:T(8,128)(2,1)}), bf16[96,32]{1,0:T(8,128)(2,1)}) %reduce-scatter.31.cloned.1.call-update) | async-done | bytes 6160
  1363.0 22.9 all-reduce.8
  1387.1 30.4 %reduce-scatter.19.cloned.1.call-done = bf16[96,256]{1,0:T(8,128)(2,1)} async-done(((bf16[1536,256]{1,0:T(8,128)(2,1)}), bf16[96,256]{1,0:T(8,128)(2,1)}) %reduce-scatter.19.cloned.1.call-update) | async-done | bytes 49168 | tf_op jit(solution)/shard_map/reduce_scatter | solution.py:441
  1417.5 59.0 %reduce-scatter.21.cloned.1.call-done = bf16[96,256]{1,0:T(8,128)(2,1)} async-done(((bf16[1536,256]{1,0:T(8,128)(2,1)}), bf16[96,256]{1,0:T(8,128)(2,1)}) %reduce-scatter.21.cloned.1.call-update) | async-done | bytes 49168 | tf_op jit(solution)/shard_map/reduce_scatter | solution.py:444
  1476.6 79.0 %reduce-scatter.17.cloned.1.call-done = bf16[96,1536]{1,0:T(8,128)(2,1)} async-done(((bf16[1536,1536]{1,0:T(8,128)(2,1)}), bf16[96,1536]{1,0:T(8,128)(2,1)}) %reduce-scatter.17.cloned.1.call-update) | async-done | bytes 294928 | tf_op jit(solution)/shard_map/reduce_scatter | solution.py:438
  1555.6 78.9 %reduce-scatter.23.cloned.1.call-done = bf16[96,1536]{1,0:T(8,128)(2,1)} async-done(((bf16[1536,1536]{1,0:T(8,128)(2,1)}), bf16[96,1536]{1,0:T(8,128)(2,1)}) %reduce-scatter.23.cloned.1.call-update) | async-done | bytes 294928 | tf_op jit(solution)/shard_map/reduce_scatter | solution.py:447
  1634.6 18.4 convolution_convert_fusion.2
  1654.3 18.4 convolution_convert_fusion.1
  1674.5 17.6 convolution_convert_fusion
  1705.5 357.4 %reduce-scatter.25.cloned.1.call-done = bf16[16,96,768]{2,1,0:T(8,128)(2,1)} async-done(((bf16[16,1536,768]{2,1,0:T(8,128)(2,1)}), bf16[16,96,768]{2,1,0:T(8,128)(2,1)}) %reduce-scatter.25.cloned.1.call-update) | async-done | bytes 2359312 | tf_op jit(solution)/shard_map/reduce_scatter | solution.py:424
  2067.3 366.8 %reduce-scatter.27.cloned.1.call-done = bf16[16,96,768]{2,1,0:T(8,128)(2,1)} async-done(((bf16[16,1536,768]{2,1,0:T(8,128)(2,1)}), bf16[16,96,768]{2,1,0:T(8,128)(2,1)}) %reduce-scatter.27.cloned.1.call-update) | async-done | bytes 2359312 | tf_op jit(solution)/shard_map/reduce_scatter | solution.py:427
  2438.4 366.9 %reduce-scatter.29.cloned.1.call-done = bf16[16,48,1536]{2,1,0:T(8,128)(2,1)} async-done(((bf16[16,768,1536]{2,1,0:T(8,128)(2,1)}), bf16[16,48,1536]{2,1,0:T(8,128)(2,1)}) %reduce-scatter.29.cloned.1.call-update) | async-done | bytes 2359312 | tf_op jit(solution)/shard_map/reduce_scatter | solution.py:430
  (638 shorter events, 495.3 us)
Async XLA Ops:
  7.2 23.1 copy-start.67
  7.2 24.4 copy-start.68
  7.2 24.7 copy-start.69
  7.2 50.1 %copy-start.6 = (bf16[1,224,1536]{2,1,0:T(8,128)(2,1)S(1)}, bf16[1,224,1536]{2,1,0:T(8,128)(2,1)}, u32[]{:S(2)}) copy-start(bf16[1,224,1536]{2,1,0:T(8,128)(2,1)} %param.27) | copy-start | bytes 2064388
  7.2 125.7 %all-gather.9.cloned.1.call-start = ((), (), s32[]{:S(2)}) async-start(), calls=%async_computation.14 | async-start | bytes 1949696 | tf_op jit(solution)/shard_map/all_gather | solution.py:128
  30.0 31.0 %copy-start.23 = (bf16[1536,256]{1,0:T(8,128)(2,1)}, bf16[1536,256]{1,0:T(8,128)(2,1)S(1)}, u32[]{:S(2)}) copy-start(bf16[1536,256]{1,0:T(8,128)(2,1)S(1)} %all_gather.37) | copy-start | bytes 2359300
  57.3 156.0 %copy-start.42 = (f32[1536]{0:T(1024)}, f32[1536]{0:T(1024)S(1)}, u32[]{:S(2)}) copy-start(f32[1536]{0:T(1024)S(1)} %convert_element_type.296) | copy-start | bytes 18436
  57.6 155.8 %copy-start.54 = (f32[224]{0:T(256)}, f32[224]{0:T(256)S(1)}, u32[]{:S(2)}) copy-start(f32[224]{0:T(256)S(1)} %add_rsqrt_fusion.1) | copy-start | bytes 2692
  60.5 156.9 %copy-start.31 = (f32[224,64]{1,0:T(8,128)}, f32[224,64]{1,0:T(8,128)S(1)}, u32[]{:S(2)}) copy-start(f32[224,64]{1,0:T(8,128)S(1)} %get-tuple-element.1017) | copy-start | bytes 172036
  61.9 89.5 %all-gather.13.cloned.1.call-start = ((), (), s32[]{:S(2)}) async-start(), calls=%async_computation.16 | async-start | bytes 1949696 | tf_op jit(solution)/shard_map/all_gather | solution.py:129
  88.8 117.9 %all-gather.11.cloned.1.call-start = ((), (), s32[]{:S(2)}) async-start(), calls=%async_computation.15 | async-start | bytes 5013504 | tf_op jit(solution)/shard_map/all_gather | solution.py:85
  89.6 380.6 %all-gather.15.cloned.1.call-start = ((), (), s32[]{:S(2)}) async-start(), calls=%async_computation.17 | async-start | bytes 5013504 | tf_op jit(solution)/shard_map/all_gather | solution.py:88
  90.2 427.6 %all-gather.17.cloned.1.call-start = ((), (), s32[]{:S(2)}) async-start(), calls=%async_computation.18 | async-start | bytes 40108032 | tf_op jit(solution)/shard_map/all_gather | solution.py:91
  90.8 547.0 %all-gather.19.cloned.1.call-start = ((), (), s32[]{:S(2)}) async-start(), calls=%async_computation.19 | async-start | bytes 40108032 | tf_op jit(solution)/shard_map/all_gather | solution.py:92
  91.4 735.8 %all-gather.21.cloned.1.call-start = ((), (), s32[]{:S(2)}) async-start(), calls=%async_computation.20 | async-start | bytes 40108032 | tf_op jit(solution)/shard_map/all_gather | solution.py:93
  92.5 381.6 %copy-start.49 = (f32[1536]{0:T(1024)}, f32[1536]{0:T(1024)S(1)}, u32[]{:S(2)}) copy-start(f32[1536]{0:T(1024)S(1)} %convert_element_type.306) | copy-start | bytes 18436
  97.9 7.5 copy-start.65
  126.1 368.6 %copy-start.37 = (bf16[1536,32]{0,1:T(8,128)(2,1)}, bf16[1536,32]{0,1:T(8,128)(2,1)S(1)}, u32[]{:S(2)}) copy-start(bf16[1536,32]{0,1:T(8,128)(2,1)S(1)} %reshape.642) | copy-start | bytes 294916
  126.2 10.5 copy-start.63
  474.7 20.0 copy-start.21
  489.7 24.0 all-to-all-start
  513.7 147.5 %all-to-all-start.2 = ((bf16[16,2,28,1536]{3,0,2,1:T(8,128)(2,1)}), bf16[16,2,28,1536]{3,0,2,1:T(8,128)(2,1)S(1)}, u32[]{:S(2)}, u32[]{:S(2)}) async-start(bf16[16,2,28,1536]{3,0,2,1:T(8,128)(2,1)} %copy.201), calls=%async_computation.2 | async-start | bytes 5505024 | tf_op jit(solution)/shard_map/all_to_all | solution.py:277
  661.2 187.0 %copy-start.2 = (bf16[16,2,28,1536]{3,0,2,1:T(8,128)(2,1)}, bf16[16,2,28,1536]{3,0,2,1:T(8,128)(2,1)S(1)}, u32[]{:S(2)}) copy-start(bf16[16,2,28,1536]{3,0,2,1:T(8,128)(2,1)S(1)} %all-to-all-done.2) | copy-start | bytes 8257540
  848.1 20.1 copy-start.11
  892.0 37.8 %all-to-all-start.3 = ((bf16[16,2,28,1536]{3,0,2,1:T(8,128)(2,1)}), bf16[16,2,28,1536]{3,0,2,1:T(8,128)(2,1)}, u32[]{:S(2)}, u32[]{:S(2)}) async-start(bf16[16,2,28,1536]{3,0,2,1:T(8,128)(2,1)} %bitcast.260), calls=%async_computation.3 | async-start | bytes 5505024 | tf_op jit(solution)/shard_map/all_to_all | solution.py:309
  929.8 37.0 %all-to-all-start.1 = ((bf16[16,2,28,1536]{3,0,2,1:T(8,128)(2,1)}), bf16[16,2,28,1536]{3,0,2,1:T(8,128)(2,1)}, u32[]{:S(2)}, u32[]{:S(2)}) async-start(bf16[16,2,28,1536]{3,0,2,1:T(8,128)(2,1)} %bitcast.34), calls=%async_computation.1 | async-start | bytes 5505024 | tf_op jit(solution)/shard_map/all_to_all | solution.py:253
  935.0 300.5 %reduce-scatter.13.cloned.1.call-start = ((), (), s32[]{:S(2)}) async-start(), calls=%async_computation.21 | async-start | bytes 1949696 | tf_op jit(solution)/shard_map/reduce_scatter | solution.py:387
  1148.2 151.1 %reduce-scatter.15.cloned.1.call-start = ((), (), s32[]{:S(2)}) async-start(), calls=%async_computation.22 | async-start | bytes 1949696 | tf_op jit(solution)/shard_map/reduce_scatter | solution.py:390
  1152.9 83.9 %copy-start.32 = (f32[224,64]{1,0:T(8,128)S(1)}, f32[224,64]{1,0:T(8,128)}, u32[]{:S(2)}) copy-start(f32[224,64]{1,0:T(8,128)} %copy-done.31) | copy-start | bytes 172036
  1152.9 83.9 %copy-start.36 = (f32[224,64]{1,0:T(8,128)S(1)}, f32[224,64]{1,0:T(8,128)}, u32[]{:S(2)}) copy-start(f32[224,64]{1,0:T(8,128)} %get-tuple-element.1015) | copy-start | bytes 172036
  1152.9 84.0 %copy-start.8 = (bf16[1,224,1536]{2,1,0:T(8,128)(2,1)S(1)}, bf16[1,224,1536]{2,1,0:T(8,128)(2,1)}, u32[]{:S(2)}) copy-start(bf16[1,224,1536]{2,1,0:T(8,128)(2,1)} %param.27) | copy-start | bytes 2064388
  1152.9 84.0 %copy-start.43 = (f32[1536]{0:T(1024)S(1)}, f32[1536]{0:T(1024)}, u32[]{:S(2)}) copy-start(f32[1536]{0:T(1024)} %copy-done.42) | copy-start | bytes 18436
  1152.9 84.0 %copy-start.55 = (f32[224]{0:T(256)S(1)}, f32[224]{0:T(256)}, u32[]{:S(2)}) copy-start(f32[224]{0:T(256)} %copy-done.54) | copy-start | bytes 2692
  1152.9 205.0 %reduce-scatter.31.cloned.1.call-start = ((), (), s32[]{:S(2)}) async-start(), calls=%async_computation.30 | async-start | bytes 417792
  1155.1 262.4 %reduce-scatter.19.cloned.1.call-start = ((), (), s32[]{:S(2)}) async-start(), calls=%async_computation.24 | async-start | bytes 835584 | tf_op jit(solution)/shard_map/reduce_scatter | solution.py:441
  1236.9 64.8 %copy-start.39 = (bf16[224,2,64]{2,0,1:T(8,128)(2,1)}, bf16[224,2,64]{2,0,1:T(8,128)(2,1)S(1)}, u32[]{:S(2)}) copy-start(bf16[224,2,64]{2,0,1:T(8,128)(2,1)S(1)} %get-tuple-element.1005) | copy-start | bytes 172036
  1236.9 64.7 %copy-start.41 = (bf16[224,2,64]{2,0,1:T(8,128)(2,1)}, bf16[224,2,64]{2,0,1:T(8,128)(2,1)S(1)}, u32[]{:S(2)}) copy-start(bf16[224,2,64]{2,0,1:T(8,128)(2,1)S(1)} %get-tuple-element.1006) | copy-start | bytes 172036
  1238.4 238.1 %reduce-scatter.21.cloned.1.call-start = ((), (), s32[]{:S(2)}) async-start(), calls=%async_computation.25 | async-start | bytes 835584 | tf_op jit(solution)/shard_map/reduce_scatter | solution.py:444
  1301.7 253.9 %reduce-scatter.17.cloned.1.call-start = ((), (), s32[]{:S(2)}) async-start(), calls=%async_computation.23 | async-start | bytes 5013504 | tf_op jit(solution)/shard_map/reduce_scatter | solution.py:438
  1307.8 326.7 %reduce-scatter.23.cloned.1.call-start = ((), (), s32[]{:S(2)}) async-start(), calls=%async_computation.26 | async-start | bytes 5013504 | tf_op jit(solution)/shard_map/reduce_scatter | solution.py:447
  1312.9 382.4 %all-reduce.15.cloned.1.call-start = ((), (), s32[]{:S(2)}) async-start(), calls=%async_computation.31 | async-start | bytes 215040 | tf_op jit(solution)/shard_map/psum | solution.py:458
  1314.0 45.3 %copy-start.24 = (bf16[1536,256]{1,0:T(8,128)(2,1)S(1)}, bf16[1536,256]{1,0:T(8,128)(2,1)}, u32[]{:S(2)}) copy-start(bf16[1536,256]{1,0:T(8,128)(2,1)} %copy-done.23) | copy-start | bytes 2359300
  1314.0 45.3 %copy-start.40 = (bf16[224,2,64]{2,0,1:T(8,128)(2,1)S(1)}, bf16[224,2,64]{2,0,1:T(8,128)(2,1)}, u32[]{:S(2)}) copy-start(bf16[224,2,64]{2,0,1:T(8,128)(2,1)} %copy-done.39) | copy-start | bytes 172036
  1361.3 273.2 %copy-start.13 = (bf16[16,56,768]{2,1,0:T(8,128)(2,1)S(1)}, bf16[16,56,768]{2,1,0:T(8,128)(2,1)}, u32[]{:S(2)}) copy-start(bf16[16,56,768]{2,1,0:T(8,128)(2,1)} %get-tuple-element.997) | copy-start | bytes 4128772
  1476.5 225.2 %all-reduce.17.cloned.1.call-start = ((), (), s32[]{:S(2)}) async-start(), calls=%async_computation.32 | async-start | bytes 1179648 | tf_op jit(solution)/shard_map/psum | solution.py:459
  1634.5 428.4 %reduce-scatter.25.cloned.1.call-start = ((), (), s32[]{:S(2)}) async-start(), calls=%async_computation.27 | async-start | bytes 40108032 | tf_op jit(solution)/shard_map/reduce_scatter | solution.py:424
  1653.0 781.0 %reduce-scatter.27.cloned.1.call-start = ((), (), s32[]{:S(2)}) async-start(), calls=%async_computation.28 | async-start | bytes 40108032 | tf_op jit(solution)/shard_map/reduce_scatter | solution.py:427
  1672.7 1132.6 %reduce-scatter.29.cloned.1.call-start = ((), (), s32[]{:S(2)}) async-start(), calls=%async_computation.29 | async-start | bytes 40108032 | tf_op jit(solution)/shard_map/reduce_scatter | solution.py:430
  (45 other events, 111.5 us)
Sparse Core Ops, SparseCore 0:
  62.0 47.0 all-gather.8
  111.9 39.3 all-gather.12
  153.6 53.0 all-gather.10
  208.9 51.7 all-gather.14
  262.1 186.3 all-gather.16
  449.9 187.8 all-gather.18
  639.3 187.7 all-gather.20
  1148.3 87.0 reduce-scatter.12
  1239.8 59.5 reduce-scatter.14
  1303.2 54.6 reduce-scatter.30
  1361.9 55.5 reduce-scatter.18
  1420.9 55.5 reduce-scatter.20
  1481.4 74.1 reduce-scatter.16
  1559.9 74.5 reduce-scatter.22
  1638.2 21.3 all-reduce.14
  1661.9 30.2 all-reduce.16
  1696.3 366.5 reduce-scatter.24
  2067.0 366.9 reduce-scatter.26
  2438.3 366.9 reduce-scatter.28
where the time goes:
time: 2840 us; the launch traced here: 2820 us
  waiting for transfers between devices  1880 us (66%)
  matrix products  291 us (10%)
  local copies, waits for them, and re-layouts  290 us (10%)
  loops' own time  137 us (5%)
  blocking collectives  115 us (4%)
  other arithmetic  67.7 us (2%)
    reduce_scatter x1, waiting for transfers between devices, local(): lax.psum_scatter(grad_down_local.astype(jnp.bfloat16), 'dp', scatter_dime...  367 us
    reduce_scatter x1, waiting for transfers between devices, local(): lax.psum_scatter(grad_up_local.astype(jnp.bfloat16), 'dp', scatter_dimens...  367 us
    reduce_scatter x1, waiting for transfers between devices, local(): lax.psum_scatter(grad_gate_local.astype(jnp.bfloat16), 'dp', scatter_dime...  357 us
    all_gather x1, waiting for transfers between devices, local(): lax.all_gather(down_weight, 'dp', axis=1, tiled=True)  166 us
    all_gather x1, waiting for transfers between devices, local(): lax.all_gather(up_weight, 'dp', axis=1, tiled=True)  97.6 us
    reduce_scatter x1, waiting for transfers between devices, local(): lax.psum_scatter(grad_key_all.astype(jnp.bfloat16), 'dp', scatter_dimensi...  80.3 us
    reduce_scatter x1, waiting for transfers between devices, local(): lax.psum_scatter(grad_query_local.astype(jnp.bfloat16), 'dp', scatter_dim...  79 us
    reduce_scatter x1, waiting for transfers between devices, local(): lax.psum_scatter(grad_out_local.astype(jnp.bfloat16), 'dp', scatter_dimen...  78.9 us
  transfers between devices with their start and end apart: 23, of which 17 were waited for; matrix products, arithmetic and copies ran while one was open for 15% of the time, Pallas kernels for 0%

commit v1 on v0

--- a/solution.py
+++ b/solution.py
@@ -1,6 +1,10 @@
+import functools
+
 import jax
 import jax.numpy as jnp
 from jax import lax
+from jax.experimental import pallas as pl
+from jax.experimental.pallas import tpu as pltpu
 from jax.sharding import PartitionSpec as P
 
 HEADS = 12
@@ -52,7 +56,7 @@
     return (grad_rows, grad_gain)
 
 
-def local(
+def local_gathered(
     tokens,
     attn_gain,
     query_weight,
@@ -479,6 +483,420 @@
     )
 
 
+SLOTS = 32
+log2e = 1.4426950408889634
+
+
+def dot_f32(a, b, dims):
+    return lax.dot_general(a, b, (dims, ((), ())), preferred_element_type=jnp.float32)
+
+
+def attend_kernel(path_ref, query_ref, keys_ref, out_ref, exact_ref, stat_ref, acc, top, total):
+    tok_count = query_ref.shape[0]
+    repeat_heads = HEADS // KV_HEADS
+    factor = log2e * HEAD ** (-0.5)
+    segment_count = keys_ref.shape[0]
+    segment = path_ref[segment_count]
+    row = lax.broadcasted_iota(jnp.int32, (tok_count, tok_count), 0)
+    column = lax.broadcasted_iota(jnp.int32, (tok_count, tok_count), 1)
+    causal = column <= row
+
+    def visit(label, own):
+        for head in range(HEADS):
+            group = head // repeat_heads
+            query = query_ref[:, head * HEAD : (head + 1) * HEAD]
+            key = keys_ref[label, :, group * HEAD : (group + 1) * HEAD]
+            value = keys_ref[label, :, (KV_HEADS + group) * HEAD : (KV_HEADS + group + 1) * HEAD]
+            scores = dot_f32(query, key, ((1,), (1,)))
+            if own:
+                scores = jnp.where(causal, scores, -1e30)
+                peak = jnp.max(scores, axis=-1, keepdims=True)
+            else:
+                peak = jnp.maximum(top[head], jnp.max(scores, axis=-1, keepdims=True))
+            prob = jnp.exp2((scores - peak) * factor)
+            prob_high = prob.astype(jnp.bfloat16)
+            prob_low = (prob - prob_high.astype(jnp.float32)).astype(jnp.bfloat16)
+            part = dot_f32(prob_high, value, ((1,), (0,))) + dot_f32(prob_low, value, ((1,), (0,)))
+            part_total = jnp.sum(prob, axis=-1, keepdims=True)
+            if own:
+                acc[head] = part
+                total[head] = part_total
+            else:
+                fade = jnp.exp2((top[head] - peak) * factor)
+                acc[head] = acc[head] * fade + part
+                total[head] = total[head] * fade + part_total
+            top[head] = peak
+
+    visit(segment, True)
+
+    @pl.loop(0, segment_count)
+    def _(label):
+        @pl.when((path_ref[label] > 0) & (label != segment))
+        def _():
+            visit(label, False)
+
+    lane = lax.broadcasted_iota(jnp.int32, (tok_count, HEAD), 1)
+    stats = jnp.zeros((tok_count, HEAD), jnp.float32)
+    for head in range(HEADS):
+        exact = acc[head] / total[head]
+        exact_ref[:, head * HEAD : (head + 1) * HEAD] = exact
+        out_ref[:, head * HEAD : (head + 1) * HEAD] = exact.astype(jnp.bfloat16)
+        stats = jnp.where(lane == head, top[head] * factor + jnp.log2(total[head]), stats)
+    stat_ref[...] = stats
+
+
+def attend(path, query, keys):
+    tok_count = query.shape[0]
+    vmem = pl.BlockSpec(memory_space=pltpu.VMEM)
+    return pl.pallas_call(
+        attend_kernel,
+        out_shape=(
+            jax.ShapeDtypeStruct(query.shape, jnp.bfloat16),
+            jax.ShapeDtypeStruct(query.shape, jnp.float32),
+            jax.ShapeDtypeStruct((tok_count, HEAD), jnp.float32),
+        ),
+        in_specs=[pl.BlockSpec(memory_space=pltpu.SMEM), vmem, vmem],
+        out_specs=(vmem, vmem, vmem),
+        scratch_shapes=[
+            pltpu.VMEM((HEADS, tok_count, HEAD), jnp.float32),
+            pltpu.VMEM((HEADS, tok_count, 1), jnp.float32),
+            pltpu.VMEM((HEADS, tok_count, 1), jnp.float32),
+        ],
+        compiler_params=pltpu.CompilerParams(vmem_limit_bytes=40 * 1024 * 1024),
+    )(path, query, keys)
+
+
+def attend_grad_kernel(
+    path_ref, query_ref, keys_ref, grad_ref, exact_ref, stat_ref, grad_query_ref, grad_keys_ref, acc, delta
+):
+    tok_count = query_ref.shape[0]
+    repeat_heads = HEADS // KV_HEADS
+    scale = HEAD ** (-0.5)
+    factor = log2e * scale
+    segment_count = keys_ref.shape[0]
+    segment = path_ref[segment_count]
+    row = lax.broadcasted_iota(jnp.int32, (tok_count, tok_count), 0)
+    column = lax.broadcasted_iota(jnp.int32, (tok_count, tok_count), 1)
+    causal = column <= row
+    for head in range(HEADS):
+        cut = slice(head * HEAD, (head + 1) * HEAD)
+        delta[head] = jnp.sum(
+            grad_ref[:, cut].astype(jnp.float32) * exact_ref[:, cut], axis=-1, keepdims=True
+        )
+
+    def visit(label, own):
+        for group in range(KV_HEADS):
+            key_cut = slice(group * HEAD, (group + 1) * HEAD)
+            value_cut = slice((KV_HEADS + group) * HEAD, (KV_HEADS + group + 1) * HEAD)
+            key = keys_ref[label, :, key_cut]
+            value = keys_ref[label, :, value_cut]
+            grad_key = jnp.zeros((tok_count, HEAD), jnp.float32)
+            grad_value = jnp.zeros((tok_count, HEAD), jnp.float32)
+            for head in range(group * repeat_heads, (group + 1) * repeat_heads):
+                cut = slice(head * HEAD, (head + 1) * HEAD)
+                query = query_ref[:, cut]
+                grad = grad_ref[:, cut]
+                scores = dot_f32(query, key, ((1,), (1,)))
+                prob = jnp.exp2(scores * factor - stat_ref[:, head : head + 1])
+                if own:
+                    prob = jnp.where(causal, prob, 0.0)
+                grad_prob = dot_f32(grad, value, ((1,), (1,)))
+                grad_score = (prob * (grad_prob - delta[head])).astype(jnp.bfloat16)
+                grad_value += dot_f32(prob.astype(jnp.bfloat16), grad, ((0,), (0,)))
+                grad_key += dot_f32(grad_score, query, ((0,), (0,)))
+                grad_query = dot_f32(grad_score, key, ((1,), (0,)))
+                if own:
+                    acc[head] = grad_query
+                else:
+                    acc[head] += grad_query
+            grad_keys_ref[label, :, key_cut] = (grad_key * scale).astype(jnp.bfloat16)
+            grad_keys_ref[label, :, value_cut] = grad_value.astype(jnp.bfloat16)
+
+    visit(segment, True)
+
+    @pl.loop(0, segment_count)
+    def _(label):
+        @pl.when((path_ref[label] > 0) & (label != segment))
+        def _():
+            visit(label, False)
+
+        @pl.when(path_ref[label] == 0)
+        def _():
+            grad_keys_ref[label] = jnp.zeros(grad_keys_ref.shape[1:], jnp.bfloat16)
+
+    for head in range(HEADS):
+        grad_query_ref[:, head * HEAD : (head + 1) * HEAD] = acc[head] * scale
+
+
+def attend_grad(path, query, keys, grad, exact, stats):
+    tok_count = query.shape[0]
+    vmem = pl.BlockSpec(memory_space=pltpu.VMEM)
+    return pl.pallas_call(
+        attend_grad_kernel,
+        out_shape=(
+            jax.ShapeDtypeStruct(query.shape, jnp.float32),
+            jax.ShapeDtypeStruct(keys.shape, jnp.bfloat16),
+        ),
+        in_specs=[pl.BlockSpec(memory_space=pltpu.SMEM)] + [vmem] * 5,
+        out_specs=(vmem, vmem),
+        scratch_shapes=[
+            pltpu.VMEM((HEADS, tok_count, HEAD), jnp.float32),
+            pltpu.VMEM((HEADS, tok_count, 1), jnp.float32),
+        ],
+        compiler_params=pltpu.CompilerParams(vmem_limit_bytes=40 * 1024 * 1024),
+    )(path, query, keys, grad, exact, stats)
+
+
+def local_owned(
+    tokens,
+    attn_gain,
+    query_weight,
+    key_weight,
+    value_weight,
+    out_weight,
+    moe_gain,
+    router_weight,
+    gate_weight,
+    up_weight,
+    down_weight,
+    parents,
+    routes,
+    claim_order,
+    cotangent,
+):
+    tok_count = tokens.shape[1]
+    model_width = tokens.shape[2]
+    ff_width = gate_weight.shape[2]
+    segment = lax.axis_index("dp")
+    segment_count = lax.axis_size("dp")
+    everyone = ("expert", "dp")
+    device_count = segment_count * lax.axis_size("expert")
+    query_width = HEADS * HEAD
+    key_width = KV_HEADS * HEAD
+
+    expert_ids = routes[0].reshape(-1)
+    order_row = claim_order[0, 0]
+    member = (expert_ids[:, None] == jnp.arange(EXPERTS, dtype=jnp.int32)[None, :]).astype(
+        jnp.bfloat16
+    )
+    earlier = (order_row[None, :] < order_row[:, None]).astype(jnp.bfloat16)
+    before = jnp.dot(earlier, member, preferred_element_type=jnp.float32)
+    slot_index = jnp.sum(before * member.astype(jnp.float32), axis=1).astype(jnp.int32)
+    target = jnp.where(slot_index < CAP, expert_ids * SLOTS + slot_index, -1).reshape(
+        tok_count, TOP
+    )
+    row_labels = jnp.arange(EXPERTS * SLOTS, dtype=jnp.int32)
+    hits = (target[:, :, None] == row_labels[None, None, :]).astype(jnp.float32)
+    placed_rows = jnp.sum(hits, axis=1).astype(jnp.bfloat16)
+
+    def exchange(rows):
+        return lax.all_to_all(
+            rows.reshape(device_count, SLOTS, rows.shape[-1]),
+            everyone,
+            split_axis=0,
+            concat_axis=0,
+            tiled=True,
+        ).reshape(EXPERTS * SLOTS, rows.shape[-1])
+
+    grad_rows_in = exchange(
+        dot_f32(placed_rows, cotangent[0], ((0,), (0,))).astype(jnp.bfloat16)
+    )
+
+    def own(weight):
+        return lax.all_to_all(weight, "dp", split_axis=0, concat_axis=1, tiled=True)[0]
+
+    gate_own, up_own, down_own = own(gate_weight), own(up_weight), own(down_weight)
+
+    small = jnp.concatenate(
+        [
+            router_weight,
+            attn_gain[:, None],
+            moe_gain[:, None],
+            jnp.zeros((router_weight.shape[0], HEAD - EXPERTS - 2), jnp.bfloat16),
+        ],
+        axis=1,
+    )
+    small_full = lax.all_gather(small, "dp", axis=0, tiled=True)
+    router_full = small_full[:, :EXPERTS]
+    gain_first = small_full[:, EXPERTS].astype(jnp.float32)
+    gain_second = small_full[:, EXPERTS + 1].astype(jnp.float32)
+    project = lax.all_gather(
+        jnp.concatenate([query_weight, key_weight, value_weight], axis=1),
+        "dp",
+        axis=0,
+        tiled=True,
+    )
+    out_full = lax.all_gather(out_weight, "dp", axis=0, tiled=True)
+
+    reach_row = ancestry(parents[0])[segment]
+    path_depth = jnp.sum(reach_row) - 1.0
+    positions = path_depth * tok_count + jnp.arange(tok_count, dtype=jnp.float32)
+    cosine, sine_part = rope_tables(positions, HEAD)
+    path = jnp.concatenate([(reach_row > 0.5).astype(jnp.int32), segment[None].astype(jnp.int32)])
+    inputs = tokens[0].astype(jnp.float32)
+    scale_one = lax.rsqrt(jnp.mean(inputs * inputs, axis=-1, keepdims=True) + epsilon)
+    normed_one = inputs * scale_one
+    hidden_one = (normed_one * gain_first).astype(jnp.bfloat16)
+    projected = jnp.dot(hidden_one, project, preferred_element_type=jnp.float32)
+    query_rot = (
+        rotate(projected[:, :query_width].reshape(tok_count, HEADS, HEAD), cosine, sine_part)
+        .astype(jnp.bfloat16)
+        .reshape(tok_count, query_width)
+    )
+    key_rot = (
+        rotate(
+            projected[:, query_width : query_width + key_width].reshape(tok_count, KV_HEADS, HEAD),
+            cosine,
+            sine_part,
+        )
+        .astype(jnp.bfloat16)
+        .reshape(tok_count, key_width)
+    )
+    value_low = projected[:, query_width + key_width :].astype(jnp.bfloat16)
+    keys = lax.all_gather(
+        jnp.concatenate([key_rot, value_low], axis=1), "dp", axis=0, tiled=False
+    )
+    attended, exact_out, stats = attend(path, query_rot, keys)
+    middle = inputs + jnp.dot(attended, out_full, preferred_element_type=jnp.float32)
+    scale_two = lax.rsqrt(jnp.mean(middle * middle, axis=-1, keepdims=True) + epsilon)
+    normed_two = middle * scale_two
+    hidden_two = (normed_two * gain_second).astype(jnp.bfloat16)
+    rows_in = exchange(dot_f32(placed_rows, hidden_two, ((0,), (0,))).astype(jnp.bfloat16))
+    logits = jnp.dot(hidden_two, router_full, preferred_element_type=jnp.float32)
+    picked_one = (
+        routes[0][:, :, None] == jnp.arange(EXPERTS, dtype=jnp.int32)[None, None, :]
+    ).astype(jnp.float32)
+    chosen = jnp.sum(picked_one * logits[:, None, :], axis=-1)
+    gate_probs = jax.nn.softmax(chosen, axis=-1)
+    gate_rows = jnp.sum(hits * gate_probs[:, :, None], axis=(0, 1))
+    gates_in = lax.all_to_all(
+        gate_rows.reshape(device_count, SLOTS), everyone, split_axis=0, concat_axis=0, tiled=True
+    ).reshape(-1)
+
+    gate_act = jnp.dot(rows_in, gate_own, preferred_element_type=jnp.float32)
+    up_act = jnp.dot(rows_in, up_own, preferred_element_type=jnp.float32)
+    sigmoid_gate = jax.nn.sigmoid(gate_act)
+    swish = gate_act * sigmoid_gate
+    inner = (swish * up_act).astype(jnp.bfloat16)
+    expert_out = jnp.dot(inner, down_own, preferred_element_type=jnp.float32).astype(jnp.bfloat16)
+    grad_in = grad_rows_in.astype(jnp.float32)
+    grad_gate_rows = jnp.sum(expert_out.astype(jnp.float32) * grad_in, axis=-1)
+    grad_expert_out = (gates_in[:, None] * grad_in).astype(jnp.bfloat16)
+    grad_inner = dot_f32(grad_expert_out, down_own, ((1,), (1,)))
+    grad_gate_act = (
+        grad_inner * up_act * (sigmoid_gate * (1.0 + gate_act * (1.0 - sigmoid_gate)))
+    ).astype(jnp.bfloat16)
+    grad_up_act = (grad_inner * swish).astype(jnp.bfloat16)
+    grad_rows = (
+        dot_f32(grad_gate_act, gate_own, ((1,), (1,)))
+        + dot_f32(grad_up_act, up_own, ((1,), (1,)))
+    ).astype(jnp.bfloat16)
+    grad_rows_back = exchange(grad_rows)
+    grad_gates_back = lax.all_to_all(
+        grad_gate_rows.reshape(device_count, SLOTS),
+        everyone,
+        split_axis=0,
+        concat_axis=0,
+        tiled=True,
+    ).reshape(-1)
+    rows_back = exchange(expert_out)
+
+    def give(grad):
+        parts = grad.astype(jnp.bfloat16).reshape(segment_count, -1, grad.shape[-1])
+        return lax.all_to_all(parts, "dp", split_axis=0, concat_axis=0, tiled=True).astype(
+            jnp.float32
+        )
+
+    grad_down_mine = give(dot_f32(inner, grad_expert_out, ((0,), (0,))))
+    grad_gate_mine = give(dot_f32(rows_in, grad_gate_act, ((0,), (0,))))
+    grad_up_mine = give(dot_f32(rows_in, grad_up_act, ((0,), (0,))))
+
+    gate_placed = jnp.sum(hits * gate_probs[:, :, None], axis=1)
+    gate_high = gate_placed.astype(jnp.bfloat16)
+    gate_low = (gate_placed - gate_high.astype(jnp.float32)).astype(jnp.bfloat16)
+    mixture = jnp.dot(gate_high, rows_back, preferred_element_type=jnp.float32) + jnp.dot(
+        gate_low, rows_back, preferred_element_type=jnp.float32
+    )
+    block_out = (middle + mixture).astype(jnp.bfloat16)
+    grad_result = cotangent[0].astype(jnp.float32)
+    grad_gates = jnp.sum(hits * grad_gates_back[None, None, :], axis=-1)
+    grad_hidden_two = jnp.dot(placed_rows, grad_rows_back, preferred_element_type=jnp.float32)
+    grad_chosen = gate_probs * (
+        grad_gates - jnp.sum(gate_probs * grad_gates, axis=-1, keepdims=True)
+    )
+    grad_logits = jnp.sum(picked_one * grad_chosen[:, :, None], axis=1).astype(jnp.bfloat16)
+    grad_hidden_two = grad_hidden_two + dot_f32(grad_logits, router_full, ((1,), (1,)))
+    grad_router_local = dot_f32(hidden_two, grad_logits, ((0,), (0,)))
+    grad_middle_norm, grad_gain_two = norm_backward(
+        grad_hidden_two, normed_two, scale_two, gain_second
+    )
+    grad_middle = grad_result + grad_middle_norm
+    grad_branch = grad_middle.astype(jnp.bfloat16)
+    grad_out_local = dot_f32(attended, grad_branch, ((0,), (0,)))
+    grad_attended = dot_f32(grad_branch, out_full, ((1,), (1,))).astype(jnp.bfloat16)
+    grad_query_rot, grad_keys = attend_grad(
+        path, query_rot, keys, grad_attended, exact_out, stats
+    )
+    grad_keys_mine = lax.psum_scatter(
+        grad_keys.reshape(segment_count * tok_count, 2 * key_width),
+        "dp",
+        scatter_dimension=0,
+        tiled=True,
+    ).astype(jnp.float32)
+    grad_query_raw = (
+        rotate(grad_query_rot.reshape(tok_count, HEADS, HEAD), cosine, -sine_part)
+        .reshape(tok_count, query_width)
+        .astype(jnp.bfloat16)
+    )
+    grad_key_raw = (
+        rotate(grad_keys_mine[:, :key_width].reshape(tok_count, KV_HEADS, HEAD), cosine, -sine_part)
+        .reshape(tok_count, key_width)
+        .astype(jnp.bfloat16)
+    )
+    grad_projected = jnp.concatenate(
+        [grad_query_raw, grad_key_raw, grad_keys_mine[:, key_width:].astype(jnp.bfloat16)], axis=1
+    )
+    grad_project_local = dot_f32(hidden_one, grad_projected, ((0,), (0,)))
+    grad_hidden_one = dot_f32(grad_projected, project, ((1,), (1,)))
+    grad_inputs_norm, grad_gain_one = norm_backward(
+        grad_hidden_one, normed_one, scale_one, gain_first
+    )
+    grad_inputs = grad_middle + grad_inputs_norm
+
+    def scatter(grad):
+        part = lax.psum_scatter(
+            grad.astype(jnp.bfloat16), "dp", scatter_dimension=0, tiled=True
+        )
+        return lax.psum(part, "expert").astype(jnp.float32)
+
+    grad_small = jnp.concatenate(
+        [
+            grad_router_local,
+            grad_gain_one[:, None],
+            grad_gain_two[:, None],
+            jnp.zeros((model_width, HEAD - EXPERTS - 2), jnp.float32),
+        ],
+        axis=1,
+    )
+    grad_out_mine = scatter(grad_out_local)
+    grad_project_mine = scatter(jnp.concatenate([grad_project_local, grad_small], axis=1))
+    small_at = query_width + 2 * key_width
+    return (
+        block_out[None],
+        grad_inputs[None],
+        grad_project_mine[:, small_at + EXPERTS],
+        grad_project_mine[:, :query_width],
+        grad_project_mine[:, query_width : query_width + key_width],
+        grad_project_mine[:, query_width + key_width : small_at],
+        grad_out_mine,
+        grad_project_mine[:, small_at + EXPERTS + 1],
+        grad_project_mine[:, small_at : small_at + EXPERTS],
+        grad_gate_mine,
+        grad_up_mine,
+        grad_down_mine,
+    )
+
+
 def solution(mesh):
     placed = (
         P("expert", "dp", None),
@@ -497,8 +915,9 @@
         P("expert", "dp", None),
         P("expert", "dp", None),
     )
+    owned = EXPERTS // mesh.shape["expert"] == mesh.shape["dp"]
     return jax.shard_map(
-        local,
+        local_owned if owned else local_gathered,
         mesh=mesh,
         in_specs=placed,
         out_specs=(

time: 2840 us -> 1040 us (0.37)
  waiting for transfers between devices: 1880 us -> 588 us
  local copies, waits for them, and re-layouts: 290 us -> 46.9 us
  matrix products: 291 us -> 98.3 us
  loops' own time: 137 us -> 0 us
  starting transfers between devices: 21.2 us -> 83.8 us
  Pallas kernels: 0 us -> 44.7 us
  other arithmetic: 67.7 us -> 36.8 us
    reduce_scatter x9 -> x2, waiting for transfers between devices: 1480 us -> 2.85 us  [scatter(): lax.psum_scatter(grad.astype(jnp.bfloat16), 'dp', scatter_dimension=0, ti...]
    all_to_all x4 -> x10, waiting for transfers between devices: 29.1 us -> 509 us  [the longest x4 279 us: exchange(): lax.all_to_all(rows.reshape(device_count, SLOTS, rows.shape[-1]), everyon...]
    all_gather x7 -> x3, waiting for transfers between devices: 327 us -> 37.4 us  [the longest x1 37.3 us: local_owned(): lax.all_gather(jnp.concatenate([query_weight, key_weight, value_weight],...]
    dot_general x70 -> x24, matrix products: 290 us -> 97 us  [the longest x14 59.1 us: dot_f32(): lax.dot_general(a, b, (dims, ((), ())), preferred_element_type=jnp.float32)]
    another operation x51 -> x0, loops' own time: 137 us -> none  [the longest x1 42.5 us: local(): lax.scan(pass_values, (zero_out, zero_out), (key_blocks, value_blocks, se...]
    all_to_all x0 -> x2, blocking collectives: none -> 97.2 us  [the longest x1 88.2 us: own(): lax.all_to_all(weight, 'dp', split_axis=0, concat_axis=1, tiled=True)[0]]
    dynamic_slice x96 -> x0, local copies, waits for them, and re-layouts: 85.6 us -> none  [the longest x48 57.6 us: on_path(): return reach_row[label] > 0.5]
    all_to_all x4 -> x10, starting transfers between devices: 19.5 us -> 83.2 us  [the longest x4 39.9 us: exchange(): lax.all_to_all(rows.reshape(device_count, SLOTS, rows.shape[-1]), everyon...]
  transfers between devices with their start and end apart: 23 -> 17, of which waited for: 17 -> 14; matrix products, arithmetic and copies ran while one was open for 15% -> 11% of each run, Pallas kernels for 0% -> 2%
where the time goes in v1:
time: 1040 us; the launch traced here: 1030 us
  waiting for transfers between devices  588 us (57%)
  blocking collectives  118 us (11%)
  matrix products  98.3 us (9%)
  starting transfers between devices  83.8 us (8%)
  local copies, waits for them, and re-layouts  46.9 us (5%)
  Pallas kernels  44.7 us (4%)
  other arithmetic  36.8 us (4%)
  between operations  16.1 us (2%)
    all_to_all x4, waiting for transfers between devices, exchange(): lax.all_to_all(rows.reshape(device_count, SLOTS, rows.shape[-1]), everyon...  279 us
    all_to_all x3, waiting for transfers between devices, give(): lax.all_to_all(parts, 'dp', split_axis=0, concat_axis=0, tiled=True)  139 us
    all_to_all x1, blocking collectives, own(): lax.all_to_all(weight, 'dp', split_axis=0, concat_axis=1, tiled=True)[0]  88.2 us
    all_to_all x2, waiting for transfers between devices, own(): lax.all_to_all(weight, 'dp', split_axis=0, concat_axis=1, tiled=True)[0]  85.2 us
    dot_general x14, matrix products, dot_f32(): lax.dot_general(a, b, (dims, ((), ())), preferred_element_type=jnp.float32)  59.1 us
    all_to_all x4, starting transfers between devices, exchange(): lax.all_to_all(rows.reshape(device_count, SLOTS, rows.shape[-1]), everyon...  39.9 us
    all_gather x1, waiting for transfers between devices, local_owned(): lax.all_gather(jnp.concatenate([query_weight, key_weight, value_weight],...  37.3 us
    psum x1, waiting for transfers between devices, scatter(): return lax.psum(part, 'expert').astype(jnp.float32)  31.5 us
  transfers between devices with their start and end apart: 17, of which 14 were waited for; matrix products, arithmetic and copies ran while one was open for 11% of the time, Pallas kernels for 2%

profile of v1, /device:TPU:8, one launch (start us, length us, event | category | flops | bytes accessed | tf_op | source)
XLA Modules:
  0.0 1032.2 jit_solution(8156540149836732903)
XLA Ops:
  15.5 20.9 %all_gather.15 = bf16[1536,128]{1,0:T(8,128)(2,1)S(1)} all-gather(bf16[96,128]{1,0:T(8,128)(2,1)S(1)} %maximum_maximum_fusion), channel_id=1, replica_groups=mesh['dp'=16,'expert'=2] {'dp'}, dimensions={0}, use_global_device_ids=true | all-gather | bytes 417792 | tf_op jit(solution)/shard_map/all_gather | solution.py:719
  37.9 37.3 %all-gather.5.cloned.1.call-done = bf16[1536,2048]{1,0:T(8,128)(2,1)} async-done(((bf16[96,2048]{1,0:T(8,128)(2,1)}), bf16[1536,2048]{1,0:T(8,128)(2,1)}) %all-gather.5.cloned.1.call-update) | async-done | bytes 6291472 | tf_op jit(solution)/shard_map/all_gather | solution.py:723
  75.3 4.4 fusion.41
  82.7 4.9 all-to-all-start.1
  88.3 72.8 %all-to-all-done.1 = bf16[16,96,768]{2,1,0:T(8,128)(2,1)} async-done(((bf16[16,96,768]{2,1,0:T(8,128)(2,1)}), bf16[16,96,768]{2,1,0:T(8,128)(2,1)}, u32[]{:S(2)}, u32[]{:S(2)}) %all-to-all-start.1) | async-done | bytes 2359328 | tf_op jit(solution)/shard_map/all_to_all | solution.py:706
  161.2 88.2 %all_to_all.80 = bf16[16,96,768]{2,1,0:T(8,128)(2,1)} all-to-all(bf16[16,96,768]{2,1,0:T(8,128)(2,1)S(1)} %copy-done.21), channel_id=1, replica_groups=mesh['dp'=16,'expert'=2] {'dp'}, dimensions={0} | all-to-all | bytes 4718592 | tf_op jit(solution)/shard_map/all_to_all | solution.py:706
  249.4 5.5 all-to-all-start.3
  262.5 22.6 %shard_map.238 = (bf16[224,1536]{1,0:T(8,128)(2,1)S(1)}, f32[224,1536]{1,0:T(8,128)S(1)}, f32[224,128]{1,0:T(8,128)S(1)}) custom-call(s32[17]{0:T(128)S(1)} %pad_add_fusion.path_ref, bf16[224,1536]{1,0:T(8,128)(2,1)S(1)} %copy.102.query_ref, bf16[16,224,512]{2,1,0:T(8,128)(2,1)S(1)} %bitcast.103), custom_call_target="tpu_custom_call" | custom-call | tf_op jit(solution)/shard_map/pallas_call | solution.py:551
  285.2 3.8 multiply_reduce_fusion.2
  293.8 12.4 %all-to-all-done.3 = bf16[16,48,1536]{2,1,0:T(8,128)(2,1)} async-done(((bf16[16,48,1536]{2,1,0:T(8,128)(2,1)}), bf16[16,48,1536]{2,1,0:T(8,128)(2,1)}, u32[]{:S(2)}, u32[]{:S(2)}) %all-to-all-start.3) | async-done | bytes 2359328 | tf_op jit(solution)/shard_map/all_to_all | solution.py:706
  306.2 15.9 %all-to-all-start = ((bf16[32,32,1536]{2,1,0:T(8,128)(2,1)}), bf16[32,32,1536]{2,1,0:T(8,128)(2,1)}, u32[]{:S(2)}, u32[]{:S(2)}) async-start(bf16[32,32,1536]{2,1,0:T(8,128)(2,1)} %bitcast.109), calls=%async_computation | async-start | bytes 6291456 | tf_op jit(solution)/shard_map/all_to_all | solution.py:693
  322.1 3.8 convolution_convert_fusion.2
  325.9 65.6 %all-to-all-done = bf16[32,32,1536]{2,1,0:T(8,128)(2,1)} async-done(((bf16[32,32,1536]{2,1,0:T(8,128)(2,1)}), bf16[32,32,1536]{2,1,0:T(8,128)(2,1)}, u32[]{:S(2)}, u32[]{:S(2)}) %all-to-all-start) | async-done | bytes 3145760 | tf_op jit(solution)/shard_map/all_to_all | solution.py:693
  391.4 7.0 all-to-all-start.6
  400.1 5.4 fusion.68
  407.2 6.8 multiply_convert_fusion.2
  414.0 53.9 %all-to-all-done.6 = bf16[32,32,1536]{2,1,0:T(8,128)(2,1)} async-done(((bf16[32,32,1536]{2,1,0:T(8,128)(2,1)}), bf16[32,32,1536]{2,1,0:T(8,128)(2,1)}, u32[]{:S(2)}, u32[]{:S(2)}) %all-to-all-start.6) | async-done | bytes 3145760 | tf_op jit(solution)/shard_map/all_to_all | solution.py:693
  467.9 7.3 fusion.1
  475.9 5.6 all-to-all-start.8
  481.6 5.9 all-to-all-done.8
  491.1 9.0 all_to_all.81
  503.9 5.1 multiply_convert_fusion
  509.0 5.5 fusion.69
  514.5 4.1 add_convert_fusion
  518.6 4.7 all-to-all-start.7
  526.0 66.9 %all-to-all-done.7 = bf16[32,32,1536]{2,1,0:T(8,128)(2,1)} async-done(((bf16[32,32,1536]{2,1,0:T(8,128)(2,1)}), bf16[32,32,1536]{2,1,0:T(8,128)(2,1)}, u32[]{:S(2)}, u32[]{:S(2)}) %all-to-all-start.7) | async-done | bytes 3145760 | tf_op jit(solution)/shard_map/all_to_all | solution.py:693
  592.8 3.9 multiply_reduce_fusion
  597.2 4.4 convolution_convert_fusion.8.grad_ref
  601.6 22.1 %shard_map.239 = (f32[224,1536]{1,0:T(8,128)S(1)}, bf16[16,224,512]{2,1,0:T(8,128)(2,1)S(1)}) custom-call(s32[17]{0:T(128)S(1)} %pad_add_fusion.path_ref, bf16[224,1536]{1,0:T(8,128)(2,1)S(1)} %copy.102.query_ref, bf16[16,224,512]{2,1,0:T(8,128)(2,1)S(1)} %bitcast.104, bf16[224,1536]{1,0:T(8,128)(2,1)S(1)} %convolution_convert_fusion.8.grad_ref, ...), custom_call_target="tpu_custom_call" | custom-call | tf_op jit(solution)/shard_map/pallas_call | solution.py:634
  628.0 6.0 convolution_convert_fusion.7
  634.0 13.3 %all-to-all-start.9 = ((bf16[16,96,768]{2,1,0:T(8,128)(2,1)}), bf16[16,96,768]{2,1,0:T(8,128)(2,1)}, u32[]{:S(2)}, u32[]{:S(2)}) async-start(bf16[16,96,768]{2,1,0:T(8,128)(2,1)} %bitcast.121), calls=%async_computation.11 | async-start | bytes 4718592 | tf_op jit(solution)/shard_map/all_to_all | solution.py:806
  647.4 3.5 convolution_convert_fusion.1
  652.4 6.1 convolution_convert_fusion.6
  658.5 55.1 %all-to-all-done.9 = bf16[16,96,768]{2,1,0:T(8,128)(2,1)} async-done(((bf16[16,96,768]{2,1,0:T(8,128)(2,1)}), bf16[16,96,768]{2,1,0:T(8,128)(2,1)}, u32[]{:S(2)}, u32[]{:S(2)}) %all-to-all-start.9) | async-done | bytes 2359328 | tf_op jit(solution)/shard_map/all_to_all | solution.py:806
  713.6 7.1 all-to-all-start.10
  725.9 3.9 convolution_convert_fusion.5
  731.9 5.9 reduce-scatter.10.cloned.1.call-done
  741.3 35.6 %all-to-all-done.10 = bf16[16,96,768]{2,1,0:T(8,128)(2,1)} async-done(((bf16[16,96,768]{2,1,0:T(8,128)(2,1)}), bf16[16,96,768]{2,1,0:T(8,128)(2,1)}, u32[]{:S(2)}, u32[]{:S(2)}) %all-to-all-start.10) | async-done | bytes 2359328 | tf_op jit(solution)/shard_map/all_to_all | solution.py:806
  776.8 6.9 all-to-all-start.11
  786.3 6.6 fusion.21
  794.0 4.6 convolution_convert_fusion
  798.7 11.2 %concatenate.44 = bf16[1536,2176]{1,0:T(8,128)(2,1)} concatenate(bf16[1536,2048]{1,0:T(8,128)(2,1)} %convolution_convert_fusion, bf16[1536,32]{1,0:T(8,128)(2,1)} %copy.114, bf16[1536,1]{1,0:T(8,128)(2,1)} %broadcast_in_dim.66, bf16[1536,1]{1,0:T(8,128)(2,1)S(1)} %broadcast_in_dim.67, bf16[1536,94]{1,0:T(8,128)(2,1)S(1)} %broadcast_in_dim.33), dimensions={1} | concatenate | bytes 13369344 | tf_op jit(solution)/shard_map/concatenate | solution.py:882
  809.9 48.8 %all-to-all-done.11 = bf16[16,48,1536]{2,1,0:T(8,128)(2,1)S(1)} async-done(((bf16[16,48,1536]{2,1,0:T(8,128)(2,1)}), bf16[16,48,1536]{2,1,0:T(8,128)(2,1)S(1)}, u32[]{:S(2)}, u32[]{:S(2)}) %all-to-all-start.11) | async-done | bytes 2359328 | tf_op jit(solution)/shard_map/all_to_all | solution.py:806
  860.2 12.3 %all-to-all-start.4 = ((bf16[32,32,1536]{2,1,0:T(8,128)(2,1)}), bf16[32,32,1536]{2,1,0:T(8,128)(2,1)S(1)}, u32[]{:S(2)}, u32[]{:S(2)}) async-start(bf16[32,32,1536]{2,1,0:T(8,128)(2,1)} %bitcast.114), calls=%async_computation.4 | async-start | bytes 6291456 | tf_op jit(solution)/shard_map/all_to_all | solution.py:693
  872.8 4.5 convert_element_type.229
  877.4 4.7 convert_element_type.231
  884.9 92.3 %all-to-all-done.4 = bf16[32,32,1536]{2,1,0:T(8,128)(2,1)S(1)} async-done(((bf16[32,32,1536]{2,1,0:T(8,128)(2,1)}), bf16[32,32,1536]{2,1,0:T(8,128)(2,1)S(1)}, u32[]{:S(2)}, u32[]{:S(2)}) %all-to-all-start.4) | async-done | bytes 3145760 | tf_op jit(solution)/shard_map/all_to_all | solution.py:693
  987.4 31.5 %all-reduce.3.cloned.1.call-done = (bf16[96,2176]{1,0:T(8,128)(2,1)}, bf16[96,1536]{1,0:T(8,128)(2,1)}) async-done(((bf16[96,2176]{1,0:T(8,128)(2,1)}, bf16[96,1536]{1,0:T(8,128)(2,1)}), (bf16[96,2176]{1,0:T(8,128)(2,1)}, bf16[96,1536]{1,0:T(8,128)(2,1)})) %all-reduce.3.cloned.1.call-update) | async-done | bytes 712720 | tf_op jit(solution)/shard_map/psum | solution.py:870
  (208 shorter events, 80.4 us)
Async XLA Ops:
  7.2 30.5 %copy-start.16 = (bf16[1,224,1536]{2,1,0:T(8,128)(2,1)S(1)}, bf16[1,224,1536]{2,1,0:T(8,128)(2,1)}, u32[]{:S(2)}) copy-start(bf16[1,224,1536]{2,1,0:T(8,128)(2,1)} %param.15) | copy-start | bytes 2064388
  7.2 68.1 %all-gather.5.cloned.1.call-start = ((), (), s32[]{:S(2)}) async-start(), calls=%async_computation.15 | async-start | bytes 6684672 | tf_op jit(solution)/shard_map/all_gather | solution.py:723
  9.1 251.3 %all-gather.9.cloned.1.call-start = ((), (), s32[]{:S(2)}) async-start(), calls=%async_computation.19 | async-start | bytes 3899392 | tf_op jit(solution)/shard_map/all_gather | solution.py:756
  15.3 65.8 %copy-start.26 = (f32[224,64]{1,0:T(8,128)}, f32[224,64]{1,0:T(8,128)S(1)}, u32[]{:S(2)}) copy-start(f32[224,64]{1,0:T(8,128)S(1)} %copy.100) | copy-start | bytes 172036
  37.7 42.0 %copy-start.32 = (f32[1536]{0:T(1024)}, f32[1536]{0:T(1024)S(1)}, u32[]{:S(2)}) copy-start(f32[1536]{0:T(1024)S(1)} %get-tuple-element.89) | copy-start | bytes 18436
  37.9 41.8 %copy-start.34 = (f32[224]{0:T(256)}, f32[224]{0:T(256)S(1)}, u32[]{:S(2)}) copy-start(f32[224]{0:T(256)S(1)} %add_rsqrt_fusion.1) | copy-start | bytes 2692
  82.7 78.5 %copy-start.21 = (bf16[16,96,768]{2,1,0:T(8,128)(2,1)S(1)}, bf16[16,96,768]{2,1,0:T(8,128)(2,1)}, u32[]{:S(2)}) copy-start(bf16[16,96,768]{2,1,0:T(8,128)(2,1)} %param.24) | copy-start | bytes 7077892
  82.7 78.5 %all-to-all-start.1 = ((bf16[16,96,768]{2,1,0:T(8,128)(2,1)}), bf16[16,96,768]{2,1,0:T(8,128)(2,1)}, u32[]{:S(2)}, u32[]{:S(2)}) async-start(bf16[16,96,768]{2,1,0:T(8,128)(2,1)} %param.23), calls=%async_computation.1 | async-start | bytes 4718592 | tf_op jit(solution)/shard_map/all_to_all | solution.py:706
  87.6 197.6 %all-gather.7.cloned.1.call-start = ((), (), s32[]{:S(2)}) async-start(), calls=%async_computation.16 | async-start | bytes 5013504 | tf_op jit(solution)/shard_map/all_gather | solution.py:729
  249.4 5.5 copy-start.37
  249.4 5.5 copy-start.36
  249.4 7.4 copy-start.25
  249.4 56.8 %all-to-all-start.3 = ((bf16[16,48,1536]{2,1,0:T(8,128)(2,1)}), bf16[16,48,1536]{2,1,0:T(8,128)(2,1)}, u32[]{:S(2)}, u32[]{:S(2)}) async-start(bf16[16,48,1536]{2,1,0:T(8,128)(2,1)} %param.25), calls=%async_computation.3 | async-start | bytes 4718592 | tf_op jit(solution)/shard_map/all_to_all | solution.py:706
  306.2 85.3 %all-to-all-start = ((bf16[32,32,1536]{2,1,0:T(8,128)(2,1)}), bf16[32,32,1536]{2,1,0:T(8,128)(2,1)}, u32[]{:S(2)}, u32[]{:S(2)}) async-start(bf16[32,32,1536]{2,1,0:T(8,128)(2,1)} %bitcast.109), calls=%async_computation | async-start | bytes 6291456 | tf_op jit(solution)/shard_map/all_to_all | solution.py:693
  391.4 76.5 %all-to-all-start.6 = ((bf16[32,32,1536]{2,1,0:T(8,128)(2,1)}), bf16[32,32,1536]{2,1,0:T(8,128)(2,1)}, u32[]{:S(2)}, u32[]{:S(2)}) async-start(bf16[32,32,1536]{2,1,0:T(8,128)(2,1)} %bitcast.108), calls=%async_computation.6 | async-start | bytes 6291456 | tf_op jit(solution)/shard_map/all_to_all | solution.py:693
  400.1 7.0 copy-start.22
  475.9 11.5 %all-to-all-start.8 = ((f32[32,1,32]{2,1,0:T(1,128)}), f32[32,1,32]{2,1,0:T(1,128)S(1)}, u32[]{:S(2)}, u32[]{:S(2)}) async-start(f32[32,1,32]{2,1,0:T(1,128)} %all_to_all.63), calls=%async_computation.8 | async-start | bytes 32768 | tf_op jit(solution)/shard_map/all_to_all | solution.py:795
  500.1 3.8 copy-start.45
  509.0 5.5 copy-start.39
  509.0 5.5 copy-start.43
  509.0 5.5 copy-start.23
  518.6 74.2 %all-to-all-start.7 = ((bf16[32,32,1536]{2,1,0:T(8,128)(2,1)}), bf16[32,32,1536]{2,1,0:T(8,128)(2,1)}, u32[]{:S(2)}, u32[]{:S(2)}) async-start(bf16[32,32,1536]{2,1,0:T(8,128)(2,1)} %bitcast.115), calls=%async_computation.7 | async-start | bytes 6291456 | tf_op jit(solution)/shard_map/all_to_all | solution.py:693
  523.4 214.4 %reduce-scatter.10.cloned.1.call-start = ((), (), s32[]{:S(2)}) async-start(), calls=%async_computation.20 | async-start | bytes 3899392
  592.8 3.9 copy-start.6
  592.8 3.9 copy-start.20
  597.1 4.5 copy-start.8
  597.2 4.5 copy-start.1
  634.0 13.4 %copy-start.9 = (f32[224,1536]{1,0:T(8,128)S(1)}, f32[224,1536]{1,0:T(8,128)}, u32[]{:S(2)}) copy-start(f32[224,1536]{1,0:T(8,128)} %copy-done.8) | copy-start | bytes 4128772
  634.0 79.6 %all-to-all-start.9 = ((bf16[16,96,768]{2,1,0:T(8,128)(2,1)}), bf16[16,96,768]{2,1,0:T(8,128)(2,1)}, u32[]{:S(2)}, u32[]{:S(2)}) async-start(bf16[16,96,768]{2,1,0:T(8,128)(2,1)} %bitcast.121), calls=%async_computation.11 | async-start | bytes 4718592 | tf_op jit(solution)/shard_map/all_to_all | solution.py:806
  647.3 333.9 %reduce-scatter.8.cloned.1.call-start = ((), (), s32[]{:S(2)}) async-start(), calls=%async_computation.18 | async-start | bytes 5013504 | tf_op jit(solution)/shard_map/reduce_scatter | solution.py:867
  713.6 7.1 copy-start.28
  713.6 7.8 copy-start.11
  713.6 63.2 %all-to-all-start.10 = ((bf16[16,96,768]{2,1,0:T(8,128)(2,1)}), bf16[16,96,768]{2,1,0:T(8,128)(2,1)}, u32[]{:S(2)}, u32[]{:S(2)}) async-start(bf16[16,96,768]{2,1,0:T(8,128)(2,1)} %bitcast.34), calls=%async_computation.12 | async-start | bytes 4718592 | tf_op jit(solution)/shard_map/all_to_all | solution.py:806
  725.9 4.0 copy-start.4
  776.8 7.0 copy-start.27
  776.8 9.4 copy-start.17
  776.8 81.9 %all-to-all-start.11 = ((bf16[16,48,1536]{2,1,0:T(8,128)(2,1)}), bf16[16,48,1536]{2,1,0:T(8,128)(2,1)S(1)}, u32[]{:S(2)}, u32[]{:S(2)}) async-start(bf16[16,48,1536]{2,1,0:T(8,128)(2,1)} %bitcast.120), calls=%async_computation.13 | async-start | bytes 4718592 | tf_op jit(solution)/shard_map/all_to_all | solution.py:806
  783.7 200.3 %reduce-scatter.6.cloned.1.call-start = ((), (), s32[]{:S(2)}) async-start(), calls=%async_computation.17 | async-start | bytes 7102464 | tf_op jit(solution)/shard_map/reduce_scatter | solution.py:867
  786.3 7.7 copy-start.19
  786.3 7.7 copy-start.29
  786.3 7.7 copy-start.30
  786.3 7.7 copy-start.33
  786.3 7.7 copy-start.35
  860.2 117.0 %all-to-all-start.4 = ((bf16[32,32,1536]{2,1,0:T(8,128)(2,1)}), bf16[32,32,1536]{2,1,0:T(8,128)(2,1)S(1)}, u32[]{:S(2)}, u32[]{:S(2)}) async-start(bf16[32,32,1536]{2,1,0:T(8,128)(2,1)} %bitcast.114), calls=%async_computation.4 | async-start | bytes 6291456 | tf_op jit(solution)/shard_map/all_to_all | solution.py:693
  872.5 146.5 %all-reduce.3.cloned.1.call-start = ((), (), s32[]{:S(2)}) async-start(), calls=%async_computation.21 | async-start | bytes 1425408 | tf_op jit(solution)/shard_map/psum | solution.py:870
  877.4 4.7 copy-start.14
  1019.0 3.0 copy-start.18
  1019.0 4.4 copy-start.31
  (15 other events, 24.7 us)
Sparse Core Ops, SparseCore 0:
  10.9 64.3 all-gather.4
  82.8 74.4 all-gather.8
  159.6 80.4 all-gather.6
  626.8 110.9 reduce-scatter.9
  741.9 113.5 reduce-scatter.7
  859.4 124.6 reduce-scatter.5
  986.4 32.5 all-reduce.2

commit v2 on v1

--- a/solution.py
+++ b/solution.py
@@ -484,19 +484,391 @@
 
 
 SLOTS = 32
+PAD_TOKENS = 32
+LANES = 128
+WAVE_FIRST = 3
+TILE = 256
+MESH = pl.DeviceIdType.MESH
 log2e = 1.4426950408889634
 
 
-def dot_f32(a, b, dims):
+def dot_f32(a, b, dims=((1,), (0,))):
     return lax.dot_general(a, b, (dims, ((), ())), preferred_element_type=jnp.float32)
 
 
-def attend_kernel(path_ref, query_ref, keys_ref, out_ref, exact_ref, stat_ref, acc, top, total):
-    tok_count = query_ref.shape[0]
+def split3(value):
+    high = value.astype(jnp.bfloat16)
+    rest = value - high.astype(jnp.float32)
+    middle = rest.astype(jnp.bfloat16)
+    low = (rest - middle.astype(jnp.float32)).astype(jnp.bfloat16)
+    return high, middle, low
+
+
+def one_hot(shape, test):
+    row = lax.broadcasted_iota(jnp.int32, shape, 0)
+    column = lax.broadcasted_iota(jnp.int32, shape, 1)
+    return jnp.where(test(row, column), 1.0, 0.0).astype(jnp.bfloat16)
+
+
+class Place:
+    def __init__(self):
+        self.dp = lax.axis_index("dp")
+        self.side = lax.axis_index("expert")
+        self.z = self.dp // 4
+        self.x = (self.dp // 2) % 2
+        self.c = self.dp % 2
+
+    def index(self, z, x, c):
+        return z * 4 + x * 2 + c
+
+    def others(self):
+        return [self.z + 1 - 2 * (self.z % 2), (self.z + 2) % 4, 3 - self.z]
+
+
+def remote(src, dst, send, recv, dp, side):
+    return pltpu.make_async_remote_copy(
+        src_ref=src,
+        dst_ref=dst,
+        send_sem=send,
+        recv_sem=recv,
+        device_id={"dp": dp, "expert": side},
+        device_id_type=MESH,
+    )
+
+
+def enter(device_count, dp_count):
+    rank = lax.axis_index("expert") * dp_count + lax.axis_index("dp")
+    barrier = pltpu.get_barrier_semaphore()
+
+    @pl.loop(1, device_count)
+    def _(step):
+        other = (rank + step) % device_count
+        pl.semaphore_signal(
+            barrier,
+            inc=1,
+            device_id={"dp": other % dp_count, "expert": other // dp_count},
+            device_id_type=MESH,
+        )
+
+    pl.semaphore_wait(barrier, device_count - 1)
+
+
+class Gather:
+    def __init__(self, place, own, slot, send, recv, local):
+        self.place, self.own, self.slot = place, own, slot
+        self.send, self.recv, self.local = send, recv, local
+
+    def copy(self, z, x, c, to_x, to_c, number, own=False, to_z=None):
+        p = self.place
+        shard = p.index(z, x, c)
+        target = p.index(p.z if to_z is None else to_z, to_x, to_c)
+        source = self.own if own else self.slot(shard)
+        return remote(
+            source, self.slot(shard), self.send.at[number], self.recv.at[shard], target, p.side
+        )
+
+    def first(self):
+        p = self.place
+        out = [
+            self.copy(p.z, p.x, p.c, p.x, p.c, 2 + i, own=True, to_z=z)
+            for i, z in enumerate(p.others())
+        ]
+        out.append(self.copy(p.z, p.x, p.c, 1 - p.x, p.c, 1, own=True))
+        out.append(self.copy(p.z, p.x, p.c, p.x, 1 - p.c, 0, own=True))
+        return out
+
+    def second(self, i):
+        p = self.place
+        z = p.others()[i]
+        return [
+            self.copy(z, p.x, p.c, 1 - p.x, p.c, 5 + 2 * i),
+            self.copy(z, p.x, p.c, p.x, 1 - p.c, 6 + 2 * i),
+        ]
+
+    def third(self, i):
+        p = self.place
+        z = ([p.z] + p.others())[i]
+        return self.copy(z, 1 - p.x, p.c, p.x, 1 - p.c, 11 + i)
+
+    def own_copy(self):
+        p = self.place
+        return pltpu.make_async_copy(self.own, self.slot(p.dp), self.local)
+
+    def start(self):
+        for copy in self.first():
+            copy.start()
+        self.own_copy().start()
+
+    def forward_z(self):
+        for i in range(3):
+            copies = self.second(i)
+            copies[0].wait_recv()
+            for copy in copies:
+                copy.start()
+
+    def forward_x(self):
+        for i in range(4):
+            copy = self.third(i)
+            copy.wait_recv()
+            copy.start()
+
+    def finish(self):
+        p = self.place
+        for z in range(4):
+            for x in range(2):
+                self.copy(z, x, 1 - p.c, p.x, 1 - p.c, 0).wait_recv()
+        for copy in self.first():
+            copy.wait_send()
+        for i in range(3):
+            for copy in self.second(i):
+                copy.wait_send()
+        for i in range(4):
+            self.third(i).wait_send()
+        self.own_copy().wait()
+
+
+class RowSwap:
+    def __init__(self, source, target, send, recv, local, dp_count, device_count):
+        self.source, self.target = source, target
+        self.send, self.recv, self.local = send, recv, local
+        self.dp_count, self.device_count = dp_count, device_count
+        self.rank = lax.axis_index("expert") * dp_count + lax.axis_index("dp")
+
+    def block(self, ref, index):
+        return ref.at[pl.ds(pl.multiple_of(index * SLOTS, SLOTS), SLOTS)]
+
+    def copy(self, step, to, landing):
+        return remote(
+            self.block(self.source, to),
+            self.block(self.target, landing),
+            self.send.at[step],
+            self.recv.at[step],
+            to % self.dp_count,
+            to // self.dp_count,
+        )
+
+    def own_copy(self):
+        return pltpu.make_async_copy(
+            self.block(self.source, self.rank), self.block(self.target, self.rank), self.local
+        )
+
+    def start(self):
+        @pl.loop(1, self.device_count)
+        def _(step):
+            self.copy(step, (self.rank + step) % self.device_count, self.rank).start()
+
+        self.own_copy().start()
+
+    def finish(self):
+        @pl.loop(1, self.device_count)
+        def _(step):
+            other = (self.rank + self.device_count - step) % self.device_count
+            self.copy(step, other, other).wait()
+
+        self.own_copy().wait()
+
+
+class WeightSwap:
+    def __init__(self, place, pairs, send, recv, local, dp_count):
+        self.place, self.pairs = place, pairs
+        self.send, self.recv, self.local = send, recv, local
+        self.dp_count = dp_count
+
+    def copies(self, step, to, landing):
+        out = []
+        for i, (source, target) in enumerate(self.pairs):
+            rows = source.shape[1]
+            out.append(
+                remote(
+                    source.at[to],
+                    target.at[pl.ds(pl.multiple_of(landing * rows, rows), rows)],
+                    self.send.at[step, i],
+                    self.recv.at[step, i],
+                    to,
+                    self.place.side,
+                )
+            )
+        return out
+
+    def own_copies(self):
+        dp = self.place.dp
+        return [
+            pltpu.make_async_copy(
+                source.at[dp],
+                target.at[pl.ds(pl.multiple_of(dp * source.shape[1], source.shape[1]), source.shape[1])],
+                self.local.at[i],
+            )
+            for i, (source, target) in enumerate(self.pairs)
+        ]
+
+    def start(self, low, high):
+        @pl.loop(low, high)
+        def _(step):
+            for copy in self.copies(step, (self.place.dp + step) % self.dp_count, self.place.dp):
+                copy.start()
+
+    def start_own(self):
+        for copy in self.own_copies():
+            copy.start()
+
+    def finish(self):
+        @pl.loop(1, self.dp_count)
+        def _(step):
+            other = (self.place.dp + self.dp_count - step) % self.dp_count
+            for copy in self.copies(step, other, other):
+                copy.wait()
+
+        for copy in self.own_copies():
+            copy.wait()
+
+
+def columns(tile, width=TILE):
+    return pl.ds(pl.multiple_of(tile * width, width), width)
+
+
+def rows_of(index, count):
+    return pl.ds(pl.multiple_of(index * count, count), count)
+
+
+def front_kernel(
+    bias_ref,
+    tokens_ref,
+    cotangent_ref,
+    project_ref,
+    out_ref,
+    placed_ref,
+    mask_ref,
+    cosine_ref,
+    sine_ref,
+    gate_ref,
+    up_ref,
+    down_ref,
+    project_full,
+    out_full,
+    keys_ref,
+    query_ref,
+    attended_ref,
+    exact_ref,
+    stat_ref,
+    middle_ref,
+    hidden_ref,
+    probs_ref,
+    rows_in,
+    grads_in,
+    gate_own,
+    up_own,
+    down_own,
+    keys_own,
+    hidden_one,
+    row_send,
+    grad_send,
+    extended,
+    acc,
+    top,
+    total,
+    project_send,
+    project_recv,
+    out_send,
+    out_recv,
+    keys_send,
+    keys_recv,
+    row_send_sem,
+    row_recv_sem,
+    grad_send_sem,
+    grad_recv_sem,
+    weight_send,
+    weight_recv,
+    weight_local,
+    local,
+):
+    dp_count = keys_ref.shape[0]
+    device_count = row_send.shape[0] // SLOTS
+    tok_count, model_width = tokens_ref.shape
+    query_width = HEADS * HEAD
+    key_width = KV_HEADS * HEAD
     repeat_heads = HEADS // KV_HEADS
     factor = log2e * HEAD ** (-0.5)
-    segment_count = keys_ref.shape[0]
-    segment = path_ref[segment_count]
+    place = Place()
+    shard_rows = project_ref.shape[0]
+
+    def shard_of(full):
+        return lambda index: full.at[rows_of(index, shard_rows)]
+
+    project = Gather(
+        place, project_ref, shard_of(project_full), project_send, project_recv, local.at[0]
+    )
+    out = Gather(place, out_ref, shard_of(out_full), out_send, out_recv, local.at[1])
+    keys = Gather(
+        place, keys_own, lambda index: keys_ref.at[index], keys_send, keys_recv, local.at[2]
+    )
+    rows = RowSwap(row_send, rows_in, row_send_sem, row_recv_sem, local.at[3], dp_count, device_count)
+    grads = RowSwap(
+        grad_send, grads_in, grad_send_sem, grad_recv_sem, local.at[4], dp_count, device_count
+    )
+    weights = WeightSwap(
+        place,
+        ((gate_ref, gate_own), (up_ref, up_own), (down_ref, down_own)),
+        weight_send,
+        weight_recv,
+        weight_local,
+        dp_count,
+    )
+
+    enter(device_count, dp_count)
+    project.start()
+    weights.start(1, WAVE_FIRST)
+
+    @pl.loop(0, model_width // TILE)
+    def _(tile):
+        grad_send[:, columns(tile)] = dot_f32(
+            placed_ref[:, :tok_count], cotangent_ref[:, columns(tile)]
+        ).astype(jnp.bfloat16)
+
+    project.forward_z()
+    project.forward_x()
+    project.finish()
+
+    lanes_of = one_hot((8, LANES), lambda row, column: column == row + EXPERTS)
+    gains = dot_f32(lanes_of, project_full[:, query_width + 2 * key_width :], ((1,), (1,)))
+    gain_first, gain_second = gains[0:1], gains[1:2]
+    chunk = 32
+
+    @pl.loop(0, tok_count // chunk)
+    def _(index):
+        value = tokens_ref[rows_of(index, chunk)].astype(jnp.float32)
+        scale = lax.rsqrt(jnp.mean(value * value, axis=-1, keepdims=True) + epsilon)
+        hidden_one[rows_of(index, chunk)] = (value * scale * gain_first).astype(jnp.bfloat16)
+
+    def turned(tile):
+        value = dot_f32(hidden_one[...], project_full[:, columns(tile)])
+        halves = []
+        for half in range(TILE // HEAD):
+            part = value[:, half * HEAD : (half + 1) * HEAD]
+            halves.append(
+                part * cosine_ref[...] + pltpu.roll(part, HEAD // 2, 1) * sine_ref[...]
+            )
+        return jnp.concatenate(halves, axis=1).astype(jnp.bfloat16)
+
+    keys_own[:, :key_width] = turned(query_width // TILE)
+    keys_own[:, key_width:] = dot_f32(
+        hidden_one[...], project_full[:, query_width + key_width : query_width + 2 * key_width]
+    ).astype(jnp.bfloat16)
+    keys.start()
+
+    @pl.loop(0, query_width // TILE)
+    def _(tile):
+        query_ref[:, columns(tile)] = turned(tile)
+
+    keys.forward_z()
+    keys.forward_x()
+    keys.finish()
+    out.start()
+    weights.start(WAVE_FIRST, dp_count)
+    weights.start_own()
+    out.forward_z()
+    out.forward_x()
+    grads.start()
+
     row = lax.broadcasted_iota(jnp.int32, (tok_count, tok_count), 0)
     column = lax.broadcasted_iota(jnp.int32, (tok_count, tok_count), 1)
     causal = column <= row
@@ -511,12 +883,15 @@
             if own:
                 scores = jnp.where(causal, scores, -1e30)
                 peak = jnp.max(scores, axis=-1, keepdims=True)
+                shift = peak
             else:
-                peak = jnp.maximum(top[head], jnp.max(scores, axis=-1, keepdims=True))
-            prob = jnp.exp2((scores - peak) * factor)
+                bias = bias_ref[label]
+                peak = jnp.maximum(top[head], jnp.max(scores, axis=-1, keepdims=True) + bias)
+                shift = peak - bias
+            prob = jnp.exp2((scores - shift) * factor)
             prob_high = prob.astype(jnp.bfloat16)
             prob_low = (prob - prob_high.astype(jnp.float32)).astype(jnp.bfloat16)
-            part = dot_f32(prob_high, value, ((1,), (0,))) + dot_f32(prob_low, value, ((1,), (0,)))
+            part = dot_f32(prob_high, value) + dot_f32(prob_low, value)
             part_total = jnp.sum(prob, axis=-1, keepdims=True)
             if own:
                 acc[head] = part
@@ -527,43 +902,122 @@
                 total[head] = total[head] * fade + part_total
             top[head] = peak
 
-    visit(segment, True)
-
-    @pl.loop(0, segment_count)
+    visit(place.dp, True)
+
+    @pl.loop(0, place.dp)
     def _(label):
-        @pl.when((path_ref[label] > 0) & (label != segment))
-        def _():
-            visit(label, False)
-
-    lane = lax.broadcasted_iota(jnp.int32, (tok_count, HEAD), 1)
-    stats = jnp.zeros((tok_count, HEAD), jnp.float32)
+        visit(label, False)
+
+    lane = lax.broadcasted_iota(jnp.int32, (tok_count, LANES), 1)
+    stats = jnp.zeros((tok_count, LANES), jnp.float32)
     for head in range(HEADS):
         exact = acc[head] / total[head]
         exact_ref[:, head * HEAD : (head + 1) * HEAD] = exact
-        out_ref[:, head * HEAD : (head + 1) * HEAD] = exact.astype(jnp.bfloat16)
+        attended_ref[:, head * HEAD : (head + 1) * HEAD] = exact.astype(jnp.bfloat16)
         stats = jnp.where(lane == head, top[head] * factor + jnp.log2(total[head]), stats)
     stat_ref[...] = stats
-
-
-def attend(path, query, keys):
-    tok_count = query.shape[0]
+    out.finish()
+
+    @pl.loop(0, model_width // TILE)
+    def _(tile):
+        middle_ref[:, columns(tile)] = tokens_ref[:, columns(tile)].astype(jnp.float32) + dot_f32(
+            attended_ref[...], out_full[:, columns(tile)]
+        )
+
+    @pl.loop(0, tok_count // chunk)
+    def _(index):
+        value = middle_ref[rows_of(index, chunk)]
+        scale = lax.rsqrt(jnp.mean(value * value, axis=-1, keepdims=True) + epsilon)
+        hidden_ref[rows_of(index, chunk)] = (value * scale * gain_second).astype(jnp.bfloat16)
+
+    router = project_full[:, query_width + 2 * key_width :]
+    logits = jnp.where(mask_ref[...] > 0, dot_f32(hidden_ref[...], router), -1e30)
+    weight = jnp.exp(logits - jnp.max(logits, axis=-1, keepdims=True))
+    probs = weight / jnp.sum(weight, axis=-1, keepdims=True)
+    probs_ref[...] = probs
+    spread = sum(dot_f32(placed_ref[:, :tok_count], part) for part in split3(probs))
+    slot_row = lax.broadcasted_iota(jnp.int32, spread.shape, 0)
+    slot_lane = lax.broadcasted_iota(jnp.int32, spread.shape, 1)
+    gate = jnp.sum(jnp.where(slot_lane == slot_row // SLOTS, spread, 0.0), axis=-1, keepdims=True)
+    high, mid, low = split3(gate)
+    part = jnp.where(
+        slot_lane < SLOTS,
+        high.astype(jnp.float32),
+        jnp.where(slot_lane < 2 * SLOTS, mid.astype(jnp.float32), low.astype(jnp.float32)),
+    )
+    part = jnp.where(
+        (slot_lane % SLOTS == slot_row % SLOTS) & (slot_lane < 3 * SLOTS), part, 0.0
+    ).astype(jnp.bfloat16)
+    fold = one_hot((device_count, row_send.shape[0]), lambda r, col: col // SLOTS == r)
+    extended[:tok_count] = hidden_ref[...]
+    extended[tok_count:] = jnp.zeros((PAD_TOKENS, model_width), jnp.bfloat16)
+    extended[tok_count:, :LANES] = dot_f32(fold, part).astype(jnp.bfloat16)
+
+    @pl.loop(0, model_width // TILE)
+    def _(tile):
+        row_send[:, columns(tile)] = dot_f32(placed_ref[...], extended[:, columns(tile)]).astype(
+            jnp.bfloat16
+        )
+
+    rows.start()
+    weights.finish()
+    grads.finish()
+    rows.finish()
+
+
+def front(bias, tokens, cotangent, project, out, placed, mask, cosine, sine, gate, up, down):
+    dp_count = lax.axis_size("dp")
+    device_count = dp_count * lax.axis_size("expert")
+    tok_count, model_width = tokens.shape
+    query_width = HEADS * HEAD
+    key_width = KV_HEADS * HEAD
     vmem = pl.BlockSpec(memory_space=pltpu.VMEM)
+    anywhere = pl.BlockSpec(memory_space=pl.ANY)
+    slots = device_count * SLOTS
+    low, full = jnp.bfloat16, jnp.float32
+    shape = jax.ShapeDtypeStruct
+    ff_width = gate.shape[2]
+    outs = (
+        (shape((model_width, project.shape[1]), low), vmem),
+        (shape((model_width, model_width), low), vmem),
+        (shape((dp_count, tok_count, 2 * key_width), low), vmem),
+        (shape((tok_count, query_width), low), vmem),
+        (shape((tok_count, query_width), low), vmem),
+        (shape((tok_count, query_width), full), vmem),
+        (shape((tok_count, LANES), full), vmem),
+        (shape((tok_count, model_width), full), vmem),
+        (shape((tok_count, model_width), low), vmem),
+        (shape((tok_count, LANES), full), vmem),
+        (shape((slots, model_width), low), anywhere),
+        (shape((slots, model_width), low), anywhere),
+        (shape((model_width, ff_width), low), anywhere),
+        (shape((model_width, ff_width), low), anywhere),
+        (shape((ff_width, model_width), low), anywhere),
+    )
+    dma = pltpu.SemaphoreType.DMA
     return pl.pallas_call(
-        attend_kernel,
-        out_shape=(
-            jax.ShapeDtypeStruct(query.shape, jnp.bfloat16),
-            jax.ShapeDtypeStruct(query.shape, jnp.float32),
-            jax.ShapeDtypeStruct((tok_count, HEAD), jnp.float32),
+        front_kernel,
+        out_shape=tuple(o[0] for o in outs),
+        in_specs=[pl.BlockSpec(memory_space=pltpu.SMEM)] + [vmem] * 8 + [anywhere] * 3,
+        out_specs=tuple(o[1] for o in outs),
+        scratch_shapes=[
+            pltpu.VMEM((tok_count, 2 * key_width), low),
+            pltpu.VMEM((tok_count, model_width), low),
+            pltpu.VMEM((slots, model_width), low),
+            pltpu.VMEM((slots, model_width), low),
+            pltpu.VMEM((tok_count + PAD_TOKENS, model_width), low),
+            pltpu.VMEM((HEADS, tok_count, HEAD), full),
+            pltpu.VMEM((HEADS, tok_count, 1), full),
+            pltpu.VMEM((HEADS, tok_count, 1), full),
+        ]
+        + [dma((15,)), dma((dp_count,))] * 3
+        + [dma((device_count,))] * 4
+        + [dma((dp_count, 3))] * 2
+        + [dma((3,)), dma((5,))],
+        compiler_params=pltpu.CompilerParams(
+            collective_id=0, has_side_effects=True, vmem_limit_bytes=58 * 1024 * 1024
         ),
-        in_specs=[pl.BlockSpec(memory_space=pltpu.SMEM), vmem, vmem],
-        out_specs=(vmem, vmem, vmem),
-        scratch_shapes=[
-            pltpu.VMEM((HEADS, tok_count, HEAD), jnp.float32),
-            pltpu.VMEM((HEADS, tok_count, 1), jnp.float32),
-            pltpu.VMEM((HEADS, tok_count, 1), jnp.float32),
-        ],
-        compiler_params=pltpu.CompilerParams(vmem_limit_bytes=40 * 1024 * 1024),
-    )(path, query, keys)
+    )(bias, tokens, cotangent, project, out, placed, mask, cosine, sine, gate, up, down)
 
 
 def attend_grad_kernel(
@@ -674,7 +1128,8 @@
     query_width = HEADS * HEAD
     key_width = KV_HEADS * HEAD
 
-    expert_ids = routes[0].reshape(-1)
+    route_rows = routes[0]
+    expert_ids = route_rows.reshape(-1)
     order_row = claim_order[0, 0]
     member = (expert_ids[:, None] == jnp.arange(EXPERTS, dtype=jnp.int32)[None, :]).astype(
         jnp.bfloat16
@@ -686,8 +1141,86 @@
         tok_count, TOP
     )
     row_labels = jnp.arange(EXPERTS * SLOTS, dtype=jnp.int32)
-    hits = (target[:, :, None] == row_labels[None, None, :]).astype(jnp.float32)
-    placed_rows = jnp.sum(hits, axis=1).astype(jnp.bfloat16)
+    placed_rows = sum(
+        (target[:, c : c + 1] == row_labels[None, :]).astype(jnp.bfloat16) for c in range(TOP)
+    )
+    turned_target = target.T
+    placed_by_slot = sum(
+        (turned_target[c : c + 1] == row_labels[:, None]).astype(jnp.bfloat16) for c in range(TOP)
+    )
+    spare = row_labels[:, None] == (jnp.arange(EXPERTS) * SLOTS + CAP)[None, :]
+    placed_by_slot = jnp.concatenate([placed_by_slot, spare.astype(jnp.bfloat16)], axis=1)
+    experts_row = jnp.arange(LANES, dtype=jnp.int32)[None, :]
+    mask = sum((route_rows[:, c : c + 1] == experts_row).astype(jnp.float32) for c in range(TOP))
+
+    small = jnp.concatenate(
+        [
+            router_weight,
+            attn_gain[:, None],
+            moe_gain[:, None],
+            jnp.zeros((router_weight.shape[0], LANES - EXPERTS - 2), jnp.bfloat16),
+        ],
+        axis=1,
+    )
+    project_shard = jnp.concatenate([query_weight, key_weight, value_weight, small], axis=1)
+    reach_row = ancestry(parents[0])[segment]
+    path_depth = jnp.sum(reach_row) - 1.0
+    positions = path_depth * tok_count + jnp.arange(tok_count, dtype=jnp.float32)
+    cosine, sine_part = rope_tables(positions, HEAD)
+    cosine_wide = jnp.concatenate([cosine[:, 0], cosine[:, 0]], axis=1)
+    sine_wide = jnp.concatenate([-sine_part[:, 0], sine_part[:, 0]], axis=1)
+    on_path = reach_row > 0.5
+    bias = jnp.where(on_path, 0.0, -1e30).astype(jnp.float32)
+    path = jnp.concatenate([on_path.astype(jnp.int32), segment[None].astype(jnp.int32)])
+    (
+        project_full,
+        out_full,
+        keys,
+        query_rot,
+        attended,
+        exact_out,
+        stats,
+        middle,
+        hidden_two,
+        probs,
+        rows_in,
+        grad_rows_in,
+        gate_own,
+        up_own,
+        down_own,
+    ) = front(
+        bias,
+        tokens[0],
+        cotangent[0],
+        project_shard,
+        out_weight,
+        placed_by_slot,
+        mask,
+        cosine_wide,
+        sine_wide,
+        gate_weight,
+        up_weight,
+        down_weight,
+    )
+    small_at = query_width + 2 * key_width
+    project = project_full[:, :small_at]
+    small_full = project_full[:, small_at:]
+    router_full = small_full[:, :EXPERTS]
+    gain_first = small_full[:, EXPERTS].astype(jnp.float32)
+    gain_second = small_full[:, EXPERTS + 1].astype(jnp.float32)
+    inputs = tokens[0].astype(jnp.float32)
+    scale_one = lax.rsqrt(jnp.mean(inputs * inputs, axis=-1, keepdims=True) + epsilon)
+    normed_one = inputs * scale_one
+    hidden_one = (normed_one * gain_first).astype(jnp.bfloat16)
+    scale_two = lax.rsqrt(jnp.mean(middle * middle, axis=-1, keepdims=True) + epsilon)
+    normed_two = middle * scale_two
+    gate_probs = probs[:, :EXPERTS]
+    gate_parts = rows_in.reshape(device_count, SLOTS, model_width)[:, CAP, : 3 * SLOTS]
+    gates_in = jnp.sum(
+        gate_parts.reshape(device_count, 3, SLOTS).astype(jnp.float32), axis=1
+    ).reshape(-1)
+    spare_row = (jnp.arange(EXPERTS * SLOTS) % SLOTS >= CAP)[:, None]
+    rows_in = jnp.where(spare_row, jnp.zeros_like(rows_in), rows_in)
 
     def exchange(rows):
         return lax.all_to_all(
@@ -697,81 +1230,6 @@
             concat_axis=0,
             tiled=True,
         ).reshape(EXPERTS * SLOTS, rows.shape[-1])
-
-    grad_rows_in = exchange(
-        dot_f32(placed_rows, cotangent[0], ((0,), (0,))).astype(jnp.bfloat16)
-    )
-
-    def own(weight):
-        return lax.all_to_all(weight, "dp", split_axis=0, concat_axis=1, tiled=True)[0]
-
-    gate_own, up_own, down_own = own(gate_weight), own(up_weight), own(down_weight)
-
-    small = jnp.concatenate(
-        [
-            router_weight,
-            attn_gain[:, None],
-            moe_gain[:, None],
-            jnp.zeros((router_weight.shape[0], HEAD - EXPERTS - 2), jnp.bfloat16),
-        ],
-        axis=1,
-    )
-    small_full = lax.all_gather(small, "dp", axis=0, tiled=True)
-    router_full = small_full[:, :EXPERTS]
-    gain_first = small_full[:, EXPERTS].astype(jnp.float32)
-    gain_second = small_full[:, EXPERTS + 1].astype(jnp.float32)
-    project = lax.all_gather(
-        jnp.concatenate([query_weight, key_weight, value_weight], axis=1),
-        "dp",
-        axis=0,
-        tiled=True,
-    )
-    out_full = lax.all_gather(out_weight, "dp", axis=0, tiled=True)
-
-    reach_row = ancestry(parents[0])[segment]
-    path_depth = jnp.sum(reach_row) - 1.0
-    positions = path_depth * tok_count + jnp.arange(tok_count, dtype=jnp.float32)
-    cosine, sine_part = rope_tables(positions, HEAD)
-    path = jnp.concatenate([(reach_row > 0.5).astype(jnp.int32), segment[None].astype(jnp.int32)])
-    inputs = tokens[0].astype(jnp.float32)
-    scale_one = lax.rsqrt(jnp.mean(inputs * inputs, axis=-1, keepdims=True) + epsilon)
-    normed_one = inputs * scale_one
-    hidden_one = (normed_one * gain_first).astype(jnp.bfloat16)
-    projected = jnp.dot(hidden_one, project, preferred_element_type=jnp.float32)
-    query_rot = (
-        rotate(projected[:, :query_width].reshape(tok_count, HEADS, HEAD), cosine, sine_part)
-        .astype(jnp.bfloat16)
-        .reshape(tok_count, query_width)
-    )
-    key_rot = (
-        rotate(
-            projected[:, query_width : query_width + key_width].reshape(tok_count, KV_HEADS, HEAD),
-            cosine,
-            sine_part,
-        )
-        .astype(jnp.bfloat16)
-        .reshape(tok_count, key_width)
-    )
-    value_low = projected[:, query_width + key_width :].astype(jnp.bfloat16)
-    keys = lax.all_gather(
-        jnp.concatenate([key_rot, value_low], axis=1), "dp", axis=0, tiled=False
-    )
-    attended, exact_out, stats = attend(path, query_rot, keys)
-    middle = inputs + jnp.dot(attended, out_full, preferred_element_type=jnp.float32)
-    scale_two = lax.rsqrt(jnp.mean(middle * middle, axis=-1, keepdims=True) + epsilon)
-    normed_two = middle * scale_two
-    hidden_two = (normed_two * gain_second).astype(jnp.bfloat16)
-    rows_in = exchange(dot_f32(placed_rows, hidden_two, ((0,), (0,))).astype(jnp.bfloat16))
-    logits = jnp.dot(hidden_two, router_full, preferred_element_type=jnp.float32)
-    picked_one = (
-        routes[0][:, :, None] == jnp.arange(EXPERTS, dtype=jnp.int32)[None, None, :]
-    ).astype(jnp.float32)
-    chosen = jnp.sum(picked_one * logits[:, None, :], axis=-1)
-    gate_probs = jax.nn.softmax(chosen, axis=-1)
-    gate_rows = jnp.sum(hits * gate_probs[:, :, None], axis=(0, 1))
-    gates_in = lax.all_to_all(
-        gate_rows.reshape(device_count, SLOTS), everyone, split_axis=0, concat_axis=0, tiled=True
-    ).reshape(-1)
 
     gate_act = jnp.dot(rows_in, gate_own, preferred_element_type=jnp.float32)
     up_act = jnp.dot(rows_in, up_own, preferred_element_type=jnp.float32)
@@ -811,7 +1269,7 @@
     grad_gate_mine = give(dot_f32(rows_in, grad_gate_act, ((0,), (0,))))
     grad_up_mine = give(dot_f32(rows_in, grad_up_act, ((0,), (0,))))
 
-    gate_placed = jnp.sum(hits * gate_probs[:, :, None], axis=1)
+    gate_placed = jnp.repeat(gate_probs, SLOTS, axis=1) * placed_rows.astype(jnp.float32)
     gate_high = gate_placed.astype(jnp.bfloat16)
     gate_low = (gate_placed - gate_high.astype(jnp.float32)).astype(jnp.bfloat16)
     mixture = jnp.dot(gate_high, rows_back, preferred_element_type=jnp.float32) + jnp.dot(
@@ -819,12 +1277,17 @@
     )
     block_out = (middle + mixture).astype(jnp.bfloat16)
     grad_result = cotangent[0].astype(jnp.float32)
-    grad_gates = jnp.sum(hits * grad_gates_back[None, None, :], axis=-1)
+    grad_gates = jnp.sum(
+        (placed_rows.astype(jnp.float32) * grad_gates_back[None, :]).reshape(
+            tok_count, EXPERTS, SLOTS
+        ),
+        axis=-1,
+    )
     grad_hidden_two = jnp.dot(placed_rows, grad_rows_back, preferred_element_type=jnp.float32)
     grad_chosen = gate_probs * (
         grad_gates - jnp.sum(gate_probs * grad_gates, axis=-1, keepdims=True)
     )
-    grad_logits = jnp.sum(picked_one * grad_chosen[:, :, None], axis=1).astype(jnp.bfloat16)
+    grad_logits = grad_chosen.astype(jnp.bfloat16)
     grad_hidden_two = grad_hidden_two + dot_f32(grad_logits, router_full, ((1,), (1,)))
     grad_router_local = dot_f32(hidden_two, grad_logits, ((0,), (0,)))
     grad_middle_norm, grad_gain_two = norm_backward(
@@ -880,7 +1343,6 @@
     )
     grad_out_mine = scatter(grad_out_local)
     grad_project_mine = scatter(jnp.concatenate([grad_project_local, grad_small], axis=1))
-    small_at = query_width + 2 * key_width
     return (
         block_out[None],
         grad_inputs[None],

time: 1040 us -> 1010 us (0.971)
  Pallas kernels: 44.7 us -> 441 us
  waiting for transfers between devices: 588 us -> 330 us
  blocking collectives: 118 us -> 0 us
  starting transfers between devices: 83.8 us -> 58.9 us
  local copies, waits for them, and re-layouts: 46.9 us -> 36.2 us
    pallas_call x1, Pallas kernels: 22.6 us -> 419 us  [front(): pl.pallas_call(front_kernel, out_shape=tuple((o[0] for o in outs)), in_sp...]
    all_to_all x4 -> x2, waiting for transfers between devices: 279 us -> 152 us  [exchange(): lax.all_to_all(rows.reshape(device_count, SLOTS, rows.shape[-1]), everyon...]
    all_to_all x2 -> x0, blocking collectives: 97.2 us -> none  [the longest x1 88.2 us: own(): lax.all_to_all(weight, 'dp', split_axis=0, concat_axis=1, tiled=True)[0]]
    all_to_all x2 -> x0, waiting for transfers between devices: 85.2 us -> none  [own(): lax.all_to_all(weight, 'dp', split_axis=0, concat_axis=1, tiled=True)[0]]
    all_gather x3 -> x0, waiting for transfers between devices: 37.4 us -> none  [the longest x1 37.3 us: local_owned(): lax.all_gather(jnp.concatenate([query_weight, key_weight, value_weight],...]
    all_to_all x4 -> x2, starting transfers between devices: 39.9 us -> 11.3 us  [exchange(): lax.all_to_all(rows.reshape(device_count, SLOTS, rows.shape[-1]), everyon...]
    all_gather x1 -> x0, blocking collectives: 20.9 us -> none  [local_owned(): small_full = lax.all_gather(small, 'dp', axis=0, tiled=True)]
    all_to_all x3, starting transfers between devices: 27.3 us -> 40.1 us  [give(): lax.all_to_all(parts, 'dp', split_axis=0, concat_axis=0, tiled=True)]
  transfers between devices with their start and end apart: 17 -> 10, of which waited for: 14 -> 7; matrix products, arithmetic and copies ran while one was open for 11% -> 10% of each run, Pallas kernels for 2% -> 0%
where the time goes in v2:
time: 1010 us; the launch traced here: 1000 us
  Pallas kernels  441 us (44%)
  waiting for transfers between devices  330 us (33%)
  matrix products  90.6 us (9%)
  starting transfers between devices  58.9 us (6%)
  local copies, waits for them, and re-layouts  36.2 us (4%)
  other arithmetic  31.6 us (3%)
  between operations  15.6 us (2%)
    pallas_call x1, Pallas kernels, front(): pl.pallas_call(front_kernel, out_shape=tuple((o[0] for o in outs)), in_sp...  419 us
    all_to_all x2, waiting for transfers between devices, exchange(): lax.all_to_all(rows.reshape(device_count, SLOTS, rows.shape[-1]), everyon...  152 us
    all_to_all x3, waiting for transfers between devices, give(): lax.all_to_all(parts, 'dp', split_axis=0, concat_axis=0, tiled=True)  144 us
    dot_general x12, matrix products, dot_f32(): lax.dot_general(a, b, (dims, ((), ())), preferred_element_type=jnp.float32)  62.1 us
    all_to_all x3, starting transfers between devices, give(): lax.all_to_all(parts, 'dp', split_axis=0, concat_axis=0, tiled=True)  40.1 us
    psum x1, waiting for transfers between devices, scatter(): return lax.psum(part, 'expert').astype(jnp.float32)  31.8 us
    pallas_call x1, Pallas kernels, attend_grad(): pl.pallas_call(attend_grad_kernel, out_shape=(jax.ShapeDtypeStruct(query....  22.1 us
  transfers between devices with their start and end apart: 10, of which 7 were waited for; matrix products, arithmetic and copies ran while one was open for 10% of the time, Pallas kernels for 0%

profile of v2, /device:TPU:8, one launch (start us, length us, event | category | flops | bytes accessed | tf_op | source)
XLA Modules:
  0.0 1003.7 jit_solution(10144535163888569923)
XLA Ops:
  20.6 419.2 %shard_map.238 = (bf16[1536,2176]{1,0:T(8,128)(2,1)}, bf16[1536,1536]{1,0:T(8,128)(2,1)}, bf16[16,224,512]{2,1,0:T(8,128)(2,1)}, bf16[224,1536]{1,0:T(8,128)(2,1...) custom-call(f32[16]{0:T(128)} %get-tuple-element.142.bias_ref, ...), custom_call_target="tpu_custom_call" | custom-call | tf_op jit(solution)/shard_map/pallas_call | solution.py:998
  439.9 7.1 fusion.98
  447.0 4.3 fusion.97
  451.6 9.8 multiply_convert_fusion
  461.4 4.0 fusion.1
  466.1 7.1 all-to-all-start.2
  473.2 4.9 fusion.102
  478.2 4.1 add_convert_fusion
  482.2 5.9 all-to-all-start.1
  488.7 2.4 convert_reduce_fusion
  492.7 1.4 fusion.71
  494.1 63.4 %all-to-all-done.1 = bf16[32,32,1536]{2,1,0:T(8,128)(2,1)} async-done(((bf16[32,32,1536]{2,1,0:T(8,128)(2,1)}), bf16[32,32,1536]{2,1,0:T(8,128)(2,1)}, u32[]{:S(2)}, u32[]{:S(2)}) %all-to-all-start.1) | async-done | bytes 3145760 | tf_op jit(solution)/shard_map/all_to_all | solution.py:1226
  557.5 4.0 multiply_reduce_fusion
  562.0 4.4 convolution_convert_fusion.6.grad_ref
  566.5 22.1 %shard_map.239 = (f32[224,1536]{1,0:T(8,128)S(1)}, bf16[16,224,512]{2,1,0:T(8,128)(2,1)S(1)}) custom-call(s32[17]{0:T(128)S(1)} %pad_add_fusion.path_ref, bf16[224,1536]{1,0:T(8,128)(2,1)S(1)} %copy-done.3, bf16[16,224,512]{2,1,0:T(8,128)(2,1)S(1)} %copy-done.1, bf16[224,1536]{1,0:T(8,128)(2,1)S(1)} %convolution_convert_fusion.6.grad_ref, ...), custom_call_target="tpu_custom_call" | custom-call | tf_op jit(solution)/shard_map/pallas_call | solution.py:1088
  588.5 1.8 copy-done
  591.1 6.6 convolution_convert_fusion.5
  597.6 25.5 %all-to-all-start.3 = ((bf16[16,96,768]{2,1,0:T(8,128)(2,1)}), bf16[16,96,768]{2,1,0:T(8,128)(2,1)}, u32[]{:S(2)}, u32[]{:S(2)}) async-start(bf16[16,96,768]{2,1,0:T(8,128)(2,1)} %bitcast.93), calls=%async_computation.5 | async-start | bytes 4718592 | tf_op jit(solution)/shard_map/all_to_all | solution.py:1264
  623.1 5.0 convolution_convert_fusion.1
  628.8 6.6 convolution_convert_fusion.4
  635.4 60.0 %all-to-all-done.3 = bf16[16,96,768]{2,1,0:T(8,128)(2,1)} async-done(((bf16[16,96,768]{2,1,0:T(8,128)(2,1)}), bf16[16,96,768]{2,1,0:T(8,128)(2,1)}, u32[]{:S(2)}, u32[]{:S(2)}) %all-to-all-start.3) | async-done | bytes 2359328 | tf_op jit(solution)/shard_map/all_to_all | solution.py:1264
  695.4 7.5 all-to-all-start.4
  703.0 1.6 copy.98
  705.5 6.6 convolution_convert_fusion.3
  712.1 58.7 %all-to-all-done.4 = bf16[16,96,768]{2,1,0:T(8,128)(2,1)} async-done(((bf16[16,96,768]{2,1,0:T(8,128)(2,1)}), bf16[16,96,768]{2,1,0:T(8,128)(2,1)}, u32[]{:S(2)}, u32[]{:S(2)}) %all-to-all-start.4) | async-done | bytes 2359328 | tf_op jit(solution)/shard_map/all_to_all | solution.py:1264
  770.8 7.1 all-to-all-start.5
  777.9 2.0 convolution_convert_fusion.7
  779.9 1.8 copy.102
  781.8 1.6 copy.96
  783.7 1.6 subtract_convert_fusion
  785.5 1.7 fusion.100
  788.1 1.7 copy.109
  790.8 6.2 fusion.23
  798.0 4.6 convolution_convert_fusion
  802.7 11.2 %concatenate.38 = bf16[1536,2176]{1,0:T(8,128)(2,1)} concatenate(bf16[1536,2048]{1,0:T(8,128)(2,1)} %convolution_convert_fusion, bf16[1536,32]{1,0:T(8,128)(2,1)} %copy.102, bf16[1536,1]{1,0:T(8,128)(2,1)} %broadcast_in_dim.96, bf16[1536,1]{1,0:T(8,128)(2,1)S(1)} %broadcast_in_dim.97, bf16[1536,94]{1,0:T(8,128)(2,1)S(1)} %broadcast_in_dim.95), dimensions={1} | concatenate | bytes 13369344 | tf_op jit(solution)/shard_map/concatenate | solution.py:1345
  813.9 24.9 %all-to-all-done.5 = bf16[16,48,1536]{2,1,0:T(8,128)(2,1)} async-done(((bf16[16,48,1536]{2,1,0:T(8,128)(2,1)}), bf16[16,48,1536]{2,1,0:T(8,128)(2,1)}, u32[]{:S(2)}, u32[]{:S(2)}) %all-to-all-start.5) | async-done | bytes 2359328 | tf_op jit(solution)/shard_map/all_to_all | solution.py:1264
  838.8 5.4 all-to-all-start
  844.7 4.6 convert_element_type.274
  849.2 4.5 convert_element_type.276
  853.8 4.7 convert_element_type.278
  858.5 88.3 %all-to-all-done = bf16[32,32,1536]{2,1,0:T(8,128)(2,1)} async-done(((bf16[32,32,1536]{2,1,0:T(8,128)(2,1)}), bf16[32,32,1536]{2,1,0:T(8,128)(2,1)}, u32[]{:S(2)}, u32[]{:S(2)}) %all-to-all-start) | async-done | bytes 3145760 | tf_op jit(solution)/shard_map/all_to_all | solution.py:1226
  946.9 3.0 convolution_bitcast_fusion
  949.9 3.9 fusion.10
  953.9 2.2 reduce-scatter.6.cloned.1.call-done
  956.1 2.8 fusion.21
  958.9 31.8 %all-reduce.3.cloned.1.call-done = (bf16[96,2176]{1,0:T(8,128)(2,1)}, bf16[96,1536]{1,0:T(8,128)(2,1)}) async-done(((bf16[96,2176]{1,0:T(8,128)(2,1)}, bf16[96,1536]{1,0:T(8,128)(2,1)}), (bf16[96,2176]{1,0:T(8,128)(2,1)}, bf16[96,1536]{1,0:T(8,128)(2,1)})) %all-reduce.3.cloned.1.call-update) | async-done | bytes 712720 | tf_op jit(solution)/shard_map/psum | solution.py:1333
  990.8 1.1 convert_element_type.270
  991.9 1.8 slice.146
  (165 shorter events, 25.5 us)
Async XLA Ops:
  7.2 439.7 %copy-start.40 = (pred[1024]{0:T(1024)(128)(4,1)}, pred[1024]{0:T(1024)(128)(4,1)S(1)}, u32[]{:S(2)}) copy-start(pred[1024]{0:T(1024)(128)(4,1)S(1)} %fusion.84) | copy-start | bytes 3076
  13.4 6.3 copy-start.18
  13.4 6.3 copy-start.23
  13.4 6.3 copy-start.24
  18.0 421.8 %copy-start.12 = (f32[224,64]{1,0:T(8,128)}, f32[224,64]{1,0:T(8,128)S(1)}, u32[]{:S(2)}) copy-start(f32[224,64]{1,0:T(8,128)S(1)} %get-tuple-element.143) | copy-start | bytes 172036
  439.9 7.1 copy-start.35
  439.9 7.1 copy-start.37
  451.6 9.8 copy-start.34
  451.6 9.8 copy-start.36
  451.6 9.8 copy-start.39
  466.1 16.2 %all-to-all-start.2 = ((f32[32,1,32]{2,1,0:T(1,128)}), f32[32,1,32]{2,1,0:T(1,128)S(1)}, u32[]{:S(2)}, u32[]{:S(2)}) async-start(f32[32,1,32]{2,1,0:T(1,128)} %all_to_all.23), calls=%async_computation.2 | async-start | bytes 32768 | tf_op jit(solution)/shard_map/all_to_all | solution.py:1253
  473.2 4.9 copy-start.38
  473.2 4.9 copy-start.44
  482.2 8.8 copy-start.5
  482.2 75.3 %all-to-all-start.1 = ((bf16[32,32,1536]{2,1,0:T(8,128)(2,1)}), bf16[32,32,1536]{2,1,0:T(8,128)(2,1)}, u32[]{:S(2)}, u32[]{:S(2)}) async-start(bf16[32,32,1536]{2,1,0:T(8,128)(2,1)} %bitcast.89), calls=%async_computation.1 | async-start | bytes 6291456 | tf_op jit(solution)/shard_map/all_to_all | solution.py:1226
  488.1 297.3 %reduce-scatter.10.cloned.1.call-start = ((), (), s32[]{:S(2)}) async-start(), calls=%async_computation.11 | async-start | bytes 3899392
  488.3 5.8 copy-start.20
  488.6 68.9 %copy-start.25 = (s32[224]{0:T(256)}, s32[224]{0:T(256)S(1)}, u32[]{:S(2)}) copy-start(s32[224]{0:T(256)S(1)} %get-tuple-element.114) | copy-start | bytes 2692
  488.6 68.9 %copy-start.27 = (s32[224]{0:T(256)}, s32[224]{0:T(256)S(1)}, u32[]{:S(2)}) copy-start(s32[224]{0:T(256)S(1)} %get-tuple-element.115) | copy-start | bytes 2692
  488.7 68.9 %copy-start.29 = (s32[224]{0:T(256)}, s32[224]{0:T(256)S(1)}, u32[]{:S(2)}) copy-start(s32[224]{0:T(256)S(1)} %get-tuple-element.116) | copy-start | bytes 2692
  488.7 68.9 %copy-start.31 = (s32[224]{0:T(256)}, s32[224]{0:T(256)S(1)}, u32[]{:S(2)}) copy-start(s32[224]{0:T(256)S(1)} %get-tuple-element.117) | copy-start | bytes 2692
  492.7 68.8 %copy-start.15 = (bf16[224,32]{1,0:T(8,128)(2,1)}, bf16[224,32]{1,0:T(8,128)(2,1)S(1)}, u32[]{:S(2)}) copy-start(bf16[224,32]{1,0:T(8,128)(2,1)S(1)} %get-tuple-element.139) | copy-start | bytes 43012
  561.9 4.5 copy-start.7
  561.9 4.5 copy-start.1
  561.9 4.5 copy-start.2
  562.0 4.5 copy-start.3
  562.0 4.5 copy-start.4
  597.6 25.5 %copy-start.11 = (bf16[224,1536]{1,0:T(8,128)(2,1)S(1)}, bf16[224,1536]{1,0:T(8,128)(2,1)}, u32[]{:S(2)}) copy-start(bf16[224,1536]{1,0:T(8,128)(2,1)} %get-tuple-element.45) | copy-start | bytes 2064388
  597.6 97.8 %all-to-all-start.3 = ((bf16[16,96,768]{2,1,0:T(8,128)(2,1)}), bf16[16,96,768]{2,1,0:T(8,128)(2,1)}, u32[]{:S(2)}, u32[]{:S(2)}) async-start(bf16[16,96,768]{2,1,0:T(8,128)(2,1)} %bitcast.93), calls=%async_computation.5 | async-start | bytes 4718592 | tf_op jit(solution)/shard_map/all_to_all | solution.py:1264
  623.1 330.8 %reduce-scatter.8.cloned.1.call-start = ((), (), s32[]{:S(2)}) async-start(), calls=%async_computation.10 | async-start | bytes 5013504 | tf_op jit(solution)/shard_map/reduce_scatter | solution.py:1330
  695.4 9.9 copy-start.6
  695.4 75.4 %all-to-all-start.4 = ((bf16[16,96,768]{2,1,0:T(8,128)(2,1)}), bf16[16,96,768]{2,1,0:T(8,128)(2,1)}, u32[]{:S(2)}, u32[]{:S(2)}) async-start(bf16[16,96,768]{2,1,0:T(8,128)(2,1)} %bitcast.92), calls=%async_computation.6 | async-start | bytes 4718592 | tf_op jit(solution)/shard_map/all_to_all | solution.py:1264
  770.8 68.0 %all-to-all-start.5 = ((bf16[16,48,1536]{2,1,0:T(8,128)(2,1)}), bf16[16,48,1536]{2,1,0:T(8,128)(2,1)}, u32[]{:S(2)}, u32[]{:S(2)}) async-start(bf16[16,48,1536]{2,1,0:T(8,128)(2,1)} %bitcast.91), calls=%async_computation.7 | async-start | bytes 4718592 | tf_op jit(solution)/shard_map/all_to_all | solution.py:1264
  777.9 5.5 copy-start.33
  777.9 5.8 copy-start.13
  777.9 178.2 %reduce-scatter.6.cloned.1.call-start = ((), (), s32[]{:S(2)}) async-start(), calls=%async_computation.9 | async-start | bytes 7102464 | tf_op jit(solution)/shard_map/reduce_scatter | solution.py:1330
  783.7 7.1 copy-start.14
  785.3 5.5 copy-start.22
  838.8 5.8 copy-start.17
  838.8 108.0 %all-to-all-start = ((bf16[32,32,1536]{2,1,0:T(8,128)(2,1)}), bf16[32,32,1536]{2,1,0:T(8,128)(2,1)}, u32[]{:S(2)}, u32[]{:S(2)}) async-start(bf16[32,32,1536]{2,1,0:T(8,128)(2,1)} %bitcast.88), calls=%async_computation | async-start | bytes 6291456 | tf_op jit(solution)/shard_map/all_to_all | solution.py:1226
  844.3 146.5 %all-reduce.3.cloned.1.call-start = ((), (), s32[]{:S(2)}) async-start(), calls=%async_computation.12 | async-start | bytes 1425408 | tf_op jit(solution)/shard_map/psum | solution.py:1333
  853.8 93.1 %copy-start.21 = (s32[32,32]{1,0:T(8,128)S(1)}, s32[32,32]{1,0:T(8,128)}, u32[]{:S(2)}) copy-start(s32[32,32]{1,0:T(8,128)} %copy-done.20) | copy-start | bytes 12292
  853.8 93.1 %copy-start.26 = (s32[224]{0:T(256)S(1)}, s32[224]{0:T(256)}, u32[]{:S(2)}) copy-start(s32[224]{0:T(256)} %copy-done.25) | copy-start | bytes 2692
  853.8 93.1 %copy-start.28 = (s32[224]{0:T(256)S(1)}, s32[224]{0:T(256)}, u32[]{:S(2)}) copy-start(s32[224]{0:T(256)} %copy-done.27) | copy-start | bytes 2692
  853.8 93.1 %copy-start.30 = (s32[224]{0:T(256)S(1)}, s32[224]{0:T(256)}, u32[]{:S(2)}) copy-start(s32[224]{0:T(256)} %copy-done.29) | copy-start | bytes 2692
  853.8 93.1 %copy-start.32 = (s32[224]{0:T(256)S(1)}, s32[224]{0:T(256)}, u32[]{:S(2)}) copy-start(s32[224]{0:T(256)} %copy-done.31) | copy-start | bytes 2692
  949.9 6.2 copy-start.8
  990.8 4.4 copy-start.19
  (7 other events, 18.0 us)
Sparse Core Ops, SparseCore 0:
  590.5 109.8 reduce-scatter.9
  704.8 129.2 reduce-scatter.7
  838.0 118.0 reduce-scatter.5
  958.3 32.4 all-reduce.2

commit v3 on v2

--- a/solution.py
+++ b/solution.py
@@ -486,7 +486,6 @@
 SLOTS = 32
 PAD_TOKENS = 32
 LANES = 128
-WAVE_FIRST = 3
 TILE = 256
 MESH = pl.DeviceIdType.MESH
 log2e = 1.4426950408889634
@@ -553,78 +552,187 @@
     pl.semaphore_wait(barrier, device_count - 1)
 
 
+class Column:
+    def __init__(self, place, own, slot, send, recv, local):
+        self.place, self.own, self.slot = place, own, slot
+        self.send, self.recv, self.local = send, recv, local
+
+    def hop(self, z, step, own=False):
+        p = self.place
+        source = self.own if own else self.slot(z)
+        number = z if step > 0 else 4 + z
+        target = p.index(p.z + step, p.x, p.c)
+        return remote(source, self.slot(z), self.send.at[number], self.recv(z), target, p.side)
+
+    def own_copy(self):
+        return pltpu.make_async_copy(self.own, self.slot(self.place.z), self.local)
+
+    def upward(self, act):
+        pl.when(self.place.z < 3)(act)
+
+    def downward(self, act):
+        pl.when(self.place.z > 0)(act)
+
+    def start(self):
+        z = self.place.z
+        self.upward(lambda: self.hop(z, 1, True).start())
+        self.downward(lambda: self.hop(z, -1, True).start())
+        self.own_copy().start()
+
+    def forward(self, low=1, high=4, then=None):
+        z = self.place.z
+
+        @pl.loop(low, high)
+        def _(away):
+            @pl.when(z - away >= 0)
+            def _():
+                self.hop(z - away, 1).wait_recv()
+                self.upward(lambda: self.hop(z - away, 1).start())
+                if then is not None:
+                    then(z - away)
+
+            @pl.when(z + away <= 3)
+            def _():
+                self.hop(z + away, -1).wait_recv()
+                self.downward(lambda: self.hop(z + away, -1).start())
+                if then is not None:
+                    then(z + away)
+
+    def finish(self):
+        z = self.place.z
+
+        @pl.loop(0, 4)
+        def _(origin):
+            @pl.when((origin <= z) & (z < 3))
+            def _():
+                self.hop(origin, 1).wait_send()
+
+            @pl.when((origin >= z) & (z > 0))
+            def _():
+                self.hop(origin, -1).wait_send()
+
+
 class Gather:
     def __init__(self, place, own, slot, send, recv, local):
         self.place, self.own, self.slot = place, own, slot
-        self.send, self.recv, self.local = send, recv, local
-
-    def copy(self, z, x, c, to_x, to_c, number, own=False, to_z=None):
+        self.send, self.recv = send, recv
+        self.column = Column(
+            place,
+            own,
+            lambda z: slot(place.index(z, place.x, place.c)),
+            send,
+            lambda z: recv.at[place.index(z, place.x, place.c)],
+            local,
+        )
+
+    def copy(self, z, x, c, to_x, to_c, number, own=False):
         p = self.place
         shard = p.index(z, x, c)
-        target = p.index(p.z if to_z is None else to_z, to_x, to_c)
         source = self.own if own else self.slot(shard)
+        target = p.index(p.z, to_x, to_c)
         return remote(
             source, self.slot(shard), self.send.at[number], self.recv.at[shard], target, p.side
         )
 
-    def first(self):
+    def to_x(self, z, own=False):
         p = self.place
-        out = [
-            self.copy(p.z, p.x, p.c, p.x, p.c, 2 + i, own=True, to_z=z)
-            for i, z in enumerate(p.others())
-        ]
-        out.append(self.copy(p.z, p.x, p.c, 1 - p.x, p.c, 1, own=True))
-        out.append(self.copy(p.z, p.x, p.c, p.x, 1 - p.c, 0, own=True))
-        return out
-
-    def second(self, i):
+        return self.copy(z, p.x, p.c, 1 - p.x, p.c, 8 + z, own)
+
+    def to_core(self, z, x, own=False):
         p = self.place
-        z = p.others()[i]
-        return [
-            self.copy(z, p.x, p.c, 1 - p.x, p.c, 5 + 2 * i),
-            self.copy(z, p.x, p.c, p.x, 1 - p.c, 6 + 2 * i),
-        ]
-
-    def third(self, i):
+        return self.copy(z, x, p.c, p.x, 1 - p.c, 12 + z * 2 + x, own)
+
+    def start(self):
         p = self.place
-        z = ([p.z] + p.others())[i]
-        return self.copy(z, 1 - p.x, p.c, p.x, 1 - p.c, 11 + i)
-
-    def own_copy(self):
+        self.column.start()
+        self.to_x(p.z, True).start()
+        self.to_core(p.z, p.x, True).start()
+
+    def forward_z(self):
+        def then(z):
+            self.to_x(z).start()
+            self.to_core(z, self.place.x).start()
+
+        self.column.forward(then=then)
+
+    def forward_x(self):
         p = self.place
-        return pltpu.make_async_copy(self.own, self.slot(p.dp), self.local)
-
-    def start(self):
-        for copy in self.first():
-            copy.start()
-        self.own_copy().start()
-
-    def forward_z(self):
-        for i in range(3):
-            copies = self.second(i)
-            copies[0].wait_recv()
-            for copy in copies:
-                copy.start()
-
-    def forward_x(self):
-        for i in range(4):
-            copy = self.third(i)
-            copy.wait_recv()
-            copy.start()
+
+        def pass_on(z):
+            self.to_core(z, 1 - p.x).wait_recv()
+            self.to_core(z, 1 - p.x).start()
+
+        pass_on(p.z)
+
+        @pl.loop(1, 4)
+        def _(away):
+            pl.when(p.z - away >= 0)(lambda: pass_on(p.z - away))
+            pl.when(p.z + away <= 3)(lambda: pass_on(p.z + away))
 
     def finish(self):
         p = self.place
-        for z in range(4):
+
+        @pl.loop(0, 4)
+        def _(z):
             for x in range(2):
-                self.copy(z, x, 1 - p.c, p.x, 1 - p.c, 0).wait_recv()
-        for copy in self.first():
-            copy.wait_send()
-        for i in range(3):
-            for copy in self.second(i):
-                copy.wait_send()
-        for i in range(4):
-            self.third(i).wait_send()
-        self.own_copy().wait()
+                self.copy(z, x, 1 - p.c, p.x, 1 - p.c, 12).wait_recv()
+                self.to_core(z, x).wait_send()
+            self.to_x(z).wait_send()
+
+        self.column.finish()
+        self.column.own_copy().wait()
+
+
+class PlaneSwap:
+    def __init__(self, place, source, target, send, recv, local, dp_count):
+        self.place, self.source, self.target = place, source, target
+        self.send, self.recv, self.local = send, recv, local
+        self.dp_count = dp_count
+
+    def of(self, member):
+        return member // 4, (member // 2) % 2, member % 2
+
+    def rank(self, z, side, x, c):
+        return side * self.dp_count + self.place.index(z, x, c)
+
+    def me(self):
+        p = self.place
+        return p.side * 4 + p.x * 2 + p.c
+
+    def block(self, rank):
+        return self.target.at[rows_of(rank, SLOTS)]
+
+    def copy(self, z, step, to, origin):
+        p = self.place
+        side, x, c = self.of(to)
+        return remote(
+            self.source.at[z, rows_of(to, SLOTS)],
+            self.block(self.rank(z, *self.of(origin))),
+            self.send.at[z, step],
+            self.recv.at[z, step],
+            p.index(p.z, x, c),
+            side,
+        )
+
+    def own_copy(self, z):
+        return pltpu.make_async_copy(
+            self.source.at[z, rows_of(self.me(), SLOTS)],
+            self.block(self.rank(z, *self.of(self.me()))),
+            self.local.at[z],
+        )
+
+    def start(self, z):
+        for step in range(1, 8):
+            self.copy(z, step, (self.me() + step) % 8, self.me()).start()
+        self.own_copy(z).start()
+
+    def finish(self):
+        @pl.loop(0, 4)
+        def _(z):
+            for step in range(1, 8):
+                other = (self.me() + 8 - step) % 8
+                self.copy(z, step, other, other).wait()
+            self.own_copy(z).wait()
 
 
 class RowSwap:
@@ -658,6 +766,12 @@
             self.copy(step, (self.rank + step) % self.device_count, self.rank).start()
 
         self.own_copy().start()
+
+    def start_one(self, to):
+        @pl.when(to != self.rank)
+        def _():
+            step = (to + self.device_count - self.rank) % self.device_count
+            self.copy(step, to, self.rank).start()
 
     def finish(self):
         @pl.loop(1, self.device_count)
@@ -736,8 +850,8 @@
     cotangent_ref,
     project_ref,
     out_ref,
-    placed_ref,
-    mask_ref,
+    target_ref,
+    route_ref,
     cosine_ref,
     sine_ref,
     gate_ref,
@@ -758,11 +872,16 @@
     gate_own,
     up_own,
     down_own,
+    hidden_one,
     keys_own,
-    hidden_one,
     row_send,
     grad_send,
-    extended,
+    target_all,
+    gate_own_row,
+    gate_all,
+    hidden_all,
+    grad_all,
+    placed,
     acc,
     top,
     total,
@@ -774,15 +893,19 @@
     keys_recv,
     row_send_sem,
     row_recv_sem,
+    row_local,
     grad_send_sem,
     grad_recv_sem,
+    grad_local,
+    column_send,
+    column_recv,
     weight_send,
     weight_recv,
     weight_local,
     local,
 ):
     dp_count = keys_ref.shape[0]
-    device_count = row_send.shape[0] // SLOTS
+    device_count = rows_in.shape[0] // SLOTS
     tok_count, model_width = tokens_ref.shape
     query_width = HEADS * HEAD
     key_width = KV_HEADS * HEAD
@@ -801,10 +924,23 @@
     keys = Gather(
         place, keys_own, lambda index: keys_ref.at[index], keys_send, keys_recv, local.at[2]
     )
-    rows = RowSwap(row_send, rows_in, row_send_sem, row_recv_sem, local.at[3], dp_count, device_count)
-    grads = RowSwap(
-        grad_send, grads_in, grad_send_sem, grad_recv_sem, local.at[4], dp_count, device_count
-    )
+    rows = PlaneSwap(place, row_send, rows_in, row_send_sem, row_recv_sem, row_local, dp_count)
+    grads = PlaneSwap(place, grad_send, grads_in, grad_send_sem, grad_recv_sem, grad_local, dp_count)
+
+    def column(number, own, land):
+        return Column(
+            place,
+            own,
+            land,
+            column_send.at[number],
+            lambda z: column_recv.at[number, z],
+            local.at[3 + number],
+        )
+
+    targets = column(0, target_ref, lambda z: target_all.at[z])
+    gates = column(1, gate_own_row, lambda z: gate_all.at[z])
+    hidden = column(2, hidden_ref, lambda z: hidden_all.at[z, pl.ds(0, tok_count)])
+    cotangents = column(3, cotangent_ref, lambda z: grad_all.at[z])
     weights = WeightSwap(
         place,
         ((gate_ref, gate_own), (up_ref, up_own), (down_ref, down_own)),
@@ -815,18 +951,33 @@
     )
 
     enter(device_count, dp_count)
+    targets.start()
     project.start()
-    weights.start(1, WAVE_FIRST)
-
-    @pl.loop(0, model_width // TILE)
-    def _(tile):
-        grad_send[:, columns(tile)] = dot_f32(
-            placed_ref[:, :tok_count], cotangent_ref[:, columns(tile)]
-        ).astype(jnp.bfloat16)
+    cotangents.start()
+    plane_slots = 8 * SLOTS
+    targets.forward()
+    targets.own_copy().wait()
+    slot_row = lax.broadcasted_iota(jnp.int32, (plane_slots, TILE), 0)
+    slot_lane = lax.broadcasted_iota(jnp.int32, (plane_slots, TILE), 1)
+    member = slot_row // SLOTS
+    label = ((member // 4) * dp_count + place.z * 4 + member % 4) * SLOTS + slot_row % SLOTS
+    label = label.astype(jnp.float32)
+    spare = (slot_lane - tok_count == member) & (slot_row % SLOTS == CAP)
+
+    def match(z, choice):
+        return label == target_all[z, choice : choice + 1]
+
+    for z in range(4):
+        hit = spare
+        for choice in range(TOP):
+            hit = hit | match(z, choice)
+        placed[z] = jnp.where(hit, 1.0, 0.0).astype(jnp.bfloat16)
+    hidden_all[:, tok_count:] = jnp.zeros((4, PAD_TOKENS, model_width), jnp.bfloat16)
 
     project.forward_z()
     project.forward_x()
     project.finish()
+    cotangents.forward(1, 2)
 
     lanes_of = one_hot((8, LANES), lambda row, column: column == row + EXPERTS)
     gains = dot_f32(lanes_of, project_full[:, query_width + 2 * key_width :], ((1,), (1,)))
@@ -863,11 +1014,9 @@
     keys.forward_x()
     keys.finish()
     out.start()
-    weights.start(WAVE_FIRST, dp_count)
+    cotangents.forward(2, 4)
+    weights.start(1, dp_count)
     weights.start_own()
-    out.forward_z()
-    out.forward_x()
-    grads.start()
 
     row = lax.broadcasted_iota(jnp.int32, (tok_count, tok_count), 0)
     column = lax.broadcasted_iota(jnp.int32, (tok_count, tok_count), 1)
@@ -908,6 +1057,20 @@
     def _(label):
         visit(label, False)
 
+    out.forward_z()
+    out.forward_x()
+    cotangents.own_copy().wait()
+
+    @pl.loop(0, 4)
+    def _(z):
+        @pl.loop(0, model_width // TILE)
+        def _(tile):
+            grad_send[z, :, columns(tile)] = dot_f32(
+                placed[z, :, :tok_count], grad_all[z, :, columns(tile)]
+            ).astype(jnp.bfloat16)
+
+        grads.start(z)
+
     lane = lax.broadcasted_iota(jnp.int32, (tok_count, LANES), 1)
     stats = jnp.zeros((tok_count, LANES), jnp.float32)
     for head in range(HEADS):
@@ -930,42 +1093,59 @@
         scale = lax.rsqrt(jnp.mean(value * value, axis=-1, keepdims=True) + epsilon)
         hidden_ref[rows_of(index, chunk)] = (value * scale * gain_second).astype(jnp.bfloat16)
 
+    hidden.start()
     router = project_full[:, query_width + 2 * key_width :]
-    logits = jnp.where(mask_ref[...] > 0, dot_f32(hidden_ref[...], router), -1e30)
+    chosen = [route_ref[:, choice : choice + 1] == lane for choice in range(TOP)]
+    mask = chosen[0]
+    for choice in range(1, TOP):
+        mask = mask | chosen[choice]
+    logits = jnp.where(mask, dot_f32(hidden_ref[...], router), -1e30)
     weight = jnp.exp(logits - jnp.max(logits, axis=-1, keepdims=True))
     probs = weight / jnp.sum(weight, axis=-1, keepdims=True)
     probs_ref[...] = probs
-    spread = sum(dot_f32(placed_ref[:, :tok_count], part) for part in split3(probs))
-    slot_row = lax.broadcasted_iota(jnp.int32, spread.shape, 0)
-    slot_lane = lax.broadcasted_iota(jnp.int32, spread.shape, 1)
-    gate = jnp.sum(jnp.where(slot_lane == slot_row // SLOTS, spread, 0.0), axis=-1, keepdims=True)
-    high, mid, low = split3(gate)
-    part = jnp.where(
-        slot_lane < SLOTS,
-        high.astype(jnp.float32),
-        jnp.where(slot_lane < 2 * SLOTS, mid.astype(jnp.float32), low.astype(jnp.float32)),
-    )
-    part = jnp.where(
-        (slot_lane % SLOTS == slot_row % SLOTS) & (slot_lane < 3 * SLOTS), part, 0.0
-    ).astype(jnp.bfloat16)
-    fold = one_hot((device_count, row_send.shape[0]), lambda r, col: col // SLOTS == r)
-    extended[:tok_count] = hidden_ref[...]
-    extended[tok_count:] = jnp.zeros((PAD_TOKENS, model_width), jnp.bfloat16)
-    extended[tok_count:, :LANES] = dot_f32(fold, part).astype(jnp.bfloat16)
-
-    @pl.loop(0, model_width // TILE)
-    def _(tile):
-        row_send[:, columns(tile)] = dot_f32(placed_ref[...], extended[:, columns(tile)]).astype(
-            jnp.bfloat16
-        )
-
-    rows.start()
+    by_choice = jnp.zeros((tok_count, LANES), jnp.float32)
+    for choice in range(TOP):
+        gate = jnp.sum(jnp.where(chosen[choice], probs, 0.0), axis=-1, keepdims=True)
+        by_choice = jnp.where(lane == choice, gate, by_choice)
+    first_lanes = one_hot((8, LANES), lambda r, col: r == col)
+    gate_own_row[...] = jnp.zeros(gate_own_row.shape, jnp.float32)
+    gate_own_row[:, :tok_count] = sum(
+        dot_f32(first_lanes, part, ((1,), (1,))) for part in split3(by_choice)
+    )
+    gates.start()
+    fold = one_hot((8, plane_slots), lambda r, col: col // SLOTS == r)
+    def dispatch(z):
+        gate = jnp.zeros((plane_slots, 1), jnp.float32)
+        for choice in range(TOP):
+            gate += jnp.sum(
+                jnp.where(match(z, choice), gate_all[z, choice : choice + 1], 0.0),
+                axis=-1,
+                keepdims=True,
+            )
+        numbers = dot_f32(fold, put_parts(gate)).astype(jnp.bfloat16)
+        numbers = jnp.concatenate([numbers, jnp.zeros((8, LANES), jnp.bfloat16)], axis=0)
+        hidden_all[z, tok_count : tok_count + 16, :LANES] = numbers
+
+        @pl.loop(0, model_width // TILE)
+        def _(tile):
+            row_send[z, :, columns(tile)] = dot_f32(
+                placed[z], hidden_all[z, :, columns(tile)]
+            ).astype(jnp.bfloat16)
+
+        rows.start(z)
+    hidden.own_copy().wait()
+    gates.own_copy().wait()
+    dispatch(place.z)
+    gates.forward()
+    hidden.forward(then=dispatch)
+    for gather in (targets, cotangents, hidden, gates):
+        gather.finish()
     weights.finish()
     grads.finish()
     rows.finish()
 
 
-def front(bias, tokens, cotangent, project, out, placed, mask, cosine, sine, gate, up, down):
+def front(bias, tokens, cotangent, project, out, target, route, cosine, sine, gate, up, down):
     dp_count = lax.axis_size("dp")
     device_count = dp_count * lax.axis_size("expert")
     tok_count, model_width = tokens.shape
@@ -993,6 +1173,7 @@
         (shape((model_width, ff_width), low), anywhere),
         (shape((model_width, ff_width), low), anywhere),
         (shape((ff_width, model_width), low), anywhere),
+        (shape((tok_count, model_width), low), vmem),
     )
     dma = pltpu.SemaphoreType.DMA
     return pl.pallas_call(
@@ -1002,41 +1183,457 @@
         out_specs=tuple(o[1] for o in outs),
         scratch_shapes=[
             pltpu.VMEM((tok_count, 2 * key_width), low),
-            pltpu.VMEM((tok_count, model_width), low),
-            pltpu.VMEM((slots, model_width), low),
-            pltpu.VMEM((slots, model_width), low),
-            pltpu.VMEM((tok_count + PAD_TOKENS, model_width), low),
+            pltpu.VMEM((4, 8 * SLOTS, model_width), low),
+            pltpu.VMEM((4, 8 * SLOTS, model_width), low),
+            pltpu.VMEM((4, 8, TILE), full),
+            pltpu.VMEM((8, TILE), full),
+            pltpu.VMEM((4, 8, TILE), full),
+            pltpu.VMEM((4, tok_count + PAD_TOKENS, model_width), low),
+            pltpu.VMEM((4, tok_count, model_width), low),
+            pltpu.VMEM((4, 8 * SLOTS, TILE), low),
             pltpu.VMEM((HEADS, tok_count, HEAD), full),
             pltpu.VMEM((HEADS, tok_count, 1), full),
             pltpu.VMEM((HEADS, tok_count, 1), full),
         ]
-        + [dma((15,)), dma((dp_count,))] * 3
-        + [dma((device_count,))] * 4
+        + [dma((20,)), dma((dp_count,))] * 3
+        + [dma((4, 8)), dma((4, 8)), dma((4,))] * 2
+        + [dma((4, 8)), dma((4, 4))]
         + [dma((dp_count, 3))] * 2
-        + [dma((3,)), dma((5,))],
+        + [dma((3,)), dma((7,))],
         compiler_params=pltpu.CompilerParams(
             collective_id=0, has_side_effects=True, vmem_limit_bytes=58 * 1024 * 1024
         ),
-    )(bias, tokens, cotangent, project, out, placed, mask, cosine, sine, gate, up, down)
-
-
-def attend_grad_kernel(
-    path_ref, query_ref, keys_ref, grad_ref, exact_ref, stat_ref, grad_query_ref, grad_keys_ref, acc, delta
+    )(bias, tokens, cotangent, project, out, target, route, cosine, sine, gate, up, down)
+
+
+def pick_gates(block):
+    rows = block.shape[0]
+    blocks = rows // SLOTS
+    spare = one_hot((blocks, rows), lambda r, col: col == r * SLOTS + CAP)
+    member = one_hot((rows, blocks), lambda r, col: r // SLOTS == col)
+    parts = dot_f32(member, dot_f32(spare, block).astype(jnp.bfloat16))
+    row = lax.broadcasted_iota(jnp.int32, parts.shape, 0)
+    lane = lax.broadcasted_iota(jnp.int32, parts.shape, 1)
+    mine = (lane % SLOTS == row % SLOTS) & (lane < 3 * SLOTS)
+    return jnp.sum(jnp.where(mine, parts, 0.0), axis=-1, keepdims=True)
+
+
+def put_parts(column):
+    shape = (column.shape[0], LANES)
+    row = lax.broadcasted_iota(jnp.int32, shape, 0)
+    lane = lax.broadcasted_iota(jnp.int32, shape, 1)
+    high, mid, low = (part.astype(jnp.float32) for part in split3(column))
+    part = jnp.where(lane < SLOTS, high, jnp.where(lane < 2 * SLOTS, mid, low))
+    mine = (lane % SLOTS == row % SLOTS) & (lane < 3 * SLOTS)
+    return jnp.where(mine, part, 0.0).astype(jnp.bfloat16)
+
+
+def expert_kernel(
+    rows_ref,
+    grads_ref,
+    gate_ref,
+    up_ref,
+    down_ref,
+    rows_back,
+    outs_back,
+    gate_grad_ref,
+    up_grad_ref,
+    down_grad_ref,
+    out_send,
+    row_send,
+    grad_out,
+    inner_ref,
+    gate_act_grad,
+    up_act_grad,
+    row_send_sem,
+    row_recv_sem,
+    out_send_sem,
+    out_recv_sem,
+    local,
 ):
-    tok_count = query_ref.shape[0]
+    dp_count = lax.axis_size("dp")
+    slots, model_width = rows_ref.shape
+    ff_width = gate_ref.shape[1]
+    device_count = slots // SLOTS
+    enter(device_count, dp_count)
+    rows = RowSwap(row_send, rows_back, row_send_sem, row_recv_sem, local.at[0], dp_count, device_count)
+    outs = RowSwap(out_send, outs_back, out_send_sem, out_recv_sem, local.at[1], dp_count, device_count)
+    tiles = slots // TILE
+    per_tile = TILE // SLOTS
+
+    @pl.loop(0, tiles)
+    def _(step):
+        tile = (step + rows.rank // per_tile) % tiles
+        cut = rows_of(tile, TILE)
+        row = rows_ref[cut]
+        gate = pick_gates(row[:, :LANES])
+        saved = []
+        for n in range(ff_width // TILE):
+            part = slice(n * TILE, (n + 1) * TILE)
+            gate_act = dot_f32(row, gate_ref[:, part])
+            up_act = dot_f32(row, up_ref[:, part])
+            sigmoid = 1.0 / (1.0 + jnp.exp(-gate_act))
+            swish = gate_act * sigmoid
+            inner_ref[cut, part] = (swish * up_act).astype(jnp.bfloat16)
+            saved.append((swish, up_act * (sigmoid * (1.0 + gate_act * (1.0 - sigmoid)))))
+        inner = inner_ref[cut]
+        gate_grad = jnp.zeros((TILE, 1), jnp.float32)
+        for n in range(model_width // TILE):
+            part = slice(n * TILE, (n + 1) * TILE)
+            expert_out = dot_f32(inner, down_ref[:, part]).astype(jnp.bfloat16)
+            out_send[cut, part] = expert_out
+            grad = grads_ref[cut, part].astype(jnp.float32)
+            gate_grad += jnp.sum(expert_out.astype(jnp.float32) * grad, axis=-1, keepdims=True)
+            grad_out[cut, part] = (gate * grad).astype(jnp.bfloat16)
+        grad = grad_out[cut]
+        for n in range(ff_width // TILE):
+            part = slice(n * TILE, (n + 1) * TILE)
+            swish, slope = saved[n]
+            grad_inner = dot_f32(grad, down_ref[part, :], ((1,), (1,)))
+            gate_act_grad[cut, part] = (grad_inner * slope).astype(jnp.bfloat16)
+            up_act_grad[cut, part] = (grad_inner * swish).astype(jnp.bfloat16)
+        fold = one_hot((per_tile, TILE), lambda r, col: col // SLOTS == r)
+        spread = one_hot((TILE, per_tile), lambda r, col: r == col * SLOTS + CAP)
+        extra = dot_f32(spread, dot_f32(fold, put_parts(gate_grad)).astype(jnp.bfloat16))
+        for n in range(model_width // TILE):
+            part = slice(n * TILE, (n + 1) * TILE)
+            back = dot_f32(gate_act_grad[cut], gate_ref[part, :], ((1,), (1,))) + dot_f32(
+                up_act_grad[cut], up_ref[part, :], ((1,), (1,))
+            )
+            row_send[cut, part] = back.astype(jnp.bfloat16)
+            if n == 0:
+                row_send[cut, :LANES] = (back[:, :LANES] + extra).astype(jnp.bfloat16)
+
+        @pl.loop(0, per_tile)
+        def _(index):
+            rows.start_one(tile * per_tile + index)
+
+    rows.own_copy().start()
+    outs.start()
+
+    @pl.loop(0, model_width // TILE)
+    def _(tile):
+        row = rows_ref[:, columns(tile)]
+        gate_grad_ref[rows_of(tile, TILE)] = dot_f32(row, gate_act_grad[...], ((0,), (0,))).astype(
+            jnp.bfloat16
+        )
+        up_grad_ref[rows_of(tile, TILE)] = dot_f32(row, up_act_grad[...], ((0,), (0,))).astype(
+            jnp.bfloat16
+        )
+
+    @pl.loop(0, ff_width // TILE)
+    def _(tile):
+        inner = inner_ref[:, columns(tile)]
+        for n in range(model_width // ff_width):
+            part = slice(n * ff_width, (n + 1) * ff_width)
+            down_grad_ref[rows_of(tile, TILE), part] = dot_f32(
+                inner, grad_out[:, part], ((0,), (0,))
+            ).astype(jnp.bfloat16)
+
+    rows.finish()
+    outs.finish()
+
+
+def experts(rows, grads, gate, up, down):
+    slots, model_width = rows.shape
+    ff_width = gate.shape[1]
+    device_count = slots // SLOTS
+    vmem = pl.BlockSpec(memory_space=pltpu.VMEM)
+    anywhere = pl.BlockSpec(memory_space=pl.ANY)
+    low = jnp.bfloat16
+    shape = jax.ShapeDtypeStruct
+    dma = pltpu.SemaphoreType.DMA
+    return pl.pallas_call(
+        expert_kernel,
+        out_shape=(
+            shape((slots, model_width), low),
+            shape((slots, model_width), low),
+            shape((model_width, ff_width), low),
+            shape((model_width, ff_width), low),
+            shape((ff_width, model_width), low),
+        ),
+        in_specs=[vmem] * 5,
+        out_specs=(anywhere, anywhere, vmem, vmem, vmem),
+        scratch_shapes=[
+            pltpu.VMEM((slots, model_width), low),
+            pltpu.VMEM((slots, model_width), low),
+            pltpu.VMEM((slots, model_width), low),
+            pltpu.VMEM((slots, ff_width), low),
+            pltpu.VMEM((slots, ff_width), low),
+            pltpu.VMEM((slots, ff_width), low),
+        ]
+        + [dma((device_count,))] * 4
+        + [dma((2,))],
+        compiler_params=pltpu.CompilerParams(
+            collective_id=1, has_side_effects=True, vmem_limit_bytes=58 * 1024 * 1024
+        ),
+    )(rows, grads, gate, up, down)
+
+
+def halves_turned(value, cosine, sine):
+    parts = []
+    for half in range(value.shape[1] // HEAD):
+        part = value[:, half * HEAD : (half + 1) * HEAD]
+        parts.append(part * cosine + pltpu.roll(part, HEAD // 2, 1) * sine)
+    return jnp.concatenate(parts, axis=1)
+
+
+def gain_rows(small):
+    lanes_of = one_hot((8, LANES), lambda row, column: column == row + EXPERTS)
+    return dot_f32(lanes_of, small, ((1,), (1,)))
+
+
+class Scatter:
+    def __init__(self, place, block, lands, send, recvs):
+        self.place, self.block = place, block
+        self.lands, self.send, self.recvs = lands, send, recvs
+
+    def hop_core(self, z, x):
+        p = self.place
+        number = z * 2 + x
+        return remote(
+            self.block(p.index(z, x, 1 - p.c)),
+            self.lands[0].at[number],
+            self.send.at[number],
+            self.recvs[0].at[number],
+            p.index(p.z, p.x, 1 - p.c),
+            p.side,
+        )
+
+    def hop_x(self, z):
+        p = self.place
+        return remote(
+            self.block(p.index(z, 1 - p.x, p.c)),
+            self.lands[1].at[z],
+            self.send.at[8 + z],
+            self.recvs[1].at[z],
+            p.index(p.z, 1 - p.x, p.c),
+            p.side,
+        )
+
+    def hop_z(self, i):
+        p = self.place
+        z = p.others()[i]
+        return remote(
+            self.block(p.index(z, p.x, p.c)),
+            self.lands[2].at[i],
+            self.send.at[12 + i],
+            self.recvs[2].at[i],
+            p.index(z, p.x, p.c),
+            p.side,
+        )
+
+    def add(self, shard, land):
+        block = self.block(shard)
+        chunk = 32
+
+        @pl.loop(0, block.shape[0] // chunk)
+        def _(index):
+            cut = rows_of(index, chunk)
+            block[cut] = (block[cut].astype(jnp.float32) + land[cut].astype(jnp.float32)).astype(
+                jnp.bfloat16
+            )
+
+    def start(self):
+        for z in range(4):
+            for x in range(2):
+                self.hop_core(z, x).start()
+
+    def order(self):
+        return self.place.others() + [self.place.z]
+
+    def pass_core(self):
+        p = self.place
+        for z in self.order():
+            for x in (1 - p.x, p.x):
+                self.hop_core(z, x).wait_recv()
+                self.add(p.index(z, x, p.c), self.lands[0].at[z * 2 + x])
+            self.hop_x(z).start()
+
+    def pass_x(self):
+        p = self.place
+        for i, z in enumerate(self.order()):
+            self.hop_x(z).wait_recv()
+            self.add(p.index(z, p.x, p.c), self.lands[1].at[z])
+            if i < 3:
+                self.hop_z(i).start()
+
+    def pass_z(self, put):
+        p = self.place
+        for i in range(3):
+            self.hop_z(i).wait_recv()
+        block = self.block(p.dp)
+        chunk = 32
+
+        @pl.loop(0, block.shape[0] // chunk)
+        def _(index):
+            cut = rows_of(index, chunk)
+            value = block[cut].astype(jnp.float32)
+            for i in range(3):
+                value += self.lands[2][i, cut].astype(jnp.float32)
+            put(cut, value)
+
+    def finish(self):
+        for z in range(4):
+            for x in range(2):
+                self.hop_core(z, x).wait_send()
+            self.hop_x(z).wait_send()
+        for i in range(3):
+            self.hop_z(i).wait_send()
+
+
+class WeightReturn(WeightSwap):
+    def copies(self, step, to, landing):
+        out = []
+        for i, (source, target) in enumerate(self.pairs):
+            rows = target.shape[1]
+            out.append(
+                remote(
+                    source.at[rows_of(to, rows)],
+                    target.at[landing],
+                    self.send.at[step, i],
+                    self.recv.at[step, i],
+                    to,
+                    self.place.side,
+                )
+            )
+        return out
+
+    def own_copies(self):
+        dp = self.place.dp
+        return [
+            pltpu.make_async_copy(
+                source.at[rows_of(dp, target.shape[1])], target.at[dp], self.local.at[i]
+            )
+            for i, (source, target) in enumerate(self.pairs)
+        ]
+
+
+def back_kernel(
+    bias_ref,
+    cotangent_ref,
+    middle_ref,
+    probs_ref,
+    exact_ref,
+    stat_ref,
+    query_ref,
+    keys_ref,
+    small_ref,
+    out_ref,
+    placed_ref,
+    rows_ref,
+    outs_ref,
+    cosine_ref,
+    sine_ref,
+    gate_ref,
+    up_ref,
+    result_ref,
+    grad_middle_ref,
+    grad_branch_ref,
+    grad_logits_ref,
+    grad_project_ref,
+    gain_ref,
+    gate_back,
+    up_back,
+    grad_hidden,
+    grad_ref,
+    acc,
+    delta,
+    grad_keys_ref,
+    land_core,
+    land_x,
+    land_z,
+    scatter_send,
+    recv_core,
+    recv_x,
+    recv_z,
+    weight_send,
+    weight_recv,
+    weight_local,
+):
+    dp_count = keys_ref.shape[0]
+    slots = rows_ref.shape[0]
+    device_count = slots // SLOTS
+    tok_count, model_width = middle_ref.shape
+    query_width = HEADS * HEAD
+    key_width = KV_HEADS * HEAD
     repeat_heads = HEADS // KV_HEADS
     scale = HEAD ** (-0.5)
     factor = log2e * scale
-    segment_count = keys_ref.shape[0]
-    segment = path_ref[segment_count]
-    row = lax.broadcasted_iota(jnp.int32, (tok_count, tok_count), 0)
-    column = lax.broadcasted_iota(jnp.int32, (tok_count, tok_count), 1)
-    causal = column <= row
+    chunk = 32
+    place = Place()
+    enter(device_count, dp_count)
+    weights = WeightReturn(
+        place,
+        ((gate_ref, gate_back), (up_ref, up_back)),
+        weight_send,
+        weight_recv,
+        weight_local,
+        dp_count,
+    )
+    weights.start(1, dp_count)
+    weights.start_own()
+    scatter = Scatter(
+        place,
+        lambda index: grad_keys_ref.at[index],
+        (land_core, land_x, land_z),
+        scatter_send,
+        (recv_core, recv_x, recv_z),
+    )
+
+    probs = probs_ref[...]
+    gate_grads = pick_gates(rows_ref[:, :LANES])
+    slot_row = lax.broadcasted_iota(jnp.int32, (slots, LANES), 0)
+    slot_lane = lax.broadcasted_iota(jnp.int32, (slots, LANES), 1)
+    by_expert = jnp.where(slot_lane == slot_row // SLOTS, gate_grads, 0.0)
+    grad_probs = sum(dot_f32(placed_ref[...], part) for part in split3(by_expert))
+    grad_logits = (
+        probs * (grad_probs - jnp.sum(probs * grad_probs, axis=-1, keepdims=True))
+    ).astype(jnp.bfloat16)
+    grad_logits_ref[...] = grad_logits
+
+    @pl.loop(0, model_width // TILE)
+    def _(tile):
+        grad_hidden[:, columns(tile)] = dot_f32(
+            placed_ref[...], rows_ref[:, columns(tile)]
+        ) + dot_f32(grad_logits_ref[...], small_ref[rows_of(tile, TILE)], ((1,), (1,)))
+
+    gain = gain_rows(small_ref[...])[1:2]
+    gain_ref[...] = jnp.zeros(gain_ref.shape, jnp.float32)
+
+    @pl.loop(0, tok_count // chunk)
+    def _(index):
+        cut = rows_of(index, chunk)
+        value = middle_ref[cut]
+        row_scale = lax.rsqrt(jnp.mean(value * value, axis=-1, keepdims=True) + epsilon)
+        normed = value * row_scale
+        grad = grad_hidden[cut]
+        gain_ref[0:1] += jnp.sum(grad * normed, axis=0, keepdims=True)
+        grad = grad * gain
+        total = cotangent_ref[cut].astype(jnp.float32) + row_scale * (
+            grad - normed * jnp.mean(grad * normed, axis=-1, keepdims=True)
+        )
+        grad_middle_ref[cut] = total
+        grad_branch_ref[cut] = total.astype(jnp.bfloat16)
+
+    @pl.loop(0, model_width // TILE)
+    def _(tile):
+        grad_ref[:, columns(tile)] = dot_f32(
+            grad_branch_ref[...], out_ref[rows_of(tile, TILE)], ((1,), (1,))
+        ).astype(jnp.bfloat16)
+
     for head in range(HEADS):
         cut = slice(head * HEAD, (head + 1) * HEAD)
         delta[head] = jnp.sum(
             grad_ref[:, cut].astype(jnp.float32) * exact_ref[:, cut], axis=-1, keepdims=True
         )
+    row = lax.broadcasted_iota(jnp.int32, (tok_count, tok_count), 0)
+    column = lax.broadcasted_iota(jnp.int32, (tok_count, tok_count), 1)
+    causal = column <= row
+
+    @pl.loop(place.dp + 1, dp_count)
+    def _(label):
+        grad_keys_ref[label] = jnp.zeros(grad_keys_ref.shape[1:], jnp.bfloat16)
 
     def visit(label, own):
         for group in range(KV_HEADS):
@@ -1050,15 +1647,18 @@
                 cut = slice(head * HEAD, (head + 1) * HEAD)
                 query = query_ref[:, cut]
                 grad = grad_ref[:, cut]
+                shift = stat_ref[:, head : head + 1]
+                if not own:
+                    shift = shift - bias_ref[label]
                 scores = dot_f32(query, key, ((1,), (1,)))
-                prob = jnp.exp2(scores * factor - stat_ref[:, head : head + 1])
+                prob = jnp.exp2(scores * factor - shift)
                 if own:
                     prob = jnp.where(causal, prob, 0.0)
                 grad_prob = dot_f32(grad, value, ((1,), (1,)))
                 grad_score = (prob * (grad_prob - delta[head])).astype(jnp.bfloat16)
                 grad_value += dot_f32(prob.astype(jnp.bfloat16), grad, ((0,), (0,)))
                 grad_key += dot_f32(grad_score, query, ((0,), (0,)))
-                grad_query = dot_f32(grad_score, key, ((1,), (0,)))
+                grad_query = dot_f32(grad_score, key)
                 if own:
                     acc[head] = grad_query
                 else:
@@ -1066,39 +1666,274 @@
             grad_keys_ref[label, :, key_cut] = (grad_key * scale).astype(jnp.bfloat16)
             grad_keys_ref[label, :, value_cut] = grad_value.astype(jnp.bfloat16)
 
-    visit(segment, True)
-
-    @pl.loop(0, segment_count)
+    visit(place.dp, True)
+
+    @pl.loop(0, place.dp)
     def _(label):
-        @pl.when((path_ref[label] > 0) & (label != segment))
-        def _():
-            visit(label, False)
-
-        @pl.when(path_ref[label] == 0)
-        def _():
-            grad_keys_ref[label] = jnp.zeros(grad_keys_ref.shape[1:], jnp.bfloat16)
-
+        visit(label, False)
+
+    scatter.start()
+    cosine, sine = cosine_ref[...], -sine_ref[...]
     for head in range(HEADS):
-        grad_query_ref[:, head * HEAD : (head + 1) * HEAD] = acc[head] * scale
-
-
-def attend_grad(path, query, keys, grad, exact, stats):
-    tok_count = query.shape[0]
+        grad_project_ref[:, head * HEAD : (head + 1) * HEAD] = halves_turned(
+            acc[head] * scale, cosine, sine
+        ).astype(jnp.bfloat16)
+    scatter.pass_core()
+    scatter.pass_x()
+
+    expand = one_hot((LANES, slots), lambda r, col: col // SLOTS == r)
+    high, mid, low = split3(probs_ref[...])
+    gates = (dot_f32(high, expand) + dot_f32(mid, expand)) * placed_ref[...].astype(jnp.float32)
+    gate_high = gates.astype(jnp.bfloat16)
+    gate_low = (gates - gate_high.astype(jnp.float32)).astype(jnp.bfloat16)
+
+    @pl.loop(0, model_width // TILE)
+    def _(tile):
+        outs = outs_ref[:, columns(tile)]
+        result_ref[:, columns(tile)] = (
+            middle_ref[:, columns(tile)] + dot_f32(gate_high, outs) + dot_f32(gate_low, outs)
+        ).astype(jnp.bfloat16)
+
+    def put(cut, value):
+        grad_project_ref[cut, query_width : query_width + key_width] = halves_turned(
+            value[:, :key_width], cosine_ref[cut], -sine_ref[cut]
+        ).astype(jnp.bfloat16)
+        grad_project_ref[cut, query_width + key_width :] = value[:, key_width:].astype(jnp.bfloat16)
+
+    scatter.pass_z(put)
+    scatter.finish()
+    weights.finish()
+
+
+def back(
+    bias, cotangent, middle, probs, exact, stats, query, keys, small, out, placed, rows, outs,
+    cosine, sine, gate_grad, up_grad, shard,
+):
+    dp_count, tok_count, both = keys.shape
+    model_width = middle.shape[1]
+    slots = rows.shape[0]
+    ff_width = gate_grad.shape[1]
     vmem = pl.BlockSpec(memory_space=pltpu.VMEM)
+    anywhere = pl.BlockSpec(memory_space=pl.ANY)
+    low, full = jnp.bfloat16, jnp.float32
+    shape = jax.ShapeDtypeStruct
+    dma = pltpu.SemaphoreType.DMA
     return pl.pallas_call(
-        attend_grad_kernel,
+        back_kernel,
         out_shape=(
-            jax.ShapeDtypeStruct(query.shape, jnp.float32),
-            jax.ShapeDtypeStruct(keys.shape, jnp.bfloat16),
+            shape((tok_count, model_width), low),
+            shape((tok_count, model_width), full),
+            shape((tok_count, model_width), low),
+            shape((tok_count, LANES), low),
+            shape((tok_count, query.shape[1] + both), low),
+            shape((8, model_width), full),
+            shape((dp_count, shard, ff_width), low),
+            shape((dp_count, shard, ff_width), low),
         ),
-        in_specs=[pl.BlockSpec(memory_space=pltpu.SMEM)] + [vmem] * 5,
-        out_specs=(vmem, vmem),
+        in_specs=[pl.BlockSpec(memory_space=pltpu.SMEM)] + [vmem] * 14 + [anywhere] * 2,
+        out_specs=(vmem,) * 6 + (anywhere,) * 2,
         scratch_shapes=[
-            pltpu.VMEM((HEADS, tok_count, HEAD), jnp.float32),
-            pltpu.VMEM((HEADS, tok_count, 1), jnp.float32),
+            pltpu.VMEM((tok_count, model_width), full),
+            pltpu.VMEM((tok_count, model_width), low),
+            pltpu.VMEM((HEADS, tok_count, HEAD), full),
+            pltpu.VMEM((HEADS, tok_count, 1), full),
+            pltpu.VMEM((dp_count, tok_count, both), low),
+            pltpu.VMEM((8, tok_count, both), low),
+            pltpu.VMEM((4, tok_count, both), low),
+            pltpu.VMEM((3, tok_count, both), low),
+            dma((15,)),
+            dma((8,)),
+            dma((4,)),
+            dma((3,)),
+            dma((dp_count, 2)),
+            dma((dp_count, 2)),
+            dma((2,)),
         ],
-        compiler_params=pltpu.CompilerParams(vmem_limit_bytes=40 * 1024 * 1024),
-    )(path, query, keys, grad, exact, stats)
+        compiler_params=pltpu.CompilerParams(
+            collective_id=2, has_side_effects=True, vmem_limit_bytes=60 * 1024 * 1024
+        ),
+    )(
+        bias, cotangent, middle, probs, exact, stats, query, keys, small, out, placed, rows, outs,
+        cosine, sine, gate_grad, up_grad,
+    )
+
+
+def finish_kernel(
+    tokens_ref,
+    hidden_one,
+    hidden_two,
+    attended_ref,
+    grad_middle_ref,
+    grad_branch_ref,
+    grad_logits_ref,
+    grad_project_ref,
+    gain_ref,
+    project_ref,
+    down_ref,
+    grad_tokens_ref,
+    mine_ref,
+    down_back,
+    grad_hidden,
+    gain_one,
+    partial_ref,
+    pair_send,
+    pair_land,
+    land_core,
+    land_x,
+    land_z,
+    scatter_send,
+    recv_core,
+    recv_x,
+    recv_z,
+    pair_sem,
+    weight_send,
+    weight_recv,
+    weight_local,
+):
+    tok_count, model_width = tokens_ref.shape
+    width = grad_project_ref.shape[1]
+    dp_count = lax.axis_size("dp")
+    device_count = dp_count * lax.axis_size("expert")
+    shard = mine_ref.shape[0]
+    place = Place()
+    chunk = 32
+    enter(device_count, dp_count)
+    weights = WeightReturn(
+        place, ((down_ref, down_back),), weight_send, weight_recv, weight_local, dp_count
+    )
+    weights.start(1, dp_count)
+    weights.start_own()
+    scatter = Scatter(
+        place,
+        lambda index: partial_ref.at[index],
+        (land_core, land_x, land_z),
+        scatter_send,
+        (recv_core, recv_x, recv_z),
+    )
+
+    @pl.loop(0, model_width // TILE)
+    def _(tile):
+        grad_hidden[:, columns(tile)] = dot_f32(
+            grad_project_ref[...], project_ref[rows_of(tile, TILE), :width], ((1,), (1,))
+        )
+
+    gain = gain_rows(project_ref[:, width:])[0:1]
+    gain_one[...] = jnp.zeros(gain_one.shape, jnp.float32)
+
+    @pl.loop(0, tok_count // chunk)
+    def _(index):
+        cut = rows_of(index, chunk)
+        value = tokens_ref[cut].astype(jnp.float32)
+        row_scale = lax.rsqrt(jnp.mean(value * value, axis=-1, keepdims=True) + epsilon)
+        normed = value * row_scale
+        grad = grad_hidden[cut]
+        gain_one[0:1] += jnp.sum(grad * normed, axis=0, keepdims=True)
+        grad = grad * gain
+        grad_tokens_ref[cut] = grad_middle_ref[cut] + row_scale * (
+            grad - normed * jnp.mean(grad * normed, axis=-1, keepdims=True)
+        )
+
+    one_lane = one_hot((8, LANES), lambda r, col: (r == 0) & (col == EXPERTS))
+    two_lane = one_hot((8, LANES), lambda r, col: (r == 0) & (col == EXPERTS + 1))
+    group = 4 * shard
+
+    @pl.loop(0, model_width // group)
+    def _(index):
+        cut = columns(index, group)
+
+        def put(at, value):
+            for i in range(4):
+                partial_ref[index * 4 + i, :, at] = value[i * shard : (i + 1) * shard].astype(
+                    jnp.bfloat16
+                )
+
+        step = 512
+        left = hidden_one[:, cut]
+        for n in range(width // step):
+            at = slice(n * step, (n + 1) * step)
+            put(at, dot_f32(left, grad_project_ref[:, at], ((0,), (0,))))
+        small = dot_f32(hidden_two[:, cut], grad_logits_ref[...], ((0,), (0,)))
+        for part in split3(gain_one[:, cut]):
+            small += dot_f32(part, one_lane, ((0,), (0,)))
+        for part in split3(gain_ref[:, cut]):
+            small += dot_f32(part, two_lane, ((0,), (0,)))
+        put(slice(width, width + LANES), small)
+        left = attended_ref[:, cut]
+        for n in range(model_width // step):
+            at = slice(n * step, (n + 1) * step)
+            put(
+                slice(width + LANES + n * step, width + LANES + (n + 1) * step),
+                dot_f32(left, grad_branch_ref[:, at], ((0,), (0,))),
+            )
+
+    scatter.start()
+    scatter.pass_core()
+    scatter.pass_x()
+
+    def keep(cut, value):
+        pair_send[cut] = value.astype(jnp.bfloat16)
+
+    scatter.pass_z(keep)
+    pair = remote(
+        pair_send, pair_land, pair_sem.at[0], pair_sem.at[1], place.dp, 1 - place.side
+    )
+    pair.start()
+    scatter.finish()
+    pair.wait()
+    weights.finish()
+
+    @pl.loop(0, shard // chunk)
+    def _(index):
+        cut = rows_of(index, chunk)
+        mine_ref[cut] = pair_send[cut].astype(jnp.float32) + pair_land[cut].astype(jnp.float32)
+
+
+def finish(
+    tokens, hidden_one, hidden_two, attended, grad_middle, grad_branch, grad_logits, grad_project,
+    gain, project, down_grad, shard, half,
+):
+    tok_count, model_width = tokens.shape
+    dp_count = lax.axis_size("dp")
+    width = project.shape[1] + model_width
+    vmem = pl.BlockSpec(memory_space=pltpu.VMEM)
+    anywhere = pl.BlockSpec(memory_space=pl.ANY)
+    low, full = jnp.bfloat16, jnp.float32
+    shape = jax.ShapeDtypeStruct
+    dma = pltpu.SemaphoreType.DMA
+    return pl.pallas_call(
+        finish_kernel,
+        out_shape=(
+            shape((tok_count, model_width), full),
+            shape((shard, width), full),
+            shape((dp_count, half, model_width), low),
+        ),
+        in_specs=[vmem] * 10 + [anywhere],
+        out_specs=(vmem, vmem, anywhere),
+        scratch_shapes=[
+            pltpu.VMEM((tok_count, model_width), full),
+            pltpu.VMEM((8, model_width), full),
+            pltpu.VMEM((dp_count, shard, width), low),
+            pltpu.VMEM((shard, width), low),
+            pltpu.VMEM((shard, width), low),
+            pltpu.VMEM((8, shard, width), low),
+            pltpu.VMEM((4, shard, width), low),
+            pltpu.VMEM((3, shard, width), low),
+            dma((15,)),
+            dma((8,)),
+            dma((4,)),
+            dma((3,)),
+            dma((2,)),
+            dma((dp_count, 1)),
+            dma((dp_count, 1)),
+            dma((1,)),
+        ],
+        compiler_params=pltpu.CompilerParams(
+            collective_id=3, has_side_effects=True, vmem_limit_bytes=58 * 1024 * 1024
+        ),
+    )(
+        tokens, hidden_one, hidden_two, attended, grad_middle, grad_branch, grad_logits,
+        grad_project, gain, project, down_grad,
+    )
 
 
 def local_owned(
@@ -1119,12 +1954,7 @@
     cotangent,
 ):
     tok_count = tokens.shape[1]
-    model_width = tokens.shape[2]
-    ff_width = gate_weight.shape[2]
     segment = lax.axis_index("dp")
-    segment_count = lax.axis_size("dp")
-    everyone = ("expert", "dp")
-    device_count = segment_count * lax.axis_size("expert")
     query_width = HEADS * HEAD
     key_width = KV_HEADS * HEAD
 
@@ -1144,14 +1974,9 @@
     placed_rows = sum(
         (target[:, c : c + 1] == row_labels[None, :]).astype(jnp.bfloat16) for c in range(TOP)
     )
-    turned_target = target.T
-    placed_by_slot = sum(
-        (turned_target[c : c + 1] == row_labels[:, None]).astype(jnp.bfloat16) for c in range(TOP)
-    )
-    spare = row_labels[:, None] == (jnp.arange(EXPERTS) * SLOTS + CAP)[None, :]
-    placed_by_slot = jnp.concatenate([placed_by_slot, spare.astype(jnp.bfloat16)], axis=1)
-    experts_row = jnp.arange(LANES, dtype=jnp.int32)[None, :]
-    mask = sum((route_rows[:, c : c + 1] == experts_row).astype(jnp.float32) for c in range(TOP))
+    target_rows = jnp.full((8, TILE), -1.0, jnp.float32)
+    target_rows = target_rows.at[:TOP, :tok_count].set(target.T.astype(jnp.float32))
+    route_lanes = jnp.pad(route_rows, ((0, 0), (0, LANES - TOP)), constant_values=-1)
 
     small = jnp.concatenate(
         [
@@ -1171,7 +1996,6 @@
     sine_wide = jnp.concatenate([-sine_part[:, 0], sine_part[:, 0]], axis=1)
     on_path = reach_row > 0.5
     bias = jnp.where(on_path, 0.0, -1e30).astype(jnp.float32)
-    path = jnp.concatenate([on_path.astype(jnp.int32), segment[None].astype(jnp.int32)])
     (
         project_full,
         out_full,
@@ -1188,14 +2012,15 @@
         gate_own,
         up_own,
         down_own,
+        hidden_one,
     ) = front(
         bias,
         tokens[0],
         cotangent[0],
         project_shard,
         out_weight,
-        placed_by_slot,
-        mask,
+        target_rows,
+        route_lanes,
         cosine_wide,
         sine_wide,
         gate_weight,
@@ -1203,159 +2028,66 @@
         down_weight,
     )
     small_at = query_width + 2 * key_width
-    project = project_full[:, :small_at]
-    small_full = project_full[:, small_at:]
-    router_full = small_full[:, :EXPERTS]
-    gain_first = small_full[:, EXPERTS].astype(jnp.float32)
-    gain_second = small_full[:, EXPERTS + 1].astype(jnp.float32)
-    inputs = tokens[0].astype(jnp.float32)
-    scale_one = lax.rsqrt(jnp.mean(inputs * inputs, axis=-1, keepdims=True) + epsilon)
-    normed_one = inputs * scale_one
-    hidden_one = (normed_one * gain_first).astype(jnp.bfloat16)
-    scale_two = lax.rsqrt(jnp.mean(middle * middle, axis=-1, keepdims=True) + epsilon)
-    normed_two = middle * scale_two
-    gate_probs = probs[:, :EXPERTS]
-    gate_parts = rows_in.reshape(device_count, SLOTS, model_width)[:, CAP, : 3 * SLOTS]
-    gates_in = jnp.sum(
-        gate_parts.reshape(device_count, 3, SLOTS).astype(jnp.float32), axis=1
-    ).reshape(-1)
-    spare_row = (jnp.arange(EXPERTS * SLOTS) % SLOTS >= CAP)[:, None]
-    rows_in = jnp.where(spare_row, jnp.zeros_like(rows_in), rows_in)
-
-    def exchange(rows):
-        return lax.all_to_all(
-            rows.reshape(device_count, SLOTS, rows.shape[-1]),
-            everyone,
-            split_axis=0,
-            concat_axis=0,
-            tiled=True,
-        ).reshape(EXPERTS * SLOTS, rows.shape[-1])
-
-    gate_act = jnp.dot(rows_in, gate_own, preferred_element_type=jnp.float32)
-    up_act = jnp.dot(rows_in, up_own, preferred_element_type=jnp.float32)
-    sigmoid_gate = jax.nn.sigmoid(gate_act)
-    swish = gate_act * sigmoid_gate
-    inner = (swish * up_act).astype(jnp.bfloat16)
-    expert_out = jnp.dot(inner, down_own, preferred_element_type=jnp.float32).astype(jnp.bfloat16)
-    grad_in = grad_rows_in.astype(jnp.float32)
-    grad_gate_rows = jnp.sum(expert_out.astype(jnp.float32) * grad_in, axis=-1)
-    grad_expert_out = (gates_in[:, None] * grad_in).astype(jnp.bfloat16)
-    grad_inner = dot_f32(grad_expert_out, down_own, ((1,), (1,)))
-    grad_gate_act = (
-        grad_inner * up_act * (sigmoid_gate * (1.0 + gate_act * (1.0 - sigmoid_gate)))
-    ).astype(jnp.bfloat16)
-    grad_up_act = (grad_inner * swish).astype(jnp.bfloat16)
-    grad_rows = (
-        dot_f32(grad_gate_act, gate_own, ((1,), (1,)))
-        + dot_f32(grad_up_act, up_own, ((1,), (1,)))
-    ).astype(jnp.bfloat16)
-    grad_rows_back = exchange(grad_rows)
-    grad_gates_back = lax.all_to_all(
-        grad_gate_rows.reshape(device_count, SLOTS),
-        everyone,
-        split_axis=0,
-        concat_axis=0,
-        tiled=True,
-    ).reshape(-1)
-    rows_back = exchange(expert_out)
-
-    def give(grad):
-        parts = grad.astype(jnp.bfloat16).reshape(segment_count, -1, grad.shape[-1])
-        return lax.all_to_all(parts, "dp", split_axis=0, concat_axis=0, tiled=True).astype(
-            jnp.float32
-        )
-
-    grad_down_mine = give(dot_f32(inner, grad_expert_out, ((0,), (0,))))
-    grad_gate_mine = give(dot_f32(rows_in, grad_gate_act, ((0,), (0,))))
-    grad_up_mine = give(dot_f32(rows_in, grad_up_act, ((0,), (0,))))
-
-    gate_placed = jnp.repeat(gate_probs, SLOTS, axis=1) * placed_rows.astype(jnp.float32)
-    gate_high = gate_placed.astype(jnp.bfloat16)
-    gate_low = (gate_placed - gate_high.astype(jnp.float32)).astype(jnp.bfloat16)
-    mixture = jnp.dot(gate_high, rows_back, preferred_element_type=jnp.float32) + jnp.dot(
-        gate_low, rows_back, preferred_element_type=jnp.float32
-    )
-    block_out = (middle + mixture).astype(jnp.bfloat16)
-    grad_result = cotangent[0].astype(jnp.float32)
-    grad_gates = jnp.sum(
-        (placed_rows.astype(jnp.float32) * grad_gates_back[None, :]).reshape(
-            tok_count, EXPERTS, SLOTS
-        ),
-        axis=-1,
-    )
-    grad_hidden_two = jnp.dot(placed_rows, grad_rows_back, preferred_element_type=jnp.float32)
-    grad_chosen = gate_probs * (
-        grad_gates - jnp.sum(gate_probs * grad_gates, axis=-1, keepdims=True)
-    )
-    grad_logits = grad_chosen.astype(jnp.bfloat16)
-    grad_hidden_two = grad_hidden_two + dot_f32(grad_logits, router_full, ((1,), (1,)))
-    grad_router_local = dot_f32(hidden_two, grad_logits, ((0,), (0,)))
-    grad_middle_norm, grad_gain_two = norm_backward(
-        grad_hidden_two, normed_two, scale_two, gain_second
-    )
-    grad_middle = grad_result + grad_middle_norm
-    grad_branch = grad_middle.astype(jnp.bfloat16)
-    grad_out_local = dot_f32(attended, grad_branch, ((0,), (0,)))
-    grad_attended = dot_f32(grad_branch, out_full, ((1,), (1,))).astype(jnp.bfloat16)
-    grad_query_rot, grad_keys = attend_grad(
-        path, query_rot, keys, grad_attended, exact_out, stats
-    )
-    grad_keys_mine = lax.psum_scatter(
-        grad_keys.reshape(segment_count * tok_count, 2 * key_width),
-        "dp",
-        scatter_dimension=0,
-        tiled=True,
-    ).astype(jnp.float32)
-    grad_query_raw = (
-        rotate(grad_query_rot.reshape(tok_count, HEADS, HEAD), cosine, -sine_part)
-        .reshape(tok_count, query_width)
-        .astype(jnp.bfloat16)
-    )
-    grad_key_raw = (
-        rotate(grad_keys_mine[:, :key_width].reshape(tok_count, KV_HEADS, HEAD), cosine, -sine_part)
-        .reshape(tok_count, key_width)
-        .astype(jnp.bfloat16)
-    )
-    grad_projected = jnp.concatenate(
-        [grad_query_raw, grad_key_raw, grad_keys_mine[:, key_width:].astype(jnp.bfloat16)], axis=1
-    )
-    grad_project_local = dot_f32(hidden_one, grad_projected, ((0,), (0,)))
-    grad_hidden_one = dot_f32(grad_projected, project, ((1,), (1,)))
-    grad_inputs_norm, grad_gain_one = norm_backward(
-        grad_hidden_one, normed_one, scale_one, gain_first
-    )
-    grad_inputs = grad_middle + grad_inputs_norm
-
-    def scatter(grad):
-        part = lax.psum_scatter(
-            grad.astype(jnp.bfloat16), "dp", scatter_dimension=0, tiled=True
-        )
-        return lax.psum(part, "expert").astype(jnp.float32)
-
-    grad_small = jnp.concatenate(
-        [
-            grad_router_local,
-            grad_gain_one[:, None],
-            grad_gain_two[:, None],
-            jnp.zeros((model_width, HEAD - EXPERTS - 2), jnp.float32),
-        ],
-        axis=1,
-    )
-    grad_out_mine = scatter(grad_out_local)
-    grad_project_mine = scatter(jnp.concatenate([grad_project_local, grad_small], axis=1))
+    rows_back, outs_back, gate_grad, up_grad, down_grad = experts(
+        rows_in, grad_rows_in, gate_own, up_own, down_own
+    )
+    (
+        block_out,
+        grad_middle,
+        grad_branch,
+        grad_logits,
+        grad_project,
+        gain_row,
+        gate_back,
+        up_back,
+    ) = back(
+        bias,
+        cotangent[0],
+        middle,
+        probs,
+        exact_out,
+        stats,
+        query_rot,
+        keys,
+        project_full[:, small_at:],
+        out_full,
+        placed_rows,
+        rows_back,
+        outs_back,
+        cosine_wide,
+        sine_wide,
+        gate_grad,
+        up_grad,
+        gate_weight.shape[1],
+    )
+    grad_tokens, mine, down_back = finish(
+        tokens[0],
+        hidden_one,
+        hidden_two,
+        attended,
+        grad_middle,
+        grad_branch,
+        grad_logits,
+        grad_project,
+        gain_row,
+        project_full,
+        down_grad,
+        query_weight.shape[0],
+        down_weight.shape[1],
+    )
     return (
         block_out[None],
-        grad_inputs[None],
-        grad_project_mine[:, small_at + EXPERTS],
-        grad_project_mine[:, :query_width],
-        grad_project_mine[:, query_width : query_width + key_width],
-        grad_project_mine[:, query_width + key_width : small_at],
-        grad_out_mine,
-        grad_project_mine[:, small_at + EXPERTS + 1],
-        grad_project_mine[:, small_at : small_at + EXPERTS],
-        grad_gate_mine,
-        grad_up_mine,
-        grad_down_mine,
+        grad_tokens[None],
+        mine[:, small_at + EXPERTS],
+        mine[:, :query_width],
+        mine[:, query_width : query_width + key_width],
+        mine[:, query_width + key_width : small_at],
+        mine[:, small_at + LANES :],
+        mine[:, small_at + EXPERTS + 1],
+        mine[:, small_at : small_at + EXPERTS],
+        gate_back.astype(jnp.float32),
+        up_back.astype(jnp.float32),
+        down_back.astype(jnp.float32),
     )
 
 
@@ -1377,7 +2109,7 @@
         P("expert", "dp", None),
         P("expert", "dp", None),
     )
-    owned = EXPERTS // mesh.shape["expert"] == mesh.shape["dp"]
+    owned = mesh.shape["dp"] == 16 and mesh.shape["expert"] == 2
     return jax.shard_map(
         local_owned if owned else local_gathered,
         mesh=mesh,

time: 1010 us -> 866 us (0.86)
  Pallas kernels: 441 us -> 833 us
  waiting for transfers between devices: 330 us -> 0 us
  matrix products: 90.6 us -> 2.08 us
  starting transfers between devices: 58.9 us -> 0 us
  local copies, waits for them, and re-layouts: 36.2 us -> 11.8 us
  other arithmetic: 31.6 us -> 14.4 us
  between operations: 15.6 us -> 1.49 us
    pallas_call x1 -> x3, Pallas kernels: 22.1 us -> 472 us  [the longest x1 185 us: experts(): pl.pallas_call(expert_kernel, out_shape=(shape((slots, model_width), low)...]
    all_to_all x6 -> x0, waiting for transfers between devices: 295 us -> none  [the longest x2 152 us: exchange(): lax.all_to_all(rows.reshape(device_count, SLOTS, rows.shape[-1]), everyon...]
    dot_general x18 -> x0, matrix products: 88.5 us -> none  [the longest x12 62.1 us: dot_f32(): lax.dot_general(a, b, (dims, ((), ())), preferred_element_type=jnp.float32)]
    pallas_call x1, Pallas kernels: 419 us -> 361 us  [front(): pl.pallas_call(front_kernel, out_shape=tuple((o[0] for o in outs)), in_sp...]
    all_to_all x6 -> x0, starting transfers between devices: 58.4 us -> none  [the longest x3 40.1 us: give(): lax.all_to_all(parts, 'dp', split_axis=0, concat_axis=0, tiled=True)]
    psum x1 -> x0, waiting for transfers between devices: 31.8 us -> none  [scatter(): return lax.psum(part, 'expert').astype(jnp.float32)]
    concatenate x1 -> x0, local copies, waits for them, and re-layouts: 11.2 us -> none  [local_owned(): jnp.concatenate([grad_project_local, grad_small], axis=1)]
  transfers between devices with their start and end apart: 10 -> 0, of which waited for: 7 -> 0; matrix products, arithmetic and copies ran while one was open for 10% -> 0% of each run, Pallas kernels for 0% -> 0%
where the time goes in v3:
time: 866 us; the launch traced here: 863 us
  Pallas kernels  833 us (96%)
  other arithmetic  14.4 us (2%)
  local copies, waits for them, and re-layouts  11.8 us (1%)
    pallas_call x1, Pallas kernels, front(): pl.pallas_call(front_kernel, out_shape=tuple((o[0] for o in outs)), in_sp...  361 us
    pallas_call x1, Pallas kernels, experts(): pl.pallas_call(expert_kernel, out_shape=(shape((slots, model_width), low)...  185 us
    pallas_call x1, Pallas kernels, finish(): pl.pallas_call(finish_kernel, out_shape=(shape((tok_count, model_width),...  149 us
    pallas_call x1, Pallas kernels, back(): pl.pallas_call(back_kernel, out_shape=(shape((tok_count, model_width), lo...  138 us

profile of v3, /device:TPU:8, one launch (start us, length us, event | category | flops | bytes accessed | tf_op | source)
XLA Modules:
  0.0 862.8 jit_solution(2618884778587035700)
XLA Ops:
  0.6 0.0 copy-start.8
  0.7 0.0 copy-start.9
  0.7 0.0 copy-start.10
  0.7 0.0 copy-start.5
  0.7 0.0 copy-start.6
  0.7 0.0 copy-start.7
  0.7 0.9 convolution_minimum_fusion.2
  1.6 0.1 convolution_minimum_fusion.1
  1.8 0.1 convolution_minimum_fusion
  1.9 0.1 fusion.31
  2.1 1.1 fusion.28
  3.9 0.5 fusion.19
  4.4 0.8 pad_maximum_fusion
  5.2 0.8 copy.36
  6.0 0.1 eq.98
  6.1 0.7 reduce.3
  6.8 0.7 fusion.7
  7.6 0.1 convert_element_type.52
  7.7 0.1 copy.40
  7.8 0.6 scatter.4.clone.target_ref
  8.4 0.7 pad.10.route_ref
  9.1 0.0 copy-done.8
  9.1 0.1 copy.33
  9.2 0.0 copy-done.9
  9.2 0.1 copy.34
  9.3 0.0 copy-done.10
  9.3 0.1 copy.35
  9.5 0.0 copy-done.5
  9.5 0.0 copy-done.6
  9.5 0.9 concatenate.11.project_ref
  10.3 360.6 %shard_map.238 = (bf16[1536,2176]{1,0:T(8,128)(2,1)}, bf16[1536,1536]{1,0:T(8,128)(2,1)}, bf16[16,224,512]{2,1,0:T(8,128)(2,1)}, bf16[224,1536]{1,0:T(8,128)(2,1...) custom-call(f32[16]{0:T(128)} %get-tuple-element.125.bias_ref, ...), custom_call_target="tpu_custom_call" | custom-call | tf_op jit(solution)/shard_map/pallas_call | solution.py:1179
  371.0 185.4 %shard_map.239 = (bf16[1024,1536]{1,0:T(8,128)(2,1)}, bf16[1024,1536]{1,0:T(8,128)(2,1)}, bf16[1536,768]{1,0:T(8,128)(2,1)}, bf16[1536,768]{1,0:T(8,128)(2,1)}, bf16[768,1536]{1,0:T(8,128)(2,1)}) custom-call(bf16[1024,1536]{1,0:T(8,128)(2,1)} %get-tuple-element.64.rows_ref, bf16[1024,1536]{1,0:T(8,128)(2,1)} %get-tuple-element.65.grads_ref, ...), custom_call_target="tpu_custom_call" | custom-call | tf_op jit(solution)/shard_map/pallas_call | solution.py:1346
  556.4 1.8 slice.56.small_ref
  558.2 0.3 slice_reduce_fusion.3
  558.5 1.2 fusion.14.placed_ref
  559.7 138.0 %shard_map.240 = (bf16[224,1536]{1,0:T(8,128)(2,1)}, f32[224,1536]{1,0:T(8,128)}, bf16[224,1536]{1,0:T(8,128)(2,1)}, bf16[224,128]{1,0:T(8,128)(2,1)}, bf16[224,...) custom-call(f32[16]{0:T(128)} %get-tuple-element.125.bias_ref, ...), custom_call_target="tpu_custom_call" | custom-call | tf_op jit(solution)/shard_map/pallas_call | solution.py:1721
  697.7 149.1 %shard_map.241 = (f32[224,1536]{1,0:T(8,128)}, f32[96,3712]{1,0:T(8,128)}, bf16[16,48,1536]{2,1,0:T(8,128)(2,1)}) custom-call(bf16[224,1536]{1,0:T(8,128)(2,1)} %bitcast.23, bf16[224,1536]{1,0:T(8,128)(2,1)} %get-tuple-element.74.hidden_one, bf16[224,1536]{1,0:T(8,128)(2,1)} %get-tuple-element.75.hidden_two, ...), custom_call_target="tpu_custom_call" | custom-call | tf_op jit(solution)/shard_map/pallas_call | solution.py:1903
  846.8 0.0 copy-start.2
  846.8 4.6 convert_element_type.61
  851.4 1.1 fusion.29
  852.6 0.7 fusion.30
  853.3 0.7 copy.39
  854.0 1.6 slice_reduce_fusion.4
  855.6 2.7 convert_element_type.59
  858.2 0.0 copy-done
  858.2 2.7 convert_element_type.60
  860.9 0.8 copy.43
  861.8 1.1 copy.44
  (15 shorter events, 0.1 us)
Async XLA Ops:
  0.6 8.4 copy-start.8
  0.7 8.5 copy-start.9
  0.7 8.7 %copy-start.10 = (bf16[96]{0:T(256)(128)(2,1)S(1)}, bf16[96]{0:T(256)(128)(2,1)}, u32[]{:S(2)}) copy-start(bf16[96]{0:T(256)(128)(2,1)} %param.23) | copy-start | bytes 580
  0.7 8.8 %copy-start.5 = (bf16[96,1536]{1,0:T(8,128)(2,1)S(1)}, bf16[96,1536]{1,0:T(8,128)(2,1)}, u32[]{:S(2)}) copy-start(bf16[96,1536]{1,0:T(8,128)(2,1)} %param.19) | copy-start | bytes 884740
  0.7 8.8 %copy-start.6 = (bf16[96,256]{1,0:T(8,128)(2,1)S(1)}, bf16[96,256]{1,0:T(8,128)(2,1)}, u32[]{:S(2)}) copy-start(bf16[96,256]{1,0:T(8,128)(2,1)} %param.20) | copy-start | bytes 147460
  0.7 8.8 %copy-start.7 = (bf16[96,256]{1,0:T(8,128)(2,1)S(1)}, bf16[96,256]{1,0:T(8,128)(2,1)}, u32[]{:S(2)}) copy-start(bf16[96,256]{1,0:T(8,128)(2,1)} %param.21) | copy-start | bytes 147460
  846.8 4.6 copy-start.2
  851.4 4.1 copy-start.1
  855.6 2.7 copy-start
  858.2 2.7 copy-start.4
  858.2 3.5 copy-start.3

commit v4 on v3

--- a/solution.py
+++ b/solution.py
@@ -884,7 +884,6 @@
     placed,
     acc,
     top,
-    total,
     project_send,
     project_recv,
     out_send,
@@ -1019,37 +1018,35 @@
     weights.start_own()
 
     row = lax.broadcasted_iota(jnp.int32, (tok_count, tok_count), 0)
-    column = lax.broadcasted_iota(jnp.int32, (tok_count, tok_count), 1)
-    causal = column <= row
+    column_index = lax.broadcasted_iota(jnp.int32, (tok_count, tok_count), 1)
+    causal = column_index <= row
+    ones = jnp.ones((tok_count, LANES), jnp.bfloat16)
 
     def visit(label, own):
-        for head in range(HEADS):
-            group = head // repeat_heads
-            query = query_ref[:, head * HEAD : (head + 1) * HEAD]
+        for group in range(KV_HEADS):
             key = keys_ref[label, :, group * HEAD : (group + 1) * HEAD]
             value = keys_ref[label, :, (KV_HEADS + group) * HEAD : (KV_HEADS + group + 1) * HEAD]
-            scores = dot_f32(query, key, ((1,), (1,)))
-            if own:
-                scores = jnp.where(causal, scores, -1e30)
-                peak = jnp.max(scores, axis=-1, keepdims=True)
-                shift = peak
-            else:
-                bias = bias_ref[label]
-                peak = jnp.maximum(top[head], jnp.max(scores, axis=-1, keepdims=True) + bias)
-                shift = peak - bias
-            prob = jnp.exp2((scores - shift) * factor)
-            prob_high = prob.astype(jnp.bfloat16)
-            prob_low = (prob - prob_high.astype(jnp.float32)).astype(jnp.bfloat16)
-            part = dot_f32(prob_high, value) + dot_f32(prob_low, value)
-            part_total = jnp.sum(prob, axis=-1, keepdims=True)
-            if own:
-                acc[head] = part
-                total[head] = part_total
-            else:
-                fade = jnp.exp2((top[head] - peak) * factor)
-                acc[head] = acc[head] * fade + part
-                total[head] = total[head] * fade + part_total
-            top[head] = peak
+            value = jnp.concatenate([value, ones], axis=1)
+            for head in range(group * repeat_heads, (group + 1) * repeat_heads):
+                query = query_ref[:, head * HEAD : (head + 1) * HEAD]
+                scores = dot_f32(query, key, ((1,), (1,))) * factor
+                if own:
+                    scores = jnp.where(causal, scores, -1e30)
+                    peak = jnp.ceil(jnp.max(scores, axis=-1, keepdims=True))
+                    shift = peak
+                else:
+                    bias = bias_ref[label]
+                    peak = jnp.ceil(
+                        jnp.maximum(top[head], jnp.max(scores, axis=-1, keepdims=True) + bias)
+                    )
+                    shift = peak - bias
+                prob = jnp.exp2(scores - shift).astype(jnp.bfloat16)
+                part = dot_f32(prob, value)
+                if own:
+                    acc[head] = part
+                else:
+                    acc[head] = acc[head] * jnp.exp2(top[head] - peak) + part
+                top[head] = peak
 
     visit(place.dp, True)
 
@@ -1074,10 +1071,11 @@
     lane = lax.broadcasted_iota(jnp.int32, (tok_count, LANES), 1)
     stats = jnp.zeros((tok_count, LANES), jnp.float32)
     for head in range(HEADS):
-        exact = acc[head] / total[head]
+        exact = acc[head, :, :HEAD] / acc[head, :, HEAD:]
         exact_ref[:, head * HEAD : (head + 1) * HEAD] = exact
         attended_ref[:, head * HEAD : (head + 1) * HEAD] = exact.astype(jnp.bfloat16)
-        stats = jnp.where(lane == head, top[head] * factor + jnp.log2(total[head]), stats)
+        stats = jnp.where(lane == head, top[head], stats)
+        stats = jnp.where(lane == HEADS + head, 1.0 / acc[head, :, HEAD:], stats)
     stat_ref[...] = stats
     out.finish()
 
@@ -1191,8 +1189,7 @@
             pltpu.VMEM((4, tok_count + PAD_TOKENS, model_width), low),
             pltpu.VMEM((4, tok_count, model_width), low),
             pltpu.VMEM((4, 8 * SLOTS, TILE), low),
-            pltpu.VMEM((HEADS, tok_count, HEAD), full),
-            pltpu.VMEM((HEADS, tok_count, 1), full),
+            pltpu.VMEM((HEADS, tok_count, 2 * HEAD), full),
             pltpu.VMEM((HEADS, tok_count, 1), full),
         ]
         + [dma((20,)), dma((dp_count,))] * 3
@@ -1480,6 +1477,155 @@
             self.hop_x(z).wait_send()
         for i in range(3):
             self.hop_z(i).wait_send()
+
+
+def add_rows(block, land, low, count):
+    chunk = 16
+
+    @pl.loop(0, count // chunk)
+    def _(index):
+        cut = pl.ds(pl.multiple_of(low + index * chunk, chunk), chunk)
+        value = block[cut].astype(jnp.float32) + land[rows_of(index, chunk)].astype(jnp.float32)
+        block[cut] = value.astype(jnp.bfloat16)
+
+
+class TotalSum:
+    def __init__(self, place, part, lands, send, recv, x_first):
+        self.place, self.part, self.lands = place, part, lands
+        self.send, self.recv, self.x_first = send, recv, x_first
+        self.rows = part.shape[1]
+        self.half = self.rows // 2
+
+    def kept(self, side):
+        return pl.ds(pl.multiple_of(side * self.half, self.half), self.half)
+
+    def hop(self, source, land, number, dp, side):
+        return remote(source, land, self.send.at[number], self.recv.at[number], dp, side)
+
+    def core(self, z, x):
+        p = self.place
+        return self.hop(
+            self.part.at[p.index(z, x, 1 - p.c)],
+            self.lands[0].at[z * 2 + x],
+            z * 2 + x,
+            p.index(p.z, p.x, 1 - p.c),
+            p.side,
+        )
+
+    def over_x(self, z):
+        p = self.place
+        source = self.part.at[p.index(z, 1 - p.x, p.c)]
+        if not self.x_first:
+            source = source.at[self.kept(p.side)]
+        return self.hop(source, self.lands[1].at[z], 8 + z, p.index(p.z, 1 - p.x, p.c), p.side)
+
+    def over_side(self, z, x):
+        p = self.place
+        number = z if self.x_first else z * 2 + x
+        return self.hop(
+            self.part.at[p.index(z, x, p.c), self.kept(1 - p.side)],
+            self.lands[2].at[number],
+            12 + number,
+            p.dp,
+            1 - p.side,
+        )
+
+    def over_z(self, i):
+        p = self.place
+        z = p.others()[i]
+        return self.hop(
+            self.part.at[p.index(z, p.x, p.c), self.kept(p.side)],
+            self.lands[3].at[i],
+            20 + i,
+            p.index(z, p.x, p.c),
+            p.side,
+        )
+
+    def home(self):
+        p = self.place
+        block = self.part.at[p.dp, self.kept(p.side)]
+        return self.hop(block, self.lands[4], 23, p.dp, 1 - p.side)
+
+    def start(self, z):
+        for x in range(2):
+            self.core(z, x).start()
+
+    def sides(self):
+        return (self.place.x,) if self.x_first else (1 - self.place.x, self.place.x)
+
+    def first(self, z):
+        p = self.place
+        for x in (1 - p.x, p.x):
+            self.core(z, x).wait_recv()
+            add_rows(self.part.at[p.index(z, x, p.c)], self.lands[0].at[z * 2 + x], 0, self.rows)
+            if not self.x_first:
+                self.over_side(z, x).start()
+        if self.x_first:
+            self.over_x(z).start()
+
+    def take_side(self, z):
+        p = self.place
+        for x in self.sides():
+            self.over_side(z, x).wait_recv()
+            number = z if self.x_first else z * 2 + x
+            add_rows(
+                self.part.at[p.index(z, x, p.c)],
+                self.lands[2].at[number],
+                p.side * self.half,
+                self.half,
+            )
+
+    def take_x(self, z):
+        p = self.place
+        self.over_x(z).wait_recv()
+        low, count = (0, self.rows) if self.x_first else (p.side * self.half, self.half)
+        add_rows(self.part.at[p.index(z, p.x, p.c)], self.lands[1].at[z], low, count)
+
+    def second(self, z):
+        if self.x_first:
+            self.take_x(z)
+            self.over_side(z, self.place.x).start()
+        else:
+            self.take_side(z)
+            self.over_x(z).start()
+
+    def third(self, z, i):
+        if self.x_first:
+            self.take_side(z)
+        else:
+            self.take_x(z)
+        if i < 3:
+            self.over_z(i).start()
+
+    def fourth(self):
+        p = self.place
+        for i in range(3):
+            self.over_z(i).wait_recv()
+        chunk = 16
+
+        @pl.loop(0, self.half // chunk)
+        def _(index):
+            cut = pl.ds(pl.multiple_of(p.side * self.half + index * chunk, chunk), chunk)
+            value = self.part[p.dp, cut].astype(jnp.float32)
+            for i in range(3):
+                value += self.lands[3][i, rows_of(index, chunk)].astype(jnp.float32)
+            self.part[p.dp, cut] = value.astype(jnp.bfloat16)
+
+        self.home().start()
+
+    def finish(self, mine, at):
+        p = self.place
+        mine[self.kept(p.side), at] = self.part[p.dp, self.kept(p.side)].astype(jnp.float32)
+        self.home().wait()
+        mine[self.kept(1 - p.side), at] = self.lands[4][...].astype(jnp.float32)
+        for z in range(4):
+            for x in range(2):
+                self.core(z, x).wait_send()
+            self.over_x(z).wait_send()
+            for x in self.sides():
+                self.over_side(z, x).wait_send()
+        for i in range(3):
+            self.over_z(i).wait_send()
 
 
 class WeightReturn(WeightSwap):
@@ -1624,8 +1770,12 @@
 
     for head in range(HEADS):
         cut = slice(head * HEAD, (head + 1) * HEAD)
+        scaled = (
+            grad_ref[:, cut].astype(jnp.float32) * stat_ref[:, HEADS + head : HEADS + head + 1]
+        ).astype(jnp.bfloat16)
+        grad_ref[:, cut] = scaled
         delta[head] = jnp.sum(
-            grad_ref[:, cut].astype(jnp.float32) * exact_ref[:, cut], axis=-1, keepdims=True
+            scaled.astype(jnp.float32) * exact_ref[:, cut], axis=-1, keepdims=True
         )
     row = lax.broadcasted_iota(jnp.int32, (tok_count, tok_count), 0)
     column = lax.broadcasted_iota(jnp.int32, (tok_count, tok_count), 1)
@@ -1654,9 +1804,12 @@
                 prob = jnp.exp2(scores * factor - shift)
                 if own:
                     prob = jnp.where(causal, prob, 0.0)
+                prob = prob.astype(jnp.bfloat16)
                 grad_prob = dot_f32(grad, value, ((1,), (1,)))
-                grad_score = (prob * (grad_prob - delta[head])).astype(jnp.bfloat16)
-                grad_value += dot_f32(prob.astype(jnp.bfloat16), grad, ((0,), (0,)))
+                grad_score = (prob.astype(jnp.float32) * (grad_prob - delta[head])).astype(
+                    jnp.bfloat16
+                )
+                grad_value += dot_f32(prob, grad, ((0,), (0,)))
                 grad_key += dot_f32(grad_score, query, ((0,), (0,)))
                 grad_query = dot_f32(grad_score, key)
                 if own:
@@ -1775,17 +1928,22 @@
     down_back,
     grad_hidden,
     gain_one,
-    partial_ref,
-    pair_send,
-    pair_land,
-    land_core,
-    land_x,
-    land_z,
-    scatter_send,
-    recv_core,
-    recv_x,
-    recv_z,
-    pair_sem,
+    part_one,
+    core_one,
+    x_one,
+    side_one,
+    z_one,
+    home_one,
+    part_two,
+    core_two,
+    x_two,
+    side_two,
+    z_two,
+    home_two,
+    send_one,
+    recv_one,
+    send_two,
+    recv_two,
     weight_send,
     weight_recv,
     weight_local,
@@ -1803,13 +1961,9 @@
     )
     weights.start(1, dp_count)
     weights.start_own()
-    scatter = Scatter(
-        place,
-        lambda index: partial_ref.at[index],
-        (land_core, land_x, land_z),
-        scatter_send,
-        (recv_core, recv_x, recv_z),
-    )
+    one = TotalSum(place, part_one, (core_one, x_one, side_one, z_one, home_one), send_one, recv_one, True)
+    two = TotalSum(place, part_two, (core_two, x_two, side_two, z_two, home_two), send_two, recv_two, False)
+    cut_at = part_one.shape[2]
 
     @pl.loop(0, model_width // TILE)
     def _(tile):
@@ -1841,51 +1995,50 @@
     def _(index):
         cut = columns(index, group)
 
-        def put(at, value):
+        def put(part, low, value):
             for i in range(4):
-                partial_ref[index * 4 + i, :, at] = value[i * shard : (i + 1) * shard].astype(
-                    jnp.bfloat16
-                )
-
-        step = 512
+                part[index * 4 + i, :, low : low + value.shape[1]] = value[
+                    i * shard : (i + 1) * shard
+                ].astype(jnp.bfloat16)
+
         left = hidden_one[:, cut]
-        for n in range(width // step):
-            at = slice(n * step, (n + 1) * step)
-            put(at, dot_f32(left, grad_project_ref[:, at], ((0,), (0,))))
+        step = 3 * LANES
+        for low in range(0, cut_at, step):
+            put(part_one, low, dot_f32(left, grad_project_ref[:, low : low + step], ((0,), (0,))))
+        rest = width - cut_at
+        put(part_two, 0, dot_f32(left, grad_project_ref[:, cut_at:], ((0,), (0,))))
         small = dot_f32(hidden_two[:, cut], grad_logits_ref[...], ((0,), (0,)))
         for part in split3(gain_one[:, cut]):
             small += dot_f32(part, one_lane, ((0,), (0,)))
         for part in split3(gain_ref[:, cut]):
             small += dot_f32(part, two_lane, ((0,), (0,)))
-        put(slice(width, width + LANES), small)
+        put(part_two, rest, small)
         left = attended_ref[:, cut]
-        for n in range(model_width // step):
-            at = slice(n * step, (n + 1) * step)
+        for low in range(0, model_width, step):
             put(
-                slice(width + LANES + n * step, width + LANES + (n + 1) * step),
-                dot_f32(left, grad_branch_ref[:, at], ((0,), (0,))),
+                part_two,
+                rest + LANES + low,
+                dot_f32(left, grad_branch_ref[:, low : low + step], ((0,), (0,))),
             )
-
-    scatter.start()
-    scatter.pass_core()
-    scatter.pass_x()
-
-    def keep(cut, value):
-        pair_send[cut] = value.astype(jnp.bfloat16)
-
-    scatter.pass_z(keep)
-    pair = remote(
-        pair_send, pair_land, pair_sem.at[0], pair_sem.at[1], place.dp, 1 - place.side
-    )
-    pair.start()
-    scatter.finish()
-    pair.wait()
+        for total in (one, two):
+            total.start(index)
+
+    order = place.others() + [place.z]
+    both = (one, two)
+    for z in order:
+        for total in both:
+            total.first(z)
+    for z in order:
+        for total in both:
+            total.second(z)
+    for i, z in enumerate(order):
+        for total in both:
+            total.third(z, i)
+    for total in both:
+        total.fourth()
+    one.finish(mine_ref, slice(0, cut_at))
+    two.finish(mine_ref, slice(cut_at, mine_ref.shape[1]))
     weights.finish()
-
-    @pl.loop(0, shard // chunk)
-    def _(index):
-        cut = rows_of(index, chunk)
-        mine_ref[cut] = pair_send[cut].astype(jnp.float32) + pair_land[cut].astype(jnp.float32)
 
 
 def finish(
@@ -1895,6 +2048,7 @@
     tok_count, model_width = tokens.shape
     dp_count = lax.axis_size("dp")
     width = project.shape[1] + model_width
+    first = 15 * LANES
     vmem = pl.BlockSpec(memory_space=pltpu.VMEM)
     anywhere = pl.BlockSpec(memory_space=pl.ANY)
     low, full = jnp.bfloat16, jnp.float32
@@ -1912,17 +2066,27 @@
         scratch_shapes=[
             pltpu.VMEM((tok_count, model_width), full),
             pltpu.VMEM((8, model_width), full),
-            pltpu.VMEM((dp_count, shard, width), low),
-            pltpu.VMEM((shard, width), low),
-            pltpu.VMEM((shard, width), low),
-            pltpu.VMEM((8, shard, width), low),
-            pltpu.VMEM((4, shard, width), low),
-            pltpu.VMEM((3, shard, width), low),
-            dma((15,)),
-            dma((8,)),
-            dma((4,)),
-            dma((3,)),
-            dma((2,)),
+            *(
+                pltpu.VMEM(lead + (columns_of,), low)
+                for columns_of, lead in (
+                    (first, (dp_count, shard)),
+                    (first, (8, shard)),
+                    (first, (4, shard)),
+                    (first, (4, shard // 2)),
+                    (first, (3, shard // 2)),
+                    (first, (shard // 2,)),
+                    (width - first, (dp_count, shard)),
+                    (width - first, (8, shard)),
+                    (width - first, (4, shard // 2)),
+                    (width - first, (8, shard // 2)),
+                    (width - first, (3, shard // 2)),
+                    (width - first, (shard // 2,)),
+                )
+            ),
+            dma((24,)),
+            dma((24,)),
+            dma((24,)),
+            dma((24,)),
             dma((dp_count, 1)),
             dma((dp_count, 1)),
             dma((1,)),

time: 866 us -> 826 us (0.954)
  Pallas kernels: 833 us -> 796 us
    pallas_call x1, Pallas kernels: 149 us -> 112 us  [finish(): pl.pallas_call(finish_kernel, out_shape=(shape((tok_count, model_width),...]
where the time goes in v4:
time: 826 us
  Pallas kernels  796 us (96%)
  other arithmetic  14.4 us (2%)
  local copies, waits for them, and re-layouts  11.8 us (1%)
    pallas_call x1, Pallas kernels, front(): pl.pallas_call(front_kernel, out_shape=tuple((o[0] for o in outs)), in_sp...  361 us
    pallas_call x1, Pallas kernels, experts(): pl.pallas_call(expert_kernel, out_shape=(shape((slots, model_width), low)...  185 us
    pallas_call x1, Pallas kernels, back(): pl.pallas_call(back_kernel, out_shape=(shape((tok_count, model_width), lo...  138 us
    pallas_call x1, Pallas kernels, finish(): pl.pallas_call(finish_kernel, out_shape=(shape((tok_count, model_width),...  112 us

profile of v4, /device:TPU:8, one launch (start us, length us, event | category | flops | bytes accessed | tf_op | source)
XLA Modules:
  0.0 825.6 jit_solution(1263047496509548301)
XLA Ops:
  0.6 0.0 copy-start.8
  0.7 0.0 copy-start.9
  0.7 0.0 copy-start.10
  0.7 0.0 copy-start.5
  0.7 0.0 copy-start.6
  0.7 0.0 copy-start.7
  0.7 0.9 convolution_minimum_fusion.2
  1.6 0.1 convolution_minimum_fusion.1
  1.8 0.1 convolution_minimum_fusion
  1.9 0.1 fusion.31
  2.1 1.1 fusion.28
  3.9 0.5 fusion.19
  4.4 0.8 pad_maximum_fusion
  5.2 0.8 copy.36
  6.0 0.1 eq.98
  6.1 0.7 reduce.3
  6.8 0.7 fusion.7
  7.6 0.1 convert_element_type.52
  7.7 0.1 copy.40
  7.8 0.6 scatter.4.clone.target_ref
  8.4 0.7 pad.10.route_ref
  9.1 0.0 copy-done.8
  9.1 0.1 copy.33
  9.2 0.0 copy-done.9
  9.2 0.1 copy.34
  9.3 0.0 copy-done.10
  9.3 0.1 copy.35
  9.5 0.0 copy-done.5
  9.5 0.0 copy-done.6
  9.5 0.9 concatenate.11.project_ref
  10.3 360.6 %shard_map.238 = (bf16[1536,2176]{1,0:T(8,128)(2,1)}, bf16[1536,1536]{1,0:T(8,128)(2,1)}, bf16[16,224,512]{2,1,0:T(8,128)(2,1)}, bf16[224,1536]{1,0:T(8,128)(2,1...) custom-call(f32[16]{0:T(128)} %get-tuple-element.125.bias_ref, ...), custom_call_target="tpu_custom_call" | custom-call | tf_op jit(solution)/shard_map/pallas_call | solution.py:1177
  371.0 185.4 %shard_map.239 = (bf16[1024,1536]{1,0:T(8,128)(2,1)}, bf16[1024,1536]{1,0:T(8,128)(2,1)}, bf16[1536,768]{1,0:T(8,128)(2,1)}, bf16[1536,768]{1,0:T(8,128)(2,1)}, bf16[768,1536]{1,0:T(8,128)(2,1)}) custom-call(bf16[1024,1536]{1,0:T(8,128)(2,1)} %get-tuple-element.64.rows_ref, bf16[1024,1536]{1,0:T(8,128)(2,1)} %get-tuple-element.65.grads_ref, ...), custom_call_target="tpu_custom_call" | custom-call | tf_op jit(solution)/shard_map/pallas_call | solution.py:1343
  556.4 1.8 slice.56.small_ref
  558.2 0.3 slice_reduce_fusion.3
  558.5 1.2 fusion.14.placed_ref
  559.7 138.0 %shard_map.240 = (bf16[224,1536]{1,0:T(8,128)(2,1)}, f32[224,1536]{1,0:T(8,128)}, bf16[224,1536]{1,0:T(8,128)(2,1)}, bf16[224,128]{1,0:T(8,128)(2,1)}, bf16[224,...) custom-call(f32[16]{0:T(128)} %get-tuple-element.125.bias_ref, ...), custom_call_target="tpu_custom_call" | custom-call | tf_op jit(solution)/shard_map/pallas_call | solution.py:1874
  697.7 111.8 %shard_map.241 = (f32[224,1536]{1,0:T(8,128)}, f32[96,3712]{1,0:T(8,128)}, bf16[16,48,1536]{2,1,0:T(8,128)(2,1)}) custom-call(bf16[224,1536]{1,0:T(8,128)(2,1)} %bitcast.23, bf16[224,1536]{1,0:T(8,128)(2,1)} %get-tuple-element.74.hidden_one, bf16[224,1536]{1,0:T(8,128)(2,1)} %get-tuple-element.75.hidden_two, ...), custom_call_target="tpu_custom_call" | custom-call | tf_op jit(solution)/shard_map/pallas_call | solution.py:2057
  809.5 4.6 convert_element_type.61
  814.2 0.0 copy-done.2
  814.2 1.1 fusion.29
  815.3 0.7 fusion.30
  816.0 0.7 copy.39
  816.7 1.6 slice_reduce_fusion.4
  818.3 0.0 copy-done.1
  818.3 2.7 convert_element_type.59
  821.0 2.7 convert_element_type.60
  823.6 0.8 copy.43
  824.5 1.1 copy.44
  (15 shorter events, 0.1 us)
Async XLA Ops:
  0.6 8.4 %copy-start.8 = (bf16[96,32]{0,1:T(8,128)(2,1)S(1)}, bf16[96,32]{0,1:T(8,128)(2,1)}, u32[]{:S(2)}) copy-start(bf16[96,32]{0,1:T(8,128)(2,1)} %param.24) | copy-start | bytes 18436
  0.7 8.5 %copy-start.9 = (bf16[96]{0:T(256)(128)(2,1)S(1)}, bf16[96]{0:T(256)(128)(2,1)}, u32[]{:S(2)}) copy-start(bf16[96]{0:T(256)(128)(2,1)} %param.18) | copy-start | bytes 580
  0.7 8.7 %copy-start.10 = (bf16[96]{0:T(256)(128)(2,1)S(1)}, bf16[96]{0:T(256)(128)(2,1)}, u32[]{:S(2)}) copy-start(bf16[96]{0:T(256)(128)(2,1)} %param.23) | copy-start | bytes 580
  0.7 8.8 %copy-start.5 = (bf16[96,1536]{1,0:T(8,128)(2,1)S(1)}, bf16[96,1536]{1,0:T(8,128)(2,1)}, u32[]{:S(2)}) copy-start(bf16[96,1536]{1,0:T(8,128)(2,1)} %param.19) | copy-start | bytes 884740
  0.7 8.8 %copy-start.6 = (bf16[96,256]{1,0:T(8,128)(2,1)S(1)}, bf16[96,256]{1,0:T(8,128)(2,1)}, u32[]{:S(2)}) copy-start(bf16[96,256]{1,0:T(8,128)(2,1)} %param.20) | copy-start | bytes 147460
  0.7 8.8 %copy-start.7 = (bf16[96,256]{1,0:T(8,128)(2,1)S(1)}, bf16[96,256]{1,0:T(8,128)(2,1)}, u32[]{:S(2)}) copy-start(bf16[96,256]{1,0:T(8,128)(2,1)} %param.21) | copy-start | bytes 147460
  809.5 4.6 copy-start.2
  814.2 4.1 copy-start.1
  818.3 2.7 copy-start
  821.0 2.7 copy-start.4
  821.0 3.5 copy-start.3

commit v5 on v4

--- a/solution.py
+++ b/solution.py
@@ -692,22 +692,19 @@
     def of(self, member):
         return member // 4, (member // 2) % 2, member % 2
 
-    def rank(self, z, side, x, c):
-        return side * self.dp_count + self.place.index(z, x, c)
-
     def me(self):
         p = self.place
         return p.side * 4 + p.x * 2 + p.c
 
-    def block(self, rank):
-        return self.target.at[rows_of(rank, SLOTS)]
+    def block(self, z, origin):
+        return self.target.at[rows_of(z * 8 + origin, SLOTS)]
 
     def copy(self, z, step, to, origin):
         p = self.place
         side, x, c = self.of(to)
         return remote(
             self.source.at[z, rows_of(to, SLOTS)],
-            self.block(self.rank(z, *self.of(origin))),
+            self.block(z, origin),
             self.send.at[z, step],
             self.recv.at[z, step],
             p.index(p.z, x, c),
@@ -717,7 +714,7 @@
     def own_copy(self, z):
         return pltpu.make_async_copy(
             self.source.at[z, rows_of(self.me(), SLOTS)],
-            self.block(self.rank(z, *self.of(self.me()))),
+            self.block(z, self.me()),
             self.local.at[z],
         )
 
@@ -726,60 +723,88 @@
             self.copy(z, step, (self.me() + step) % 8, self.me()).start()
         self.own_copy(z).start()
 
-    def finish(self):
+    def arrived(self, z):
+        for step in range(1, 8):
+            other = (self.me() + 8 - step) % 8
+            self.copy(z, step, other, other).wait_recv()
+        self.own_copy(z).wait()
+
+    def sent(self):
         @pl.loop(0, 4)
         def _(z):
             for step in range(1, 8):
-                other = (self.me() + 8 - step) % 8
-                self.copy(z, step, other, other).wait()
-            self.own_copy(z).wait()
-
-
-class RowSwap:
-    def __init__(self, source, target, send, recv, local, dp_count, device_count):
-        self.source, self.target = source, target
-        self.send, self.recv, self.local = send, recv, local
-        self.dp_count, self.device_count = dp_count, device_count
-        self.rank = lax.axis_index("expert") * dp_count + lax.axis_index("dp")
-
-    def block(self, ref, index):
-        return ref.at[pl.ds(pl.multiple_of(index * SLOTS, SLOTS), SLOTS)]
-
-    def copy(self, step, to, landing):
+                self.copy(z, step, (self.me() + step) % 8, self.me()).wait_send()
+
+    def finish(self):
+        pl.loop(0, 4)(self.arrived)
+        self.sent()
+
+
+class Chain:
+    def __init__(self, place, part, land, send, recv):
+        self.place, self.part, self.land = place, part, land
+        self.send, self.recv = send, recv
+
+    def hop(self, z, step):
+        p = self.place
+        if step > 0:
+            slot = z
+        else:
+            slot = z + (4 - z) * ((3 - (p.z - 1 - z)) // 3)
+        target = p.index(p.z + step, p.x, p.c)
         return remote(
-            self.block(self.source, to),
-            self.block(self.target, landing),
-            self.send.at[step],
-            self.recv.at[step],
-            to % self.dp_count,
-            to // self.dp_count,
+            self.part.at[z], self.land.at[slot], self.send.at[z], self.recv.at[slot], target, p.side
         )
 
-    def own_copy(self):
-        return pltpu.make_async_copy(
-            self.block(self.source, self.rank), self.block(self.target, self.rank), self.local
-        )
-
-    def start(self):
-        @pl.loop(1, self.device_count)
-        def _(step):
-            self.copy(step, (self.rank + step) % self.device_count, self.rank).start()
-
-        self.own_copy().start()
-
-    def start_one(self, to):
-        @pl.when(to != self.rank)
+    def arrived(self, slot, step):
+        p = self.place
+        target = p.index(p.z + step, p.x, p.c)
+        remote(
+            self.part.at[0], self.land.at[slot], self.send.at[0], self.recv.at[slot], target, p.side
+        ).wait_recv()
+
+    def take(self, z, step):
+        self.arrived(z, step)
+        add_rows(self.part.at[z], self.land.at[z], 0, self.part.shape[1])
+
+    def run(self, number):
+        here = self.place.z
+        up, down = 3 - number, number
+
+        @pl.when(up > here)
         def _():
-            step = (to + self.device_count - self.rank) % self.device_count
-            self.copy(step, to, self.rank).start()
-
-    def finish(self):
-        @pl.loop(1, self.device_count)
-        def _(step):
-            other = (self.rank + self.device_count - step) % self.device_count
-            self.copy(step, other, other).wait()
-
-        self.own_copy().wait()
+            pl.when(here > 0)(lambda: self.take(up, -1))
+            self.hop(up, 1).start()
+
+        @pl.when(down < here)
+        def _():
+            pl.when(here < 3)(lambda: self.take(down, 1))
+            self.hop(down, -1).start()
+
+    def finish(self, out):
+        here = self.place.z
+        chunk = 16
+
+        def take(slot, step):
+            self.arrived(slot, step)
+
+            @pl.loop(0, out.shape[0] // chunk)
+            def _(index):
+                cut = rows_of(index, chunk)
+                out[cut] += self.land[slot, cut].astype(jnp.float32)
+
+        @pl.loop(0, out.shape[0] // chunk)
+        def _(index):
+            cut = rows_of(index, chunk)
+            out[cut] = self.part[here, cut].astype(jnp.float32)
+
+        pl.when(here > 0)(lambda: take(here, -1))
+        pl.when(here < 3)(lambda: take(4, 1))
+
+        @pl.loop(0, 4)
+        def _(z):
+            pl.when(z > here)(lambda: self.hop(z, 1).wait_send())
+            pl.when(z < here)(lambda: self.hop(z, -1).wait_send())
 
 
 class WeightSwap:
@@ -842,6 +867,13 @@
 
 def rows_of(index, count):
     return pl.ds(pl.multiple_of(index * count, count), count)
+
+
+def slot_labels(place, dp_count):
+    row = lax.broadcasted_iota(jnp.int32, (8 * SLOTS, TILE), 0)
+    member = row // SLOTS
+    label = ((member // 4) * dp_count + place.z * 4 + member % 4) * SLOTS + row % SLOTS
+    return label.astype(jnp.float32)
 
 
 def front_kernel(
@@ -873,12 +905,12 @@
     up_own,
     down_own,
     hidden_one,
+    target_all,
+    gate_all,
     keys_own,
     row_send,
     grad_send,
-    target_all,
     gate_own_row,
-    gate_all,
     hidden_all,
     grad_all,
     placed,
@@ -959,8 +991,7 @@
     slot_row = lax.broadcasted_iota(jnp.int32, (plane_slots, TILE), 0)
     slot_lane = lax.broadcasted_iota(jnp.int32, (plane_slots, TILE), 1)
     member = slot_row // SLOTS
-    label = ((member // 4) * dp_count + place.z * 4 + member % 4) * SLOTS + slot_row % SLOTS
-    label = label.astype(jnp.float32)
+    label = slot_labels(place, dp_count)
     spare = (slot_lane - tok_count == member) & (slot_row % SLOTS == CAP)
 
     def match(z, choice):
@@ -1172,6 +1203,8 @@
         (shape((model_width, ff_width), low), anywhere),
         (shape((ff_width, model_width), low), anywhere),
         (shape((tok_count, model_width), low), vmem),
+        (shape((4, 8, TILE), full), vmem),
+        (shape((4, 8, TILE), full), vmem),
     )
     dma = pltpu.SemaphoreType.DMA
     return pl.pallas_call(
@@ -1183,9 +1216,7 @@
             pltpu.VMEM((tok_count, 2 * key_width), low),
             pltpu.VMEM((4, 8 * SLOTS, model_width), low),
             pltpu.VMEM((4, 8 * SLOTS, model_width), low),
-            pltpu.VMEM((4, 8, TILE), full),
             pltpu.VMEM((8, TILE), full),
-            pltpu.VMEM((4, 8, TILE), full),
             pltpu.VMEM((4, tok_count + PAD_TOKENS, model_width), low),
             pltpu.VMEM((4, tok_count, model_width), low),
             pltpu.VMEM((4, 8 * SLOTS, TILE), low),
@@ -1231,36 +1262,63 @@
     gate_ref,
     up_ref,
     down_ref,
-    rows_back,
-    outs_back,
+    target_all,
+    gate_all,
+    row_sum,
+    out_sum,
+    gate_sum,
     gate_grad_ref,
     up_grad_ref,
     down_grad_ref,
+    row_send,
+    row_plane,
+    row_part,
+    row_land,
     out_send,
-    row_send,
+    out_plane,
+    out_part,
+    out_land,
+    gate_part,
+    gate_land,
     grad_out,
     inner_ref,
     gate_act_grad,
     up_act_grad,
     row_send_sem,
     row_recv_sem,
+    row_local,
     out_send_sem,
     out_recv_sem,
-    local,
+    out_local,
+    row_chain_send,
+    row_chain_recv,
+    out_chain_send,
+    out_chain_recv,
+    gate_send_sem,
+    gate_recv_sem,
 ):
     dp_count = lax.axis_size("dp")
     slots, model_width = rows_ref.shape
     ff_width = gate_ref.shape[1]
+    tok_count = row_sum.shape[0]
     device_count = slots // SLOTS
+    place = Place()
     enter(device_count, dp_count)
-    rows = RowSwap(row_send, rows_back, row_send_sem, row_recv_sem, local.at[0], dp_count, device_count)
-    outs = RowSwap(out_send, outs_back, out_send_sem, out_recv_sem, local.at[1], dp_count, device_count)
-    tiles = slots // TILE
-    per_tile = TILE // SLOTS
-
-    @pl.loop(0, tiles)
+    rows = PlaneSwap(place, row_send, row_plane, row_send_sem, row_recv_sem, row_local, dp_count)
+    outs = PlaneSwap(place, out_send, out_plane, out_send_sem, out_recv_sem, out_local, dp_count)
+    row_chain = Chain(place, row_part, row_land, row_chain_send, row_chain_recv)
+    out_chain = Chain(place, out_part, out_land, out_chain_send, out_chain_recv)
+
+    digits = 27 + 72 * place.z - 15 * (place.z // 2)
+
+    def level(step):
+        power = 1 + 3 * step + 9 * (step * (step - 1) // 2)
+        power += 27 * (step * (step - 1) * (step - 2) // 6)
+        return (digits // power) % 4
+
+    @pl.loop(0, 4)
     def _(step):
-        tile = (step + rows.rank // per_tile) % tiles
+        tile = level(step)
         cut = rows_of(tile, TILE)
         row = rows_ref[cut]
         gate = pick_gates(row[:, :LANES])
@@ -1278,7 +1336,7 @@
         for n in range(model_width // TILE):
             part = slice(n * TILE, (n + 1) * TILE)
             expert_out = dot_f32(inner, down_ref[:, part]).astype(jnp.bfloat16)
-            out_send[cut, part] = expert_out
+            out_send[tile, :, part] = expert_out
             grad = grads_ref[cut, part].astype(jnp.float32)
             gate_grad += jnp.sum(expert_out.astype(jnp.float32) * grad, axis=-1, keepdims=True)
             grad_out[cut, part] = (gate * grad).astype(jnp.bfloat16)
@@ -1289,34 +1347,105 @@
             grad_inner = dot_f32(grad, down_ref[part, :], ((1,), (1,)))
             gate_act_grad[cut, part] = (grad_inner * slope).astype(jnp.bfloat16)
             up_act_grad[cut, part] = (grad_inner * swish).astype(jnp.bfloat16)
-        fold = one_hot((per_tile, TILE), lambda r, col: col // SLOTS == r)
-        spread = one_hot((TILE, per_tile), lambda r, col: r == col * SLOTS + CAP)
+        blocks = TILE // SLOTS
+        fold = one_hot((blocks, TILE), lambda r, col: col // SLOTS == r)
+        spread = one_hot((TILE, blocks), lambda r, col: r == col * SLOTS + CAP)
         extra = dot_f32(spread, dot_f32(fold, put_parts(gate_grad)).astype(jnp.bfloat16))
         for n in range(model_width // TILE):
             part = slice(n * TILE, (n + 1) * TILE)
             back = dot_f32(gate_act_grad[cut], gate_ref[part, :], ((1,), (1,))) + dot_f32(
                 up_act_grad[cut], up_ref[part, :], ((1,), (1,))
             )
-            row_send[cut, part] = back.astype(jnp.bfloat16)
+            row_send[tile, :, part] = back.astype(jnp.bfloat16)
             if n == 0:
-                row_send[cut, :LANES] = (back[:, :LANES] + extra).astype(jnp.bfloat16)
-
-        @pl.loop(0, per_tile)
-        def _(index):
-            rows.start_one(tile * per_tile + index)
-
-    rows.own_copy().start()
-    outs.start()
-
-    @pl.loop(0, model_width // TILE)
-    def _(tile):
-        row = rows_ref[:, columns(tile)]
-        gate_grad_ref[rows_of(tile, TILE)] = dot_f32(row, gate_act_grad[...], ((0,), (0,))).astype(
-            jnp.bfloat16
+                row_send[tile, :, :LANES] = (back[:, :LANES] + extra).astype(jnp.bfloat16)
+        rows.start(tile)
+
+    @pl.loop(0, 4)
+    def _(step):
+        outs.start(level(step))
+
+    label = slot_labels(place, dp_count)
+    shape = (8 * SLOTS, LANES)
+    member = lax.broadcasted_iota(jnp.int32, shape, 0) // SLOTS
+    lane = lax.broadcasted_iota(jnp.int32, shape, 1)
+    expert = (member // 4) * dp_count + place.z * 4 + member % 4
+
+    def match(z, choice):
+        return label == target_all[z, choice : choice + 1]
+
+    def row_partial(step):
+        z = level(step)
+        rows.arrived(z)
+        hit = match(z, 0)
+        for choice in range(1, TOP):
+            hit = hit | match(z, choice)
+        placed = jnp.where(hit, 1.0, 0.0).astype(jnp.bfloat16)
+        cut = rows_of(z, TILE)
+        numbers = jnp.where(lane == expert, pick_gates(row_plane[cut, :LANES]), 0.0)
+        gate_part[z] = sum(dot_f32(placed, part, ((0,), (0,))) for part in split3(numbers))[
+            :tok_count
+        ]
+        for n in range(model_width // TILE):
+            part = slice(n * TILE, (n + 1) * TILE)
+            row_part[z, :, part] = dot_f32(placed, row_plane[cut, part], ((0,), (0,)))[
+                :tok_count
+            ].astype(jnp.bfloat16)
+
+    row_partial(0)
+    row_partial(1)
+    row_chain.run(0)
+    row_partial(2)
+    row_chain.run(1)
+    row_partial(3)
+    row_chain.run(2)
+
+    def gate_hop(i):
+        z = place.others()[i]
+        target = place.index(z, place.x, place.c)
+        return remote(
+            gate_part.at[z],
+            gate_land.at[i],
+            gate_send_sem.at[i],
+            gate_recv_sem.at[i],
+            target,
+            place.side,
         )
-        up_grad_ref[rows_of(tile, TILE)] = dot_f32(row, up_act_grad[...], ((0,), (0,))).astype(
-            jnp.bfloat16
-        )
+
+    for i in range(3):
+        gate_hop(i).start()
+
+    def out_partial(step):
+        z = level(step)
+        outs.arrived(z)
+        gates = jnp.zeros((8 * SLOTS, TILE), jnp.float32)
+        for choice in range(TOP):
+            gates += jnp.where(match(z, choice), gate_all[z, choice : choice + 1], 0.0)
+        high = gates.astype(jnp.bfloat16)
+        low = (gates - high.astype(jnp.float32)).astype(jnp.bfloat16)
+        cut = rows_of(z, TILE)
+        for n in range(model_width // TILE):
+            part = slice(n * TILE, (n + 1) * TILE)
+            out = out_plane[cut, part]
+            value = dot_f32(high, out, ((0,), (0,))) + dot_f32(low, out, ((0,), (0,)))
+            out_part[z, :, part] = value[:tok_count].astype(jnp.bfloat16)
+
+    def weight_grad(target, act):
+        @pl.loop(0, model_width // TILE)
+        def _(tile):
+            target[rows_of(tile, TILE)] = dot_f32(
+                rows_ref[:, columns(tile)], act[...], ((0,), (0,))
+            ).astype(jnp.bfloat16)
+
+    out_partial(0)
+    out_partial(1)
+    out_chain.run(0)
+    weight_grad(gate_grad_ref, gate_act_grad)
+    out_partial(2)
+    out_chain.run(1)
+    weight_grad(up_grad_ref, up_act_grad)
+    out_partial(3)
+    out_chain.run(2)
 
     @pl.loop(0, ff_width // TILE)
     def _(tile):
@@ -1327,44 +1456,57 @@
                 inner, grad_out[:, part], ((0,), (0,))
             ).astype(jnp.bfloat16)
 
-    rows.finish()
-    outs.finish()
-
-
-def experts(rows, grads, gate, up, down):
+    row_chain.finish(row_sum)
+    gate_sum[...] = gate_part[place.z]
+    for i in range(3):
+        gate_hop(i).wait()
+        gate_sum[...] += gate_land[i]
+    out_chain.finish(out_sum)
+    rows.sent()
+    outs.sent()
+
+
+def experts(rows, grads, gate, up, down, target, gates, tok_count):
     slots, model_width = rows.shape
     ff_width = gate.shape[1]
-    device_count = slots // SLOTS
     vmem = pl.BlockSpec(memory_space=pltpu.VMEM)
-    anywhere = pl.BlockSpec(memory_space=pl.ANY)
-    low = jnp.bfloat16
+    low, full = jnp.bfloat16, jnp.float32
     shape = jax.ShapeDtypeStruct
     dma = pltpu.SemaphoreType.DMA
     return pl.pallas_call(
         expert_kernel,
         out_shape=(
-            shape((slots, model_width), low),
-            shape((slots, model_width), low),
+            shape((tok_count, model_width), full),
+            shape((tok_count, model_width), full),
+            shape((tok_count, LANES), full),
             shape((model_width, ff_width), low),
             shape((model_width, ff_width), low),
             shape((ff_width, model_width), low),
         ),
-        in_specs=[vmem] * 5,
-        out_specs=(anywhere, anywhere, vmem, vmem, vmem),
+        in_specs=[vmem] * 7,
+        out_specs=(vmem,) * 6,
         scratch_shapes=[
+            pltpu.VMEM((4, 8 * SLOTS, model_width), low),
             pltpu.VMEM((slots, model_width), low),
-            pltpu.VMEM((slots, model_width), low),
+            pltpu.VMEM((4, tok_count, model_width), low),
+            pltpu.VMEM((5, tok_count, model_width), low),
+        ]
+        * 2
+        + [
+            pltpu.VMEM((4, tok_count, LANES), full),
+            pltpu.VMEM((3, tok_count, LANES), full),
             pltpu.VMEM((slots, model_width), low),
             pltpu.VMEM((slots, ff_width), low),
             pltpu.VMEM((slots, ff_width), low),
             pltpu.VMEM((slots, ff_width), low),
         ]
-        + [dma((device_count,))] * 4
-        + [dma((2,))],
+        + [dma((4, 8)), dma((4, 8)), dma((4,))] * 2
+        + [dma((4,)), dma((5,))] * 2
+        + [dma((3,))] * 2,
         compiler_params=pltpu.CompilerParams(
-            collective_id=1, has_side_effects=True, vmem_limit_bytes=58 * 1024 * 1024
+            collective_id=1, has_side_effects=True, vmem_limit_bytes=60 * 1024 * 1024
         ),
-    )(rows, grads, gate, up, down)
+    )(rows, grads, gate, up, down, target, gates)
 
 
 def halves_turned(value, cosine, sine):
@@ -1666,9 +1808,9 @@
     keys_ref,
     small_ref,
     out_ref,
-    placed_ref,
-    rows_ref,
-    outs_ref,
+    row_sum,
+    out_sum,
+    gate_sum,
     cosine_ref,
     sine_ref,
     gate_ref,
@@ -1698,8 +1840,7 @@
     weight_local,
 ):
     dp_count = keys_ref.shape[0]
-    slots = rows_ref.shape[0]
-    device_count = slots // SLOTS
+    device_count = dp_count * lax.axis_size("expert")
     tok_count, model_width = middle_ref.shape
     query_width = HEADS * HEAD
     key_width = KV_HEADS * HEAD
@@ -1728,11 +1869,7 @@
     )
 
     probs = probs_ref[...]
-    gate_grads = pick_gates(rows_ref[:, :LANES])
-    slot_row = lax.broadcasted_iota(jnp.int32, (slots, LANES), 0)
-    slot_lane = lax.broadcasted_iota(jnp.int32, (slots, LANES), 1)
-    by_expert = jnp.where(slot_lane == slot_row // SLOTS, gate_grads, 0.0)
-    grad_probs = sum(dot_f32(placed_ref[...], part) for part in split3(by_expert))
+    grad_probs = gate_sum[...]
     grad_logits = (
         probs * (grad_probs - jnp.sum(probs * grad_probs, axis=-1, keepdims=True))
     ).astype(jnp.bfloat16)
@@ -1740,9 +1877,9 @@
 
     @pl.loop(0, model_width // TILE)
     def _(tile):
-        grad_hidden[:, columns(tile)] = dot_f32(
-            placed_ref[...], rows_ref[:, columns(tile)]
-        ) + dot_f32(grad_logits_ref[...], small_ref[rows_of(tile, TILE)], ((1,), (1,)))
+        grad_hidden[:, columns(tile)] = row_sum[:, columns(tile)] + dot_f32(
+            grad_logits_ref[...], small_ref[rows_of(tile, TILE)], ((1,), (1,))
+        )
 
     gain = gain_rows(small_ref[...])[1:2]
     gain_ref[...] = jnp.zeros(gain_ref.shape, jnp.float32)
@@ -1834,18 +1971,7 @@
     scatter.pass_core()
     scatter.pass_x()
 
-    expand = one_hot((LANES, slots), lambda r, col: col // SLOTS == r)
-    high, mid, low = split3(probs_ref[...])
-    gates = (dot_f32(high, expand) + dot_f32(mid, expand)) * placed_ref[...].astype(jnp.float32)
-    gate_high = gates.astype(jnp.bfloat16)
-    gate_low = (gates - gate_high.astype(jnp.float32)).astype(jnp.bfloat16)
-
-    @pl.loop(0, model_width // TILE)
-    def _(tile):
-        outs = outs_ref[:, columns(tile)]
-        result_ref[:, columns(tile)] = (
-            middle_ref[:, columns(tile)] + dot_f32(gate_high, outs) + dot_f32(gate_low, outs)
-        ).astype(jnp.bfloat16)
+    result_ref[...] = (middle_ref[...] + out_sum[...]).astype(jnp.bfloat16)
 
     def put(cut, value):
         grad_project_ref[cut, query_width : query_width + key_width] = halves_turned(
@@ -1859,12 +1985,11 @@
 
 
 def back(
-    bias, cotangent, middle, probs, exact, stats, query, keys, small, out, placed, rows, outs,
+    bias, cotangent, middle, probs, exact, stats, query, keys, small, out, row_sum, out_sum, gate_sum,
     cosine, sine, gate_grad, up_grad, shard,
 ):
     dp_count, tok_count, both = keys.shape
     model_width = middle.shape[1]
-    slots = rows.shape[0]
     ff_width = gate_grad.shape[1]
     vmem = pl.BlockSpec(memory_space=pltpu.VMEM)
     anywhere = pl.BlockSpec(memory_space=pl.ANY)
@@ -1906,7 +2031,7 @@
             collective_id=2, has_side_effects=True, vmem_limit_bytes=60 * 1024 * 1024
         ),
     )(
-        bias, cotangent, middle, probs, exact, stats, query, keys, small, out, placed, rows, outs,
+        bias, cotangent, middle, probs, exact, stats, query, keys, small, out, row_sum, out_sum, gate_sum,
         cosine, sine, gate_grad, up_grad,
     )
 
@@ -2134,10 +2259,6 @@
     target = jnp.where(slot_index < CAP, expert_ids * SLOTS + slot_index, -1).reshape(
         tok_count, TOP
     )
-    row_labels = jnp.arange(EXPERTS * SLOTS, dtype=jnp.int32)
-    placed_rows = sum(
-        (target[:, c : c + 1] == row_labels[None, :]).astype(jnp.bfloat16) for c in range(TOP)
-    )
     target_rows = jnp.full((8, TILE), -1.0, jnp.float32)
     target_rows = target_rows.at[:TOP, :tok_count].set(target.T.astype(jnp.float32))
     route_lanes = jnp.pad(route_rows, ((0, 0), (0, LANES - TOP)), constant_values=-1)
@@ -2177,6 +2298,8 @@
         up_own,
         down_own,
         hidden_one,
+        target_all,
+        gate_all,
     ) = front(
         bias,
         tokens[0],
@@ -2192,8 +2315,8 @@
         down_weight,
     )
     small_at = query_width + 2 * key_width
-    rows_back, outs_back, gate_grad, up_grad, down_grad = experts(
-        rows_in, grad_rows_in, gate_own, up_own, down_own
+    row_sum, out_sum, gate_sum, gate_grad, up_grad, down_grad = experts(
+        rows_in, grad_rows_in, gate_own, up_own, down_own, target_all, gate_all, tok_count
     )
     (
         block_out,
@@ -2215,9 +2338,9 @@
         keys,
         project_full[:, small_at:],
         out_full,
-        placed_rows,
-        rows_back,
-        outs_back,
+        row_sum,
+        out_sum,
+        gate_sum,
         cosine_wide,
         sine_wide,
         gate_grad,

time: 826 us -> 816 us (0.988)
  Pallas kernels: 796 us -> 782 us
    pallas_call x1, Pallas kernels: 185 us -> 163 us  [experts(): pl.pallas_call(expert_kernel, out_shape=(shape((tok_count, model_width),...]
where the time goes in v5:
time: 816 us; the launch traced here: 810 us
  Pallas kernels  782 us (96%)
  other arithmetic  13.1 us (2%)
  local copies, waits for them, and re-layouts  11.5 us (1%)
    pallas_call x1, Pallas kernels, front(): pl.pallas_call(front_kernel, out_shape=tuple((o[0] for o in outs)), in_sp...  361 us
    pallas_call x1, Pallas kernels, experts(): pl.pallas_call(expert_kernel, out_shape=(shape((tok_count, model_width),...  163 us
    pallas_call x1, Pallas kernels, back(): pl.pallas_call(back_kernel, out_shape=(shape((tok_count, model_width), lo...  146 us
    pallas_call x1, Pallas kernels, finish(): pl.pallas_call(finish_kernel, out_shape=(shape((tok_count, model_width),...  112 us

profile of v5, /device:TPU:8, one launch (start us, length us, event | category | flops | bytes accessed | tf_op | source)
XLA Modules:
  0.0 810.3 jit_solution(13091524459672898890)
XLA Ops:
  0.6 0.0 copy-start.8
  0.7 0.0 copy-start.9
  0.7 0.0 copy-start.10
  0.7 0.0 copy-start.5
  0.7 0.0 copy-start.6
  0.7 0.0 copy-start.7
  0.7 0.9 convolution_minimum_fusion.2
  1.6 0.1 convolution_minimum_fusion.1
  1.8 0.1 convolution_minimum_fusion
  1.9 0.1 fusion.24
  2.1 1.1 fusion.21
  3.9 0.5 fusion.12
  4.4 0.8 pad_maximum_fusion
  5.2 0.8 copy.36
  6.0 0.1 eq.38
  6.1 0.7 reduce.3
  6.8 0.7 fusion.7
  7.6 0.1 convert_element_type.40
  7.7 0.1 copy.40
  7.8 0.6 scatter.4.clone.target_ref
  8.4 0.7 pad.10.route_ref
  9.1 0.0 copy-done.8
  9.1 0.1 copy.33
  9.2 0.0 copy-done.9
  9.2 0.1 copy.34
  9.3 0.0 copy-done.10
  9.3 0.1 copy.35
  9.5 0.0 copy-done.5
  9.5 0.0 copy-done.6
  9.5 0.0 copy-done.7
  9.5 0.9 concatenate.11.project_ref
  10.3 360.7 %shard_map.238 = (bf16[1536,2176]{1,0:T(8,128)(2,1)}, bf16[1536,1536]{1,0:T(8,128)(2,1)}, bf16[16,224,512]{2,1,0:T(8,128)(2,1)}, bf16[224,1536]{1,0:T(8,128)(2,1...) custom-call(f32[16]{0:T(128)} %get-tuple-element.125.bias_ref, ...), custom_call_target="tpu_custom_call" | custom-call | tf_op jit(solution)/shard_map/pallas_call | solution.py:1210
  371.1 163.5 %shard_map.239 = (f32[224,1536]{1,0:T(8,128)}, f32[224,1536]{1,0:T(8,128)}, f32[224,128]{1,0:T(8,128)}, bf16[1536,768]{1,0:T(8,128)(2,1)}, bf16[1536,768]{1,0:T(8,128)(2,1)}, /*index=5*/bf16[768,1536]{1,0:T(8,128)(2,1)}) custom-call(bf16[1024,1536]{1,0:T(8,128)(2,1)} %get-tuple-element.67.rows_ref, bf16[1024,1536]{1,0:T(8,128)(2,1)} %get-tuple-element.68.grads_ref, ...), custom_call_target="tpu_custom_call" | custom-call | tf_op jit(solution)/shard_map/pallas_call | solution.py:1476
  534.6 1.8 slice.44.small_ref
  536.3 145.7 %shard_map.240 = (bf16[224,1536]{1,0:T(8,128)(2,1)}, f32[224,1536]{1,0:T(8,128)}, bf16[224,1536]{1,0:T(8,128)(2,1)}, bf16[224,128]{1,0:T(8,128)(2,1)}, bf16[224,...) custom-call(f32[16]{0:T(128)} %get-tuple-element.125.bias_ref, ...), custom_call_target="tpu_custom_call" | custom-call | tf_op jit(solution)/shard_map/pallas_call | solution.py:1999
  682.0 111.8 %shard_map.241 = (f32[224,1536]{1,0:T(8,128)}, f32[96,3712]{1,0:T(8,128)}, bf16[16,48,1536]{2,1,0:T(8,128)(2,1)}) custom-call(bf16[224,1536]{1,0:T(8,128)(2,1)} %bitcast.20, bf16[224,1536]{1,0:T(8,128)(2,1)} %get-tuple-element.80.hidden_one, bf16[224,1536]{1,0:T(8,128)(2,1)} %get-tuple-element.81.hidden_two, ...), custom_call_target="tpu_custom_call" | custom-call | tf_op jit(solution)/shard_map/pallas_call | solution.py:2182
  793.9 0.0 copy-start.2
  793.9 4.6 convert_element_type.45
  798.5 0.0 copy-done.2
  798.5 1.1 fusion.22
  799.6 0.7 fusion.23
  800.3 0.7 copy.39
  801.0 1.6 slice_reduce_fusion
  802.6 2.7 convert_element_type.43
  805.3 2.7 convert_element_type.44
  808.0 0.8 copy.43
  808.8 0.0 copy-done.3
  808.8 1.1 copy.44
  (13 shorter events, 0.1 us)
Async XLA Ops:
  0.6 8.4 %copy-start.8 = (bf16[96,32]{0,1:T(8,128)(2,1)S(1)}, bf16[96,32]{0,1:T(8,128)(2,1)}, u32[]{:S(2)}) copy-start(bf16[96,32]{0,1:T(8,128)(2,1)} %param.24) | copy-start | bytes 18436
  0.7 8.5 %copy-start.9 = (bf16[96]{0:T(256)(128)(2,1)S(1)}, bf16[96]{0:T(256)(128)(2,1)}, u32[]{:S(2)}) copy-start(bf16[96]{0:T(256)(128)(2,1)} %param.18) | copy-start | bytes 580
  0.7 8.7 %copy-start.10 = (bf16[96]{0:T(256)(128)(2,1)S(1)}, bf16[96]{0:T(256)(128)(2,1)}, u32[]{:S(2)}) copy-start(bf16[96]{0:T(256)(128)(2,1)} %param.23) | copy-start | bytes 580
  0.7 8.8 %copy-start.5 = (bf16[96,1536]{1,0:T(8,128)(2,1)S(1)}, bf16[96,1536]{1,0:T(8,128)(2,1)}, u32[]{:S(2)}) copy-start(bf16[96,1536]{1,0:T(8,128)(2,1)} %param.19) | copy-start | bytes 884740
  0.7 8.8 %copy-start.6 = (bf16[96,256]{1,0:T(8,128)(2,1)S(1)}, bf16[96,256]{1,0:T(8,128)(2,1)}, u32[]{:S(2)}) copy-start(bf16[96,256]{1,0:T(8,128)(2,1)} %param.20) | copy-start | bytes 147460
  0.7 8.8 %copy-start.7 = (bf16[96,256]{1,0:T(8,128)(2,1)S(1)}, bf16[96,256]{1,0:T(8,128)(2,1)}, u32[]{:S(2)}) copy-start(bf16[96,256]{1,0:T(8,128)(2,1)} %param.21) | copy-start | bytes 147460
  793.9 4.6 copy-start.2
  798.5 4.1 copy-start.1
  802.6 2.7 copy-start
  805.3 2.7 copy-start.4
  805.3 3.5 copy-start.3

commit v6 on v5

--- a/solution.py
+++ b/solution.py
@@ -1040,11 +1040,12 @@
     def _(tile):
         query_ref[:, columns(tile)] = turned(tile)
 
+    cotangents.forward(2, 3)
+
     keys.forward_z()
     keys.forward_x()
     keys.finish()
     out.start()
-    cotangents.forward(2, 4)
     weights.start(1, dp_count)
     weights.start_own()
 
@@ -1087,6 +1088,7 @@
 
     out.forward_z()
     out.forward_x()
+    cotangents.forward(3, 4)
     cotangents.own_copy().wait()
 
     @pl.loop(0, 4)

time: 816 us -> 806 us (0.988)
  Pallas kernels: 782 us -> 771 us
where the time goes in v6:
time: 806 us; the launch traced here: 800 us
  Pallas kernels  771 us (96%)
  other arithmetic  13.1 us (2%)
  local copies, waits for them, and re-layouts  11.5 us (1%)
    pallas_call x1, Pallas kernels, front(): pl.pallas_call(front_kernel, out_shape=tuple((o[0] for o in outs)), in_sp...  360 us
    pallas_call x1, Pallas kernels, experts(): pl.pallas_call(expert_kernel, out_shape=(shape((tok_count, model_width),...  160 us
    pallas_call x1, Pallas kernels, back(): pl.pallas_call(back_kernel, out_shape=(shape((tok_count, model_width), lo...  140 us
    pallas_call x1, Pallas kernels, finish(): pl.pallas_call(finish_kernel, out_shape=(shape((tok_count, model_width),...  112 us

profile of v6, /device:TPU:8, one launch (start us, length us, event | category | flops | bytes accessed | tf_op | source)
XLA Modules:
  0.0 799.8 jit_solution(4916764021916154564)
XLA Ops:
  0.6 0.0 copy-start.8
  0.7 0.0 copy-start.9
  0.7 0.0 copy-start.10
  0.7 0.0 copy-start.5
  0.7 0.0 copy-start.6
  0.7 0.0 copy-start.7
  0.7 0.9 convolution_minimum_fusion.2
  1.6 0.1 convolution_minimum_fusion.1
  1.8 0.1 convolution_minimum_fusion
  1.9 0.1 fusion.24
  2.1 1.1 fusion.21
  3.9 0.5 fusion.12
  4.4 0.8 pad_maximum_fusion
  5.2 0.8 copy.36
  6.0 0.1 eq.38
  6.1 0.7 reduce.3
  6.8 0.7 fusion.7
  7.6 0.1 convert_element_type.40
  7.7 0.1 copy.40
  7.8 0.6 scatter.4.clone.target_ref
  8.4 0.7 pad.10.route_ref
  9.1 0.0 copy-done.8
  9.1 0.1 copy.33
  9.2 0.0 copy-done.9
  9.2 0.1 copy.34
  9.3 0.0 copy-done.10
  9.3 0.1 copy.35
  9.5 0.0 copy-done.5
  9.5 0.0 copy-done.6
  9.5 0.0 copy-done.7
  9.5 0.9 concatenate.11.project_ref
  10.3 359.7 %shard_map.238 = (bf16[1536,2176]{1,0:T(8,128)(2,1)}, bf16[1536,1536]{1,0:T(8,128)(2,1)}, bf16[16,224,512]{2,1,0:T(8,128)(2,1)}, bf16[224,1536]{1,0:T(8,128)(2,1...) custom-call(f32[16]{0:T(128)} %get-tuple-element.125.bias_ref, ...), custom_call_target="tpu_custom_call" | custom-call | tf_op jit(solution)/shard_map/pallas_call | solution.py:1212
  370.0 159.6 %shard_map.239 = (f32[224,1536]{1,0:T(8,128)}, f32[224,1536]{1,0:T(8,128)}, f32[224,128]{1,0:T(8,128)}, bf16[1536,768]{1,0:T(8,128)(2,1)}, bf16[1536,768]{1,0:T(8,128)(2,1)}, /*index=5*/bf16[768,1536]{1,0:T(8,128)(2,1)}) custom-call(bf16[1024,1536]{1,0:T(8,128)(2,1)} %get-tuple-element.67.rows_ref, bf16[1024,1536]{1,0:T(8,128)(2,1)} %get-tuple-element.68.grads_ref, ...), custom_call_target="tpu_custom_call" | custom-call | tf_op jit(solution)/shard_map/pallas_call | solution.py:1478
  529.6 1.8 slice.44.small_ref
  531.4 140.2 %shard_map.240 = (bf16[224,1536]{1,0:T(8,128)(2,1)}, f32[224,1536]{1,0:T(8,128)}, bf16[224,1536]{1,0:T(8,128)(2,1)}, bf16[224,128]{1,0:T(8,128)(2,1)}, bf16[224,...) custom-call(f32[16]{0:T(128)} %get-tuple-element.125.bias_ref, ...), custom_call_target="tpu_custom_call" | custom-call | tf_op jit(solution)/shard_map/pallas_call | solution.py:2001
  671.6 111.8 %shard_map.241 = (f32[224,1536]{1,0:T(8,128)}, f32[96,3712]{1,0:T(8,128)}, bf16[16,48,1536]{2,1,0:T(8,128)(2,1)}) custom-call(bf16[224,1536]{1,0:T(8,128)(2,1)} %bitcast.20, bf16[224,1536]{1,0:T(8,128)(2,1)} %get-tuple-element.80.hidden_one, bf16[224,1536]{1,0:T(8,128)(2,1)} %get-tuple-element.81.hidden_two, ...), custom_call_target="tpu_custom_call" | custom-call | tf_op jit(solution)/shard_map/pallas_call | solution.py:2184
  783.4 4.6 convert_element_type.45
  788.0 0.0 copy-done.2
  788.0 1.1 fusion.22
  789.1 0.7 fusion.23
  789.8 0.7 copy.39
  790.5 1.6 slice_reduce_fusion
  792.1 2.7 convert_element_type.43
  794.8 0.0 copy-done
  794.8 2.7 convert_element_type.44
  797.5 0.0 copy-done.4
  797.5 0.8 copy.43
  798.3 1.1 copy.44
  (13 shorter events, 0.1 us)
Async XLA Ops:
  0.6 8.4 %copy-start.8 = (bf16[96,32]{0,1:T(8,128)(2,1)S(1)}, bf16[96,32]{0,1:T(8,128)(2,1)}, u32[]{:S(2)}) copy-start(bf16[96,32]{0,1:T(8,128)(2,1)} %param.24) | copy-start | bytes 18436
  0.7 8.5 %copy-start.9 = (bf16[96]{0:T(256)(128)(2,1)S(1)}, bf16[96]{0:T(256)(128)(2,1)}, u32[]{:S(2)}) copy-start(bf16[96]{0:T(256)(128)(2,1)} %param.18) | copy-start | bytes 580
  0.7 8.7 %copy-start.10 = (bf16[96]{0:T(256)(128)(2,1)S(1)}, bf16[96]{0:T(256)(128)(2,1)}, u32[]{:S(2)}) copy-start(bf16[96]{0:T(256)(128)(2,1)} %param.23) | copy-start | bytes 580
  0.7 8.8 %copy-start.5 = (bf16[96,1536]{1,0:T(8,128)(2,1)S(1)}, bf16[96,1536]{1,0:T(8,128)(2,1)}, u32[]{:S(2)}) copy-start(bf16[96,1536]{1,0:T(8,128)(2,1)} %param.19) | copy-start | bytes 884740
  0.7 8.8 %copy-start.6 = (bf16[96,256]{1,0:T(8,128)(2,1)S(1)}, bf16[96,256]{1,0:T(8,128)(2,1)}, u32[]{:S(2)}) copy-start(bf16[96,256]{1,0:T(8,128)(2,1)} %param.20) | copy-start | bytes 147460
  0.7 8.8 %copy-start.7 = (bf16[96,256]{1,0:T(8,128)(2,1)S(1)}, bf16[96,256]{1,0:T(8,128)(2,1)}, u32[]{:S(2)}) copy-start(bf16[96,256]{1,0:T(8,128)(2,1)} %param.21) | copy-start | bytes 147460
  783.4 4.6 copy-start.2
  788.0 4.1 copy-start.1
  792.1 2.7 copy-start
  794.8 2.7 copy-start.4
  794.8 3.5 copy-start.3

commit v7 on v5

--- a/solution.py
+++ b/solution.py
@@ -1044,7 +1044,6 @@
     keys.forward_x()
     keys.finish()
     out.start()
-    cotangents.forward(2, 4)
     weights.start(1, dp_count)
     weights.start_own()
 
@@ -1087,6 +1086,7 @@
 
     out.forward_z()
     out.forward_x()
+    cotangents.forward(2, 4)
     cotangents.own_copy().wait()
 
     @pl.loop(0, 4)

time: 816 us -> 816 us (level)
  no operation moved by 1% of the time
where the time goes in v7:
time: 816 us; the launch traced here: 810 us
  Pallas kernels  781 us (96%)
  other arithmetic  13.1 us (2%)
  local copies, waits for them, and re-layouts  11.5 us (1%)
    pallas_call x1, Pallas kernels, front(): pl.pallas_call(front_kernel, out_shape=tuple((o[0] for o in outs)), in_sp...  356 us
    pallas_call x1, Pallas kernels, experts(): pl.pallas_call(expert_kernel, out_shape=(shape((tok_count, model_width),...  170 us
    pallas_call x1, Pallas kernels, back(): pl.pallas_call(back_kernel, out_shape=(shape((tok_count, model_width), lo...  143 us
    pallas_call x1, Pallas kernels, finish(): pl.pallas_call(finish_kernel, out_shape=(shape((tok_count, model_width),...  112 us

profile of v7, /device:TPU:8, one launch (start us, length us, event | category | flops | bytes accessed | tf_op | source)
XLA Modules:
  0.0 809.7 jit_solution(18444625301913050243)
XLA Ops:
  0.6 0.0 copy-start.8
  0.7 0.0 copy-start.9
  0.7 0.0 copy-start.10
  0.7 0.0 copy-start.5
  0.7 0.0 copy-start.6
  0.7 0.0 copy-start.7
  0.7 0.9 convolution_minimum_fusion.2
  1.6 0.1 convolution_minimum_fusion.1
  1.8 0.1 convolution_minimum_fusion
  1.9 0.1 fusion.24
  2.1 1.1 fusion.21
  3.9 0.5 fusion.12
  4.4 0.8 pad_maximum_fusion
  5.2 0.8 copy.36
  6.0 0.1 eq.38
  6.1 0.7 reduce.3
  6.8 0.7 fusion.7
  7.6 0.1 convert_element_type.40
  7.7 0.1 copy.40
  7.8 0.6 scatter.4.clone.target_ref
  8.4 0.7 pad.10.route_ref
  9.1 0.0 copy-done.8
  9.1 0.1 copy.33
  9.2 0.0 copy-done.9
  9.2 0.1 copy.34
  9.3 0.0 copy-done.10
  9.3 0.1 copy.35
  9.5 0.0 copy-done.5
  9.5 0.0 copy-done.6
  9.5 0.0 copy-done.7
  9.5 0.9 concatenate.11.project_ref
  10.3 356.2 %shard_map.238 = (bf16[1536,2176]{1,0:T(8,128)(2,1)}, bf16[1536,1536]{1,0:T(8,128)(2,1)}, bf16[16,224,512]{2,1,0:T(8,128)(2,1)}, bf16[224,1536]{1,0:T(8,128)(2,1...) custom-call(f32[16]{0:T(128)} %get-tuple-element.125.bias_ref, ...), custom_call_target="tpu_custom_call" | custom-call | tf_op jit(solution)/shard_map/pallas_call | solution.py:1210
  366.5 170.1 %shard_map.239 = (f32[224,1536]{1,0:T(8,128)}, f32[224,1536]{1,0:T(8,128)}, f32[224,128]{1,0:T(8,128)}, bf16[1536,768]{1,0:T(8,128)(2,1)}, bf16[1536,768]{1,0:T(8,128)(2,1)}, /*index=5*/bf16[768,1536]{1,0:T(8,128)(2,1)}) custom-call(bf16[1024,1536]{1,0:T(8,128)(2,1)} %get-tuple-element.67.rows_ref, bf16[1024,1536]{1,0:T(8,128)(2,1)} %get-tuple-element.68.grads_ref, ...), custom_call_target="tpu_custom_call" | custom-call | tf_op jit(solution)/shard_map/pallas_call | solution.py:1476
  536.7 1.8 slice.44.small_ref
  538.5 142.9 %shard_map.240 = (bf16[224,1536]{1,0:T(8,128)(2,1)}, f32[224,1536]{1,0:T(8,128)}, bf16[224,1536]{1,0:T(8,128)(2,1)}, bf16[224,128]{1,0:T(8,128)(2,1)}, bf16[224,...) custom-call(f32[16]{0:T(128)} %get-tuple-element.125.bias_ref, ...), custom_call_target="tpu_custom_call" | custom-call | tf_op jit(solution)/shard_map/pallas_call | solution.py:1999
  681.4 111.8 %shard_map.241 = (f32[224,1536]{1,0:T(8,128)}, f32[96,3712]{1,0:T(8,128)}, bf16[16,48,1536]{2,1,0:T(8,128)(2,1)}) custom-call(bf16[224,1536]{1,0:T(8,128)(2,1)} %bitcast.20, bf16[224,1536]{1,0:T(8,128)(2,1)} %get-tuple-element.80.hidden_one, bf16[224,1536]{1,0:T(8,128)(2,1)} %get-tuple-element.81.hidden_two, ...), custom_call_target="tpu_custom_call" | custom-call | tf_op jit(solution)/shard_map/pallas_call | solution.py:2182
  793.2 0.0 copy-start.2
  793.2 4.6 convert_element_type.45
  797.8 0.0 copy-done.2
  797.8 1.1 fusion.22
  799.0 0.7 fusion.23
  799.7 0.7 copy.39
  800.3 1.6 slice_reduce_fusion
  801.9 0.0 copy-done.1
  801.9 2.7 convert_element_type.43
  804.6 2.7 convert_element_type.44
  807.3 0.8 copy.43
  808.1 1.1 copy.44
  (13 shorter events, 0.1 us)
Async XLA Ops:
  0.6 8.4 %copy-start.8 = (bf16[96,32]{0,1:T(8,128)(2,1)S(1)}, bf16[96,32]{0,1:T(8,128)(2,1)}, u32[]{:S(2)}) copy-start(bf16[96,32]{0,1:T(8,128)(2,1)} %param.24) | copy-start | bytes 18436
  0.7 8.5 %copy-start.9 = (bf16[96]{0:T(256)(128)(2,1)S(1)}, bf16[96]{0:T(256)(128)(2,1)}, u32[]{:S(2)}) copy-start(bf16[96]{0:T(256)(128)(2,1)} %param.18) | copy-start | bytes 580
  0.7 8.7 %copy-start.10 = (bf16[96]{0:T(256)(128)(2,1)S(1)}, bf16[96]{0:T(256)(128)(2,1)}, u32[]{:S(2)}) copy-start(bf16[96]{0:T(256)(128)(2,1)} %param.23) | copy-start | bytes 580
  0.7 8.8 %copy-start.5 = (bf16[96,1536]{1,0:T(8,128)(2,1)S(1)}, bf16[96,1536]{1,0:T(8,128)(2,1)}, u32[]{:S(2)}) copy-start(bf16[96,1536]{1,0:T(8,128)(2,1)} %param.19) | copy-start | bytes 884740
  0.7 8.8 %copy-start.6 = (bf16[96,256]{1,0:T(8,128)(2,1)S(1)}, bf16[96,256]{1,0:T(8,128)(2,1)}, u32[]{:S(2)}) copy-start(bf16[96,256]{1,0:T(8,128)(2,1)} %param.20) | copy-start | bytes 147460
  0.7 8.8 %copy-start.7 = (bf16[96,256]{1,0:T(8,128)(2,1)S(1)}, bf16[96,256]{1,0:T(8,128)(2,1)}, u32[]{:S(2)}) copy-start(bf16[96,256]{1,0:T(8,128)(2,1)} %param.21) | copy-start | bytes 147460
  793.2 4.6 copy-start.2
  797.8 4.1 copy-start.1
  801.9 2.7 copy-start
  804.6 2.7 copy-start.4
  804.6 3.5 copy-start.3
